TPU v7x, 32 devices: a whole 2x2x4 slice. The times are simulated.
32 devices in a mesh: fib: 8 (over y, x, core), blk: 4 (over z).
Axes of the slice: x: 2, y: 2, z: 4, core: 2. Of those that a mesh axis runs over, the one named last changes fastest.
Arguments:
- field_data: float32 [33, 8, 512, 128], P(None, 'blk', 'fib'), may hold values from -120 to 120
- start_block: float32 [512, 64], replicated, may hold values from -6 to 6
Outputs:
- core_out: float32 [33, 8, 64, 128], P(None, 'blk', 'fib')
All inputs are finite; a program needn't handle non-finite values.
Results may differ from a plain program's by a relative error of at most 0.00013.
Values sent between devices are 32-bit elements; how exact they have to be, the bound alone decides.
No kernel may reach another device: no remote copies, remote signals or barrier semaphores. Data moves between devices by JAX's collectives and lax.ppermute only.
A program may use at most 192 MiB of HBM per device.

v0:
```python
import jax
import jax.numpy as jnp
from jax import lax
from jax.sharding import PartitionSpec as P


def shards(field_data, start_block):
    highest = lax.Precision.HIGHEST
    received = lax.all_to_all(field_data, "fib", split_axis=3, concat_axis=2, tiled=True)
    width_x = received.shape[2]
    unfolded = jnp.transpose(received, (0, 1, 3, 2)).reshape(-1, width_x)
    contract_rows = (((0,), (0,)), ((), ()))
    local_gram = lax.dot_general(unfolded, unfolded, contract_rows, precision=highest)
    gram_total = lax.psum(local_gram, ("fib", "blk"))
    raw_basis = jnp.dot(gram_total, start_block, precision=highest)
    inner_block = jnp.dot(raw_basis.T, raw_basis, precision=highest)
    lower_factor = jnp.linalg.cholesky(inner_block)
    basis_cols = jax.scipy.linalg.solve_triangular(lower_factor, raw_basis.T, lower=True).T
    core_local = jnp.einsum("szxy,xr->szry", received, basis_cols, precision=highest)
    return lax.all_to_all(core_local, "fib", split_axis=2, concat_axis=3, tiled=True)


def solution(mesh):
    in_specs = (P(None, "blk", "fib", None), P())
    out_specs = P(None, "blk", "fib", None)
    return jax.shard_map(shards, mesh=mesh, in_specs=in_specs, out_specs=out_specs, check_vma=False)
```

profile of v0, /device:TPU:0, one launch (start us, length us, event | category | flops | bytes accessed | tf_op | source)
XLA Modules:
  0.0 252.1 jit_solution(2194777635643599147)
XLA Ops:
  6.5 0.0 copy-start
  6.5 0.0 all-reduce.2.cloned.1.call-start
  6.5 6.4 %copy.13 = f32[33,2,64,128]{2,1,0,3:T(2,128)} copy(f32[33,2,64,128]{3,2,1,0:T(8,128)} %param.2) | data formatting | bytes 4325376 | tf_op args[0]
  13.0 7.2 %reshape.13 = f32[8,1,67584]{2,1,0:T(1,128)S(1)} reshape(f32[128,33,2,64]{3,2,1,0:T(2,128)} %bitcast.45) | data formatting | bytes 4325376
  20.2 32.4 %all_to_all.36 = f32[8,1,67584]{2,1,0:T(1,128)} all-to-all(f32[8,1,67584]{2,1,0:T(1,128)S(1)} %reshape.13), channel_id=1, replica_groups=mesh['fib'=8,'blk'=4] {'fib'}, dimensions={0} | all-to-all | bytes 4325376 | tf_op jit(solution)/shard_map/all_to_all | solution.py:9
  52.6 0.5 broadcast.53
  53.1 7.4 %reduce.6 = f32[8,67584]{1,0:T(8,128)S(1)} reduce(f32[8,1,67584]{2,1,0:T(1,128)} %all_to_all.36, f32[]{:T(128)} %broadcast.53), dimensions={1}, to_apply=%all_to_all.26.reduce_sub_computation | reduce | bytes 4325380 | tf_op jit(solution)/shard_map/all_to_all | solution.py:9
  60.5 5.1 %reshape.14 = f32[128,33,2,64]{3,2,1,0:T(2,128)} reshape(f32[8,67584]{1,0:T(8,128)S(1)} %reduce.6) | data formatting | bytes 4325376
  65.6 2.8 %copy.14 = f32[33,2,64,128]{2,3,1,0:T(8,128)S(1)} copy(f32[33,2,64,128]{2,1,0,3:T(2,128)} %bitcast.46) | data formatting | bytes 4325376 | tf_op jit(solution)/shard_map/all_to_all | solution.py:9
  68.4 4.0 %copy.15 = f32[33,2,8,64,16]{3,2,4,1,0:T(8,128)} copy(f32[33,2,8,64,16]{3,4,2,1,0:T(8,128)S(1)} %bitcast.47) | data formatting | bytes 4325376 | tf_op jit(solution)/shard_map/all_to_all | solution.py:9
  72.4 3.7 %all_to_all.29 = f32[33,2,512,16]{2,3,1,0:T(8,128)S(1)} reshape(f32[33,2,8,64,16]{3,2,4,1,0:T(8,128)} %copy.15) | data formatting | bytes 4325376 | tf_op jit(solution)/shard_map/all_to_all | solution.py:9
  76.2 5.4 %fusion.4 = f32[512,512]{1,0:T(8,128)} fusion(f32[33,2,512,16]{2,3,1,0:T(8,128)S(1)} %all_to_all.29), kind=kOutput, calls=%fused_computation.4 | convolution fusion | flops 3321888768 | bytes 3211264 | tf_op jit(solution)/shard_map/dot_general | solution.py:13
  81.5 0.0 all-reduce.2.cloned.1.call-update
  81.6 129.4 %all-reduce.2.cloned.1.call-done = f32[512,512]{1,0:T(8,128)} async-done(((f32[512,512]{1,0:T(8,128)}), f32[512,512]{1,0:T(8,128)}) %all-reduce.2.cloned.1.call-update) | async-done | bytes 1048592 | tf_op jit(solution)/shard_map/psum | solution.py:14
  210.9 0.0 copy-done
  210.9 2.4 fusion.13
  213.3 0.3 fusion.14
  213.6 0.1 copy.16
  213.7 5.8 %cholesky.16 = f32[64,64]{1,0:T(8,128)S(1)} custom-call(f32[64,64]{1,0:T(8,128)S(1)} %fusion.12), custom_call_target="Cholesky" | custom-call | tf_op jit(solution)/shard_map/jit(cholesky)/cholesky | solution.py:17
  219.5 0.7 compare_reduce_fusion
  220.3 0.7 fusion.10
  221.0 4.9 %custom-call.7 = f32[1,64,64]{1,2,0:T(8,128)S(1)} custom-call(f32[1,64,64]{2,1,0:T(8,128)S(1)} %fusion.10), custom_call_target="InvertDiagBlocksLowerTriangular" | custom-call | tf_op jit(solution)/shard_map/jit(_solve_triangular)/triangular_solve | solution.py:18
  225.9 0.3 convolution_bitcast_fusion
  226.2 3.0 %fusion.7 = f32[33,2,64,16]{2,0,3,1:T(8,128)S(1)} fusion(f32[64,512,1,1]{1,0,3,2:T(8,128)S(1)} %convolution_bitcast_fusion, f32[33,2,512,16]{2,3,1,0:T(8,128)S(1)} %all_to_all.29), kind=kOutput, calls=%fused_computation.5 | convolution fusion | flops 415236096 | bytes 2564096 | tf_op jit(solution)/shard_map/szxy,xr->szry/dot_general | solution.py:19
  229.2 1.0 copy.18
  230.2 1.0 reshape.15
  231.3 10.4 %all_to_all.37 = f32[8,1,8448]{2,1,0:T(1,128)S(1)} all-to-all(f32[8,1,8448]{2,1,0:T(1,128)S(1)} %reshape.15), channel_id=1, replica_groups=mesh['fib'=8,'blk'=4] {'fib'}, dimensions={0} | all-to-all | bytes 540672 | tf_op jit(solution)/shard_map/all_to_all | solution.py:20
  241.7 1.3 reduce.7
  243.0 1.1 reshape.16
  244.1 0.1 copy.20
  244.2 1.0 copy.21
  (2 shorter events, 0.0 us)
Async XLA Ops:
  6.5 204.4 %copy-start = (f32[512,64]{0,1:T(8,128)S(1)}, f32[512,64]{0,1:T(8,128)}, u32[]{:S(2)}) copy-start(f32[512,64]{0,1:T(8,128)} %param.3) | copy-start | bytes 393220
  6.5 204.4 %all-reduce.2.cloned.1.call-start = ((), (), s32[]{:S(2)}) async-start(), calls=%async_computation.2 | async-start | bytes 2097152 | tf_op jit(solution)/shard_map/psum | solution.py:14
Sparse Core Ops, SparseCore 0:
  81.7 129.2 all-reduce.1
where the time goes:
time: 253 us; the launch traced here: 252 us
  waiting for transfers between devices  129 us (51%)
  blocking collectives  42.8 us (17%)
  local copies, waits for them, and re-layouts  34.3 us (14%)
  other arithmetic  20.9 us (8%)
  between operations  13.5 us (5%)
  matrix products  11.3 us (4%)
    psum x1, waiting for transfers between devices, shards(): gram_total = lax.psum(local_gram, ('fib', 'blk'))  129 us
    all_to_all x1, blocking collectives, shards(): lax.all_to_all(field_data, 'fib', split_axis=3, concat_axis=2, tiled=True)  32.4 us
    unnamed x7, local copies, waits for them, and re-layouts  20.9 us
    all_to_all x4, local copies, waits for them, and re-layouts, shards(): lax.all_to_all(field_data, 'fib', split_axis=3, concat_axis=2, tiled=True)  11.1 us
    all_to_all x1, blocking collectives, shards(): lax.all_to_all(core_local, 'fib', split_axis=2, concat_axis=3, tiled=True)  10.4 us
    all_to_all x1, other arithmetic, shards(): lax.all_to_all(field_data, 'fib', split_axis=3, concat_axis=2, tiled=True)  7.4 us
    another operation x3, other arithmetic, shards(): lower_factor = jnp.linalg.cholesky(inner_block)  6.6 us
    another operation x2, other arithmetic, shards(): jax.scipy.linalg.solve_triangular(lower_factor, raw_basis.T, lower=True)  5.59 us
  transfers between devices with their start and end apart: 1, of which 1 were waited for; matrix products, arithmetic and copies ran while one was open for 0% of the time, Pallas kernels for 0%

commit v1 on v0

v1 whole, which is shorter than its diff:
```python
import functools

import jax
import jax.numpy as jnp
from jax import lax
from jax.experimental import pallas as pl
from jax.experimental.pallas import tpu as pltpu
from jax.sharding import PartitionSpec as P

F32, BF16 = jnp.float32, jnp.bfloat16
HIGHEST = lax.Precision.HIGHEST
NN = (((1,), (0,)), ((), ()))
NT = (((1,), (1,)), ((), ()))
VMEM_LIMIT = 40 * 1024 * 1024
PARAMS = pltpu.CompilerParams(vmem_limit_bytes=VMEM_LIMIT)


def halves(value):
    high = value.astype(BF16)
    return high, (value - high.astype(F32)).astype(BF16)


def dot(left, right, dims):
    return lax.dot_general(left, right, dims, preferred_element_type=F32)


def dot_split(left, right, dims):
    rows = left.shape[0] // 2
    right_high, right_low = right
    both = dot(left, right_high, dims)
    return both[:rows] + both[rows:] + dot(left[:rows], right_low, dims)


def stack(value):
    return jnp.concatenate(halves(value), axis=0)


def pack_kernel(cells, slabs_ref, left_ref, send_ref, turned):
    own, width, ny = slabs_ref.shape
    left = left_ref.shape[0]
    g = pl.program_id(0)

    @pl.when(g == 0)
    def _():
        turned[:, : left * width] = left_ref[...].reshape(left * width, ny).T

    send_ref[0, : own * width] = slabs_ref[...].reshape(own * width, ny)
    send_ref[0, own * width :] = turned[pl.ds(pl.multiple_of(g * cells, cells), cells), :]


def pack(slabs, n, own, left):
    total, width, ny = slabs.shape
    cells = ny // n
    rows = own * width + cells
    return pl.pallas_call(
        functools.partial(pack_kernel, cells),
        grid=(n,),
        in_specs=[
            pl.BlockSpec((own, width, ny), lambda g: (g, 0, 0)),
            pl.BlockSpec((left, width, ny), lambda g: (n * own // left, 0, 0)),
        ],
        out_specs=pl.BlockSpec((1, rows, ny), lambda g: (g, 0, 0)),
        out_shape=jax.ShapeDtypeStruct((n, rows, ny), F32),
        scratch_shapes=[pltpu.VMEM((ny, ny), F32)],
        compiler_params=PARAMS,
    )(slabs, slabs)


def raw_kernel(left, width, slab_ref, rest_ref, start_ref, out_ref, start_two, total):
    n, _, ny = slab_ref.shape
    rank = start_ref.shape[0]
    s = pl.program_id(0)

    @pl.when(s == 0)
    def _():
        start_two[...] = stack(start_ref[...])
        cells = rest_ref.shape[1]
        columns = [halves(rest_ref[f]) for f in range(n)]
        for k in range(left):
            lanes = slice(k * width, (k + 1) * width)
            projected = jnp.zeros((rank, cells), F32)
            for f in range(n):
                part = [half[:, lanes] for half in columns[f]]
                projected += dot_split(start_two[:, f * width : (f + 1) * width], part, NT)
            two = stack(projected)
            for f in range(n):
                part = [half[:, lanes] for half in columns[f]]
                value = dot_split(two, part, NN)
                at = slice(f * width, (f + 1) * width)
                total[:, at] = value if k == 0 else total[:, at] + value

    block = halves(slab_ref[...].reshape(n * width, ny))
    projected = dot_split(start_two[...], block, NN)
    total[...] += dot_split(stack(projected), block, NT)

    @pl.when(s == pl.num_programs(0) - 1)
    def _():
        out_ref[...] = total[...]


def raw_basis(received, start_t, n, own, left, width):
    rows, ny = received.shape[1:]
    rank, nx = start_t.shape
    cells = rows - own * width
    return pl.pallas_call(
        functools.partial(raw_kernel, left, width),
        grid=(own,),
        in_specs=[
            pl.BlockSpec((n, width, ny), lambda s: (0, s, 0)),
            pl.BlockSpec((n, cells, ny), lambda s: (0, own * width // cells, 0)),
            pl.BlockSpec((rank, nx), lambda s: (0, 0)),
        ],
        out_specs=pl.BlockSpec((rank, nx), lambda s: (0, 0)),
        out_shape=jax.ShapeDtypeStruct((rank, nx), F32),
        scratch_shapes=[pltpu.VMEM((2 * rank, nx), BF16), pltpu.VMEM((rank, nx), F32)],
        compiler_params=PARAMS,
    )(received, received, start_t)


def inverse_factor(gram):
    rank = gram.shape[0]
    row = lax.broadcasted_iota(jnp.int32, (rank, rank), 0)
    col = lax.broadcasted_iota(jnp.int32, (rank, rank), 1)
    table = jnp.concatenate([gram, jnp.where(row == col, 1.0, 0.0).astype(F32)], axis=1)
    blocks = [table[8 * b : 8 * b + 8] for b in range(rank // 8)]
    sub = lax.broadcasted_iota(jnp.int32, (8, 1), 0)
    for j in range(rank):
        b, k = divmod(j, 8)
        pivot = blocks[b][k : k + 1]
        scaled = pivot * (1.0 / pivot[:, j : j + 1])
        for i in range(b, rank // 8):
            factor = blocks[i][:, j : j + 1]
            if i == b:
                factor = jnp.where(sub > k, factor, 0.0)
            blocks[i] = blocks[i] - factor * scaled
    table = jnp.concatenate(blocks, axis=0)
    diagonal = jnp.sum(jnp.where(row == col, table[:, :rank], 0.0), axis=1, keepdims=True)
    return table[:, rank:] * lax.rsqrt(diagonal)


def core_kernel(left, width, slab_ref, rest_ref, raw_ref, out_ref, basis_two):
    n, _, ny = slab_ref.shape
    rank = raw_ref.shape[0]
    each = rank // n
    s = pl.program_id(0)

    @pl.when(s == 0)
    def _():
        raw = raw_ref[...]
        gram = lax.dot_general(raw, raw, NT, precision=HIGHEST, preferred_element_type=F32)
        inverse = inverse_factor(gram)
        basis = lax.dot_general(inverse, raw, NN, precision=HIGHEST, preferred_element_type=F32)
        basis_two[...] = stack(basis)

    @pl.when(s < pl.num_programs(0) - 1)
    def _():
        block = halves(slab_ref[...].reshape(n * width, ny))
        out_ref[:, 0] = dot_split(basis_two[...], block, NN).reshape(n, each, ny)

    @pl.when(s == pl.num_programs(0) - 1)
    def _():
        cells = rest_ref.shape[1]
        columns = [halves(rest_ref[f]) for f in range(n)]
        out_ref[...] = jnp.zeros_like(out_ref)
        for k in range(left):
            lanes = slice(k * width, (k + 1) * width)
            value = jnp.zeros((rank, cells), F32)
            for f in range(n):
                part = [half[:, lanes] for half in columns[f]]
                value += dot_split(basis_two[:, f * width : (f + 1) * width], part, NT)
            out_ref[:, 0, :, k * cells : (k + 1) * cells] = value.reshape(n, each, cells)


def core(received, raw_t, n, own, left, width):
    rows, ny = received.shape[1:]
    rank, nx = raw_t.shape
    cells, each = rows - own * width, rank // n
    return pl.pallas_call(
        functools.partial(core_kernel, left, width),
        grid=(own + 1,),
        in_specs=[
            pl.BlockSpec((n, width, ny), lambda s: (0, jnp.minimum(s, own - 1), 0)),
            pl.BlockSpec((n, cells, ny), lambda s: (0, own * width // cells, 0)),
            pl.BlockSpec((rank, nx), lambda s: (0, 0)),
        ],
        out_specs=pl.BlockSpec((n, 1, each, ny), lambda s: (0, s, 0, 0)),
        out_shape=jax.ShapeDtypeStruct((n, own + 1, each, ny), F32),
        scratch_shapes=[pltpu.VMEM((2 * rank, nx), BF16)],
        compiler_params=PARAMS,
    )(received, received, raw_t)


def sum_over_devices(raw_t, devices):
    rank, nx = raw_t.shape
    tiles = (rank // 8) * (nx // 128)
    if tiles % devices:
        return lax.psum(raw_t, ("fib", "blk"))
    parts = raw_t.reshape(rank // 8, 8, nx // 128, 128).transpose(0, 2, 1, 3)
    parts = parts.reshape(devices, tiles // devices, 8, 128)
    terms = lax.all_to_all(parts, ("fib", "blk"), split_axis=0, concat_axis=0, tiled=True)
    mine = jnp.broadcast_to(jnp.sum(terms, axis=0, keepdims=True), terms.shape)
    whole = lax.all_to_all(mine, ("fib", "blk"), split_axis=0, concat_axis=0, tiled=True)
    return whole.reshape(rank // 8, nx // 128, 8, 128).transpose(0, 2, 1, 3).reshape(rank, nx)


def shards(n, devices, field_data, start_block):
    species, planes, width, ny = field_data.shape
    rank = start_block.shape[1]
    total = species * planes
    own, left = divmod(total, n)
    cells, each = ny // n, rank // n
    slabs = field_data.reshape(total, width, ny)
    send = pack(slabs, n, own, left)
    received = lax.all_to_all(send, "fib", split_axis=0, concat_axis=0, tiled=True)
    raw_t = sum_over_devices(raw_basis(received, start_block.T, n, own, left, width), devices)
    core_send = core(received, raw_t, n, own, left, width)
    core_got = lax.all_to_all(core_send, "fib", split_axis=0, concat_axis=0, tiled=True)
    out_main = core_got[:, :own].reshape(n * own, each, ny)
    out_rest = core_got[:, own, :, : left * cells].reshape(n, each, left, cells)
    out_rest = out_rest.transpose(2, 1, 0, 3).reshape(left, each, ny)
    return jnp.concatenate([out_main, out_rest], axis=0).reshape(species, planes, each, ny)


def solution(mesh):
    n, devices = mesh.shape["fib"], mesh.size
    in_specs = (P(None, "blk", "fib", None), P())
    out_specs = P(None, "blk", "fib", None)
    return jax.shard_map(
        functools.partial(shards, n, devices), mesh=mesh, in_specs=in_specs, out_specs=out_specs, check_vma=False
    )
```

time: 253 us -> 81.2 us (0.32)
  waiting for transfers between devices: 129 us -> 0 us
  local copies, waits for them, and re-layouts: 34.3 us -> 1.85 us
  blocking collectives: 42.8 us -> 64.4 us
  other arithmetic: 20.9 us -> 0.76 us
  Pallas kernels: 0 us -> 13.9 us
  between operations: 13.5 us -> 0.06 us
  matrix products: 11.3 us -> 0 us
    psum x1 -> x0, waiting for transfers between devices: 129 us -> none  [shards(): gram_total = lax.psum(local_gram, ('fib', 'blk'))]
    all_to_all x2 -> x4, blocking collectives: 42.8 us -> 64.4 us  [the longest x1 32.4 us: shards(): lax.all_to_all(send, 'fib', split_axis=0, concat_axis=0, tiled=True)]
    unnamed x7 -> x4, local copies, waits for them, and re-layouts: 20.9 us -> 1.62 us
    pallas_call x0 -> x3, Pallas kernels: none -> 13.9 us  [the longest x1 8.76 us: core(): pl.pallas_call(functools.partial(core_kernel, left, width), grid=(own + 1...]
    all_to_all x6 -> x0, local copies, waits for them, and re-layouts: 12.2 us -> none  [the longest x4 11.1 us: shards(): lax.all_to_all(field_data, 'fib', split_axis=3, concat_axis=2, tiled=True)]
    another operation x5 -> x0, other arithmetic: 12.2 us -> none  [the longest x3 6.6 us: shards(): lower_factor = jnp.linalg.cholesky(inner_block)]
    dot_general x4 -> x0, matrix products: 11 us -> none  [the longest x1 5.37 us: shards(): lax.dot_general(unfolded, unfolded, contract_rows, precision=highest)]
    all_to_all x2 -> x0, other arithmetic: 8.67 us -> none  [the longest x1 7.4 us: shards(): lax.all_to_all(field_data, 'fib', split_axis=3, concat_axis=2, tiled=True)]
  transfers between devices with their start and end apart: 1 -> 0, of which waited for: 1 -> 0; matrix products, arithmetic and copies ran while one was open for 0% -> 0% of each run, Pallas kernels for 0% -> 0%
where the time goes in v1:
time: 81.2 us; the launch traced here: 80.9 us
  blocking collectives  64.4 us (79%)
  Pallas kernels  13.9 us (17%)
  local copies, waits for them, and re-layouts  1.85 us (2%)
    all_to_all x1, blocking collectives, shards(): lax.all_to_all(send, 'fib', split_axis=0, concat_axis=0, tiled=True)  32.4 us
    all_to_all x1, blocking collectives, sum_over_devices(): lax.all_to_all(parts, ('fib', 'blk'), split_axis=0, concat_axis=0, tiled=...  12.2 us
    all_to_all x1, blocking collectives, sum_over_devices(): lax.all_to_all(mine, ('fib', 'blk'), split_axis=0, concat_axis=0, tiled=T...  10.1 us
    all_to_all x1, blocking collectives, shards(): lax.all_to_all(core_send, 'fib', split_axis=0, concat_axis=0, tiled=True)  9.66 us
    pallas_call x1, Pallas kernels, core(): pl.pallas_call(functools.partial(core_kernel, left, width), grid=(own + 1...  8.76 us
    pallas_call x1, Pallas kernels, raw_basis(): pl.pallas_call(functools.partial(raw_kernel, left, width), grid=(own,), i...  4.77 us

profile of v1, /device:TPU:0, one launch (start us, length us, event | category | flops | bytes accessed | tf_op | source)
XLA Modules:
  0.0 80.9 jit_solution(16734063923142660049)
XLA Ops:
  0.0 0.0 copy-start
  0.0 1.6 %copy-done = f32[33,2,64,128]{3,2,1,0:T(8,128)S(1)} copy-done((f32[33,2,64,128]{3,2,1,0:T(8,128)S(1)}, f32[33,2,64,128]{3,2,1,0:T(8,128)}, u32[]{:S(2)}) %copy-start) | copy-done | bytes 2162712
  1.6 0.4 shard_map.28
  2.0 0.0 copy-start.1
  2.0 32.4 %all_to_all.20.slab_ref.rest_ref = f32[8,528,128]{2,1,0:T(8,128)S(1)} all-to-all(f32[8,528,128]{2,1,0:T(8,128)S(1)} %shard_map.28), channel_id=1, replica_groups=mesh['fib'=8,'blk'=4] {'fib'}, dimensions={0} | all-to-all | bytes 4325376 | tf_op jit(solution)/shard_map/all_to_all | solution.py:214
  34.4 0.0 copy-done.1
  34.4 4.8 %shard_map.29 = f32[64,512]{1,0:T(8,128)S(1)} custom-call(f32[8,528,128]{2,1,0:T(8,128)S(1)} %all_to_all.20.slab_ref.rest_ref, f32[8,528,128]{2,1,0:T(8,128)S(1)} %all_to_all.20.slab_ref.rest_ref, f32[64,512]{1,0:T(8,128)S(1)} %bitcast.25), custom_call_target="tpu_custom_call" | custom-call | tf_op jit(solution)/shard_map/pallas_call | solution.py:105
  39.2 12.2 %all_to_all.21 = f32[32,1,8,128]{3,2,1,0:T(8,128)S(1)} all-to-all(f32[32,1,8,128]{3,2,1,0:T(8,128)S(1)} %bitcast.24), channel_id=1, replica_groups=mesh['fib'=8,'blk'=4] {'fib','blk'}, dimensions={0} | all-to-all | bytes 262144 | tf_op jit(solution)/shard_map/all_to_all | solution.py:200
  51.4 10.1 %all_to_all.22 = f32[32,1,8,128]{3,2,1,0:T(8,128)S(1)} all-to-all(f32[32,1,8,128]{3,2,1,0:T(8,128)S(1)} %broadcast_in_dim.2), channel_id=1, replica_groups=mesh['fib'=8,'blk'=4] {'fib','blk'}, dimensions={0} | all-to-all | bytes 262144 | tf_op jit(solution)/shard_map/all_to_all | solution.py:202
  61.5 8.8 %shard_map.30 = f32[8,9,8,128]{3,2,1,0:T(8,128)S(1)} custom-call(f32[8,528,128]{2,1,0:T(8,128)S(1)} %all_to_all.20.slab_ref.rest_ref, f32[8,528,128]{2,1,0:T(8,128)S(1)} %all_to_all.20.slab_ref.rest_ref, f32[64,512]{1,0:T(8,128)S(1)} %bitcast.23), custom_call_target="tpu_custom_call" | custom-call | tf_op jit(solution)/shard_map/pallas_call | solution.py:178
  70.3 9.7 %all_to_all.23 = f32[8,9,8,128]{3,2,1,0:T(8,128)S(1)} all-to-all(f32[8,9,8,128]{3,2,1,0:T(8,128)S(1)} %shard_map.30), channel_id=1, replica_groups=mesh['fib'=8,'blk'=4] {'fib'}, dimensions={0} | all-to-all | bytes 589824 | tf_op jit(solution)/shard_map/all_to_all | solution.py:217
  79.9 0.1 reshape_squeeze.3
  80.1 0.1 reshape.35
  80.2 0.7 pad_maximum_fusion
  (5 shorter events, 0.1 us)
Async XLA Ops:
  0.0 1.6 %copy-start = (f32[33,2,64,128]{3,2,1,0:T(8,128)S(1)}, f32[33,2,64,128]{3,2,1,0:T(8,128)}, u32[]{:S(2)}) copy-start(f32[33,2,64,128]{3,2,1,0:T(8,128)} %param.2) | copy-start | bytes 6488068
  2.0 32.4 %copy-start.1 = (f32[512,64]{0,1:T(8,128)S(1)}, f32[512,64]{0,1:T(8,128)}, u32[]{:S(2)}) copy-start(f32[512,64]{0,1:T(8,128)} %param.3) | copy-start | bytes 393220

commit v2 on v1

v2 whole, which is shorter than its diff:
```python
import functools

import jax
import jax.numpy as jnp
from jax import lax
from jax.experimental import pallas as pl
from jax.experimental.pallas import tpu as pltpu
from jax.sharding import PartitionSpec as P

F32, BF16 = jnp.float32, jnp.bfloat16
HIGHEST = lax.Precision.HIGHEST
NN = (((1,), (0,)), ((), ()))
NT = (((1,), (1,)), ((), ()))
VMEM_LIMIT = 40 * 1024 * 1024
PARAMS = pltpu.CompilerParams(vmem_limit_bytes=VMEM_LIMIT)


def halves(value):
    high = value.astype(BF16)
    return high, (value - high.astype(F32)).astype(BF16)


def dot(left, right, dims):
    return lax.dot_general(left, right, dims, preferred_element_type=F32)


def dot_split(left, right, dims):
    rows = left.shape[0] // 2
    right_high, right_low = right
    both = dot(left, right_high, dims)
    return both[:rows] + both[rows:] + dot(left[:rows], right_low, dims)


def stack(value):
    return jnp.concatenate(halves(value), axis=0)


def pack_kernel(cells, slabs_ref, left_ref, send_ref, turned):
    own, width, ny = slabs_ref.shape
    left = left_ref.shape[0]
    g = pl.program_id(0)

    @pl.when(g == 0)
    def _():
        turned[:, : left * width] = left_ref[...].reshape(left * width, ny).T

    send_ref[0, : own * width] = slabs_ref[...].reshape(own * width, ny)
    send_ref[0, own * width :] = turned[pl.ds(pl.multiple_of(g * cells, cells), cells), :]


def pack(slabs, n, own, left):
    total, width, ny = slabs.shape
    cells = ny // n
    rows = own * width + cells
    return pl.pallas_call(
        functools.partial(pack_kernel, cells),
        grid=(n,),
        in_specs=[
            pl.BlockSpec((own, width, ny), lambda g: (g, 0, 0)),
            pl.BlockSpec((left, width, ny), lambda g: (n * own // left, 0, 0)),
        ],
        out_specs=pl.BlockSpec((1, rows, ny), lambda g: (g, 0, 0)),
        out_shape=jax.ShapeDtypeStruct((n, rows, ny), F32),
        scratch_shapes=[pltpu.VMEM((ny, ny), F32)],
        compiler_params=PARAMS,
    )(slabs, slabs)


def by_cell(rest_ref, left, width):
    blocks = [rest_ref[f] for f in range(rest_ref.shape[0])]
    slabs = [[block[:, k * width : (k + 1) * width] for block in blocks] for k in range(left)]
    return jnp.concatenate([jnp.concatenate(parts, axis=1) for parts in slabs], axis=0)


def raw_kernel(own, left, width, cells_ref, start_ref, out_ref):
    n, _, ny = cells_ref.shape
    start = stack(start_ref[...])
    rest = halves(by_cell(cells_ref.at[:, own * width :], left, width))
    total = dot_split(stack(dot_split(start, rest, NT)), rest, NN)
    for s in range(own):
        slab = halves(cells_ref[:, s * width : (s + 1) * width].reshape(n * width, ny))
        total += dot_split(stack(dot_split(start, slab, NN)), slab, NT)
    out_ref[...] = total


def raw_basis(received, start_t, own, left, width):
    return pl.pallas_call(
        functools.partial(raw_kernel, own, left, width),
        in_specs=[pl.BlockSpec(memory_space=pltpu.VMEM)] * 2,
        out_specs=pl.BlockSpec(memory_space=pltpu.VMEM),
        out_shape=jax.ShapeDtypeStruct(start_t.shape, F32),
        compiler_params=PARAMS,
    )(received, start_t)


def inverse_factor(gram):
    rank = gram.shape[0]
    row = lax.broadcasted_iota(jnp.int32, (rank, rank), 0)
    col = lax.broadcasted_iota(jnp.int32, (rank, rank), 1)
    table = jnp.concatenate([gram, jnp.where(row == col, 1.0, 0.0).astype(F32)], axis=1)
    rows = [table[8 * b : 8 * b + 8] for b in range(rank // 8)]
    wide = rows[0].shape
    sub = lax.broadcasted_iota(jnp.int32, wide, 0)

    def spread(value, k):
        return jnp.broadcast_to(value[k : k + 1], wide)

    inverse = []
    for b in range(len(rows)):
        columns = [
            [jnp.broadcast_to(block[:, 8 * b + k : 8 * b + k + 1], wide) for k in range(8)] for block in rows[b:]
        ]
        pivots = jnp.ones(wide, F32)
        for k in range(8):
            pivot = spread(columns[0][k], k)
            pivots = jnp.where(sub == k, pivot, pivots)
            scale = 1.0 / pivot
            scaled = spread(rows[b], k) * scale
            ahead = [spread(columns[0][m], k) * scale for m in range(k + 1, 8)]
            for i, column in enumerate(columns):
                factor = jnp.where(sub > k, column[k], 0.0) if i == 0 else column[k]
                for m in range(k + 1, 8):
                    column[m] = column[m] - factor * ahead[m - k - 1]
                rows[b + i] = rows[b + i] - factor * scaled
        inverse.append(rows[b][:, rank:] * lax.rsqrt(pivots[:, rank:]))
    return jnp.concatenate(inverse, axis=0)


def core_kernel(own, left, width, cells_ref, raw_ref, out_ref):
    n, rows, ny = cells_ref.shape
    cells = rows - own * width
    rank = raw_ref.shape[0]
    each = rank // n
    raw = raw_ref[...]
    gram = lax.dot_general(raw, raw, NT, precision=HIGHEST, preferred_element_type=F32)
    basis = lax.dot_general(inverse_factor(gram), raw, NN, precision=HIGHEST, preferred_element_type=F32)
    basis = stack(basis)
    for s in range(own):
        slab = halves(cells_ref[:, s * width : (s + 1) * width].reshape(n * width, ny))
        out_ref[:, s] = dot_split(basis, slab, NN).reshape(n, each, ny)
    rest = halves(by_cell(cells_ref.at[:, own * width :], left, width))
    value = dot_split(basis, rest, NT)
    value = jnp.concatenate([value, jnp.zeros((rank, ny - left * cells), F32)], axis=1)
    out_ref[:, own] = value.reshape(n, each, ny)


def core(received, raw_t, own, left, width):
    n, _, ny = received.shape
    return pl.pallas_call(
        functools.partial(core_kernel, own, left, width),
        in_specs=[pl.BlockSpec(memory_space=pltpu.VMEM)] * 2,
        out_specs=pl.BlockSpec(memory_space=pltpu.VMEM),
        out_shape=jax.ShapeDtypeStruct((n, own + 1, raw_t.shape[0] // n, ny), F32),
        compiler_params=PARAMS,
    )(received, raw_t)


def sum_over_devices(raw_t, devices):
    rank, nx = raw_t.shape
    tiles = (rank // 8) * (nx // 128)
    if tiles % devices:
        return lax.psum(raw_t, ("fib", "blk"))
    parts = raw_t.reshape(rank // 8, 8, nx // 128, 128).transpose(0, 2, 1, 3)
    parts = parts.reshape(devices, tiles // devices, 8, 128)
    terms = lax.all_to_all(parts, ("fib", "blk"), split_axis=0, concat_axis=0, tiled=True)
    mine = jnp.broadcast_to(jnp.sum(terms, axis=0, keepdims=True), terms.shape)
    whole = lax.all_to_all(mine, ("fib", "blk"), split_axis=0, concat_axis=0, tiled=True)
    return whole.reshape(rank // 8, nx // 128, 8, 128).transpose(0, 2, 1, 3).reshape(rank, nx)


def shards(n, devices, field_data, start_block):
    species, planes, width, ny = field_data.shape
    rank = start_block.shape[1]
    total = species * planes
    own, left = divmod(total, n)
    cells, each = ny // n, rank // n
    slabs = field_data.reshape(total, width, ny)
    send = pack(slabs, n, own, left)
    received = lax.all_to_all(send, "fib", split_axis=0, concat_axis=0, tiled=True)
    raw_t = sum_over_devices(raw_basis(received, start_block.T, own, left, width), devices)
    core_send = core(received, raw_t, own, left, width)
    core_got = lax.all_to_all(core_send, "fib", split_axis=0, concat_axis=0, tiled=True)
    out_main = core_got[:, :own].reshape(n * own, each, ny)
    out_rest = core_got[:, own, :, : left * cells].reshape(n, each, left, cells)
    out_rest = out_rest.transpose(2, 1, 0, 3).reshape(left, each, ny)
    return jnp.concatenate([out_main, out_rest], axis=0).reshape(species, planes, each, ny)


def solution(mesh):
    n, devices = mesh.shape["fib"], mesh.size
    in_specs = (P(None, "blk", "fib", None), P())
    out_specs = P(None, "blk", "fib", None)
    return jax.shard_map(
        functools.partial(shards, n, devices), mesh=mesh, in_specs=in_specs, out_specs=out_specs, check_vma=False
    )
```

time: 81.2 us -> 72.7 us (0.90)
  Pallas kernels: 13.9 us -> 5.4 us
    pallas_call x2, Pallas kernels: 13.5 us -> 5.05 us  [the longest x1 3.11 us: core(): pl.pallas_call(functools.partial(core_kernel, own, left, width), in_specs...]
where the time goes in v2:
time: 72.7 us; the launch traced here: 72.4 us
  blocking collectives  64.3 us (88%)
  Pallas kernels  5.4 us (7%)
  local copies, waits for them, and re-layouts  1.85 us (3%)
  other arithmetic  0.76 us (1%)
    all_to_all x1, blocking collectives, shards(): lax.all_to_all(send, 'fib', split_axis=0, concat_axis=0, tiled=True)  32.4 us
    all_to_all x1, blocking collectives, sum_over_devices(): lax.all_to_all(parts, ('fib', 'blk'), split_axis=0, concat_axis=0, tiled=...  12.2 us
    all_to_all x1, blocking collectives, sum_over_devices(): lax.all_to_all(mine, ('fib', 'blk'), split_axis=0, concat_axis=0, tiled=T...  10.1 us
    all_to_all x1, blocking collectives, shards(): lax.all_to_all(core_send, 'fib', split_axis=0, concat_axis=0, tiled=True)  9.66 us
    pallas_call x1, Pallas kernels, core(): pl.pallas_call(functools.partial(core_kernel, own, left, width), in_specs...  3.11 us
    pallas_call x1, Pallas kernels, raw_basis(): pl.pallas_call(functools.partial(raw_kernel, own, left, width), in_specs=...  1.94 us
    unnamed x4, local copies, waits for them, and re-layouts  1.62 us

profile of v2, /device:TPU:0, one launch (start us, length us, event | category | flops | bytes accessed | tf_op | source)
XLA Modules:
  0.0 72.4 jit_solution(12207751709024902431)
XLA Ops:
  0.0 0.0 copy-start
  0.0 1.6 %copy-done = f32[33,2,64,128]{3,2,1,0:T(8,128)S(1)} copy-done((f32[33,2,64,128]{3,2,1,0:T(8,128)S(1)}, f32[33,2,64,128]{3,2,1,0:T(8,128)}, u32[]{:S(2)}) %copy-start) | copy-done | bytes 2162712
  1.6 0.4 shard_map.28
  2.0 0.0 copy-start.1
  2.0 32.4 %all_to_all.20.cells_ref = f32[8,528,128]{2,1,0:T(8,128)S(1)} all-to-all(f32[8,528,128]{2,1,0:T(8,128)S(1)} %shard_map.28), channel_id=1, replica_groups=mesh['fib'=8,'blk'=4] {'fib'}, dimensions={0} | all-to-all | bytes 4325376 | tf_op jit(solution)/shard_map/all_to_all | solution.py:179
  34.4 0.0 copy-done.1
  34.4 1.9 %shard_map.29 = f32[64,512]{1,0:T(8,128)S(1)} custom-call(f32[8,528,128]{2,1,0:T(8,128)S(1)} %all_to_all.20.cells_ref, f32[64,512]{1,0:T(8,128)S(1)} %bitcast.25), custom_call_target="tpu_custom_call" | custom-call | tf_op jit(solution)/shard_map/pallas_call | solution.py:87
  36.3 12.2 %all_to_all.21 = f32[32,1,8,128]{3,2,1,0:T(8,128)S(1)} all-to-all(f32[32,1,8,128]{3,2,1,0:T(8,128)S(1)} %bitcast.24), channel_id=1, replica_groups=mesh['fib'=8,'blk'=4] {'fib','blk'}, dimensions={0} | all-to-all | bytes 262144 | tf_op jit(solution)/shard_map/all_to_all | solution.py:165
  48.6 10.1 %all_to_all.22 = f32[32,1,8,128]{3,2,1,0:T(8,128)S(1)} all-to-all(f32[32,1,8,128]{3,2,1,0:T(8,128)S(1)} %broadcast_in_dim.2), channel_id=1, replica_groups=mesh['fib'=8,'blk'=4] {'fib','blk'}, dimensions={0} | all-to-all | bytes 262144 | tf_op jit(solution)/shard_map/all_to_all | solution.py:167
  58.7 3.1 %shard_map.30 = f32[8,9,8,128]{3,2,1,0:T(8,128)S(1)} custom-call(f32[8,528,128]{2,1,0:T(8,128)S(1)} %all_to_all.20.cells_ref, f32[64,512]{1,0:T(8,128)S(1)} %bitcast.23), custom_call_target="tpu_custom_call" | custom-call | tf_op jit(solution)/shard_map/pallas_call | solution.py:149
  61.8 9.7 %all_to_all.23 = f32[8,9,8,128]{3,2,1,0:T(8,128)S(1)} all-to-all(f32[8,9,8,128]{3,2,1,0:T(8,128)S(1)} %shard_map.30), channel_id=1, replica_groups=mesh['fib'=8,'blk'=4] {'fib'}, dimensions={0} | all-to-all | bytes 589824 | tf_op jit(solution)/shard_map/all_to_all | solution.py:182
  71.4 0.1 reshape_squeeze.3
  71.6 0.1 reshape.35
  71.7 0.7 %pad_maximum_fusion = f32[66,8,128]{2,1,0:T(8,128)} fusion(f32[2,8,128]{2,1,0:T(8,128)S(1)} %reshape.35, f32[64,8,128]{2,1,0:T(8,128)S(1)} %bitcast.26), kind=kLoop, calls=%fused_computation | loop fusion | flops 67584 | bytes 540672 | tf_op jit(solution)/shard_map/concatenate | solution.py:186
  (5 shorter events, 0.1 us)
Async XLA Ops:
  0.0 1.6 %copy-start = (f32[33,2,64,128]{3,2,1,0:T(8,128)S(1)}, f32[33,2,64,128]{3,2,1,0:T(8,128)}, u32[]{:S(2)}) copy-start(f32[33,2,64,128]{3,2,1,0:T(8,128)} %param.2) | copy-start | bytes 6488068
  2.0 32.4 %copy-start.1 = (f32[512,64]{0,1:T(8,128)S(1)}, f32[512,64]{0,1:T(8,128)}, u32[]{:S(2)}) copy-start(f32[512,64]{0,1:T(8,128)} %param.3) | copy-start | bytes 393220

commit v3 on v2

--- a/solution.py
+++ b/solution.py
@@ -35,62 +35,90 @@
     return jnp.concatenate(halves(value), axis=0)
 
 
-def pack_kernel(cells, slabs_ref, left_ref, send_ref, turned):
-    own, width, ny = slabs_ref.shape
-    left = left_ref.shape[0]
-    g = pl.program_id(0)
-
-    @pl.when(g == 0)
-    def _():
-        turned[:, : left * width] = left_ref[...].reshape(left * width, ny).T
-
-    send_ref[0, : own * width] = slabs_ref[...].reshape(own * width, ny)
-    send_ref[0, own * width :] = turned[pl.ds(pl.multiple_of(g * cells, cells), cells), :]
-
-
-def pack(slabs, n, own, left):
-    total, width, ny = slabs.shape
+def partners(n):
+    return [[(i, i ^ k) for i in range(n)] for k in range(1, n)]
+
+
+def reorder(value, me, n):
+    width = value.shape[1] // n
+    bit = 1
+    while bit < n:
+        step = bit * width
+        parts = [value[:, i * step : (i + 1) * step] for i in range(n // bit)]
+        swapped = jnp.concatenate([parts[i ^ 1] for i in range(n // bit)], axis=1)
+        value = jnp.where((me & bit) != 0, swapped, value)
+        bit *= 2
+    return value
+
+
+def pack_kernel(n, own, left, width, me_ref, rows_ref, *refs):
+    blocks, (turned, rest, sems) = refs[:n], refs[n:]
+    ny = rows_ref.shape[1]
     cells = ny // n
-    rows = own * width + cells
+    me = me_ref[0]
+    first = pltpu.make_async_copy(rows_ref.at[pl.ds(n * own * width, left * width)], rest, sems.at[n])
+    first.start()
+    copies = []
+    for k, block in enumerate(blocks):
+        source = rows_ref.at[pl.ds((me ^ k) * (own * width), own * width)]
+        copies.append(pltpu.make_async_copy(source, block.at[pl.ds(0, own * width)], sems.at[k]))
+        copies[-1].start()
+    first.wait()
+    turned[:, : left * width] = rest[...].T
+    for k, block in enumerate(blocks):
+        at = pl.multiple_of((me ^ k) * cells, cells)
+        block[own * width :] = turned[pl.ds(at, cells), :]
+    for copy in copies:
+        copy.wait()
+
+
+def pack(rows, me, n, own, left, width):
+    ny = rows.shape[1]
     return pl.pallas_call(
-        functools.partial(pack_kernel, cells),
-        grid=(n,),
-        in_specs=[
-            pl.BlockSpec((own, width, ny), lambda g: (g, 0, 0)),
-            pl.BlockSpec((left, width, ny), lambda g: (n * own // left, 0, 0)),
+        functools.partial(pack_kernel, n, own, left, width),
+        in_specs=[pl.BlockSpec(memory_space=pltpu.SMEM), pl.BlockSpec(memory_space=pltpu.HBM)],
+        out_specs=[pl.BlockSpec(memory_space=pltpu.VMEM)] * n,
+        out_shape=[jax.ShapeDtypeStruct((own * width + ny // n, ny), F32)] * n,
+        scratch_shapes=[
+            pltpu.VMEM((ny, ny), F32),
+            pltpu.VMEM((left * width, ny), F32),
+            pltpu.SemaphoreType.DMA((n + 1,)),
         ],
-        out_specs=pl.BlockSpec((1, rows, ny), lambda g: (g, 0, 0)),
-        out_shape=jax.ShapeDtypeStruct((n, rows, ny), F32),
-        scratch_shapes=[pltpu.VMEM((ny, ny), F32)],
         compiler_params=PARAMS,
-    )(slabs, slabs)
-
-
-def by_cell(rest_ref, left, width):
-    blocks = [rest_ref[f] for f in range(rest_ref.shape[0])]
+    )(me, rows)
+
+
+def by_cell(refs, own, left, width):
+    blocks = [ref[own * width :] for ref in refs]
     slabs = [[block[:, k * width : (k + 1) * width] for block in blocks] for k in range(left)]
     return jnp.concatenate([jnp.concatenate(parts, axis=1) for parts in slabs], axis=0)
 
 
-def raw_kernel(own, left, width, cells_ref, start_ref, out_ref):
-    n, _, ny = cells_ref.shape
-    start = stack(start_ref[...])
-    rest = halves(by_cell(cells_ref.at[:, own * width :], left, width))
+def slab_of(refs, s, width):
+    return halves(jnp.concatenate([ref[s * width : (s + 1) * width] for ref in refs], axis=0))
+
+
+def raw_kernel(own, left, width, me_ref, start_ref, *refs):
+    refs, out_ref = refs[:-1], refs[-1]
+    n, me = len(refs), me_ref[0]
+    start = stack(reorder(start_ref[...], me, n))
+    rest = halves(by_cell(refs, own, left, width))
     total = dot_split(stack(dot_split(start, rest, NT)), rest, NN)
     for s in range(own):
-        slab = halves(cells_ref[:, s * width : (s + 1) * width].reshape(n * width, ny))
+        slab = slab_of(refs, s, width)
         total += dot_split(stack(dot_split(start, slab, NN)), slab, NT)
-    out_ref[...] = total
-
-
-def raw_basis(received, start_t, own, left, width):
+    out_ref[...] = reorder(total, me, n)
+
+
+def raw_basis(blocks, start_t, me, own, left, width):
+    specs = [pl.BlockSpec(memory_space=pltpu.SMEM)] + [pl.BlockSpec(memory_space=pltpu.VMEM)] * (len(blocks) + 1)
     return pl.pallas_call(
         functools.partial(raw_kernel, own, left, width),
-        in_specs=[pl.BlockSpec(memory_space=pltpu.VMEM)] * 2,
+        in_specs=specs,
         out_specs=pl.BlockSpec(memory_space=pltpu.VMEM),
         out_shape=jax.ShapeDtypeStruct(start_t.shape, F32),
         compiler_params=PARAMS,
-    )(received, start_t)
+    )(me, start_t, *blocks)
 
 
 def inverse_factor(gram):
@@ -126,33 +154,31 @@
     return jnp.concatenate(inverse, axis=0)
 
 
-def core_kernel(own, left, width, cells_ref, raw_ref, out_ref):
-    n, rows, ny = cells_ref.shape
-    cells = rows - own * width
+def core_kernel(own, left, width, me_ref, raw_ref, *refs):
+    refs, out_ref = refs[:-1], refs[-1]
+    n, ny = len(refs), out_ref.shape[-1]
     rank = raw_ref.shape[0]
     each = rank // n
-    raw = raw_ref[...]
+    raw = reorder(raw_ref[...], me_ref[0], n)
     gram = lax.dot_general(raw, raw, NT, precision=HIGHEST, preferred_element_type=F32)
     basis = lax.dot_general(inverse_factor(gram), raw, NN, precision=HIGHEST, preferred_element_type=F32)
     basis = stack(basis)
     for s in range(own):
-        slab = halves(cells_ref[:, s * width : (s + 1) * width].reshape(n * width, ny))
-        out_ref[:, s] = dot_split(basis, slab, NN).reshape(n, each, ny)
-    rest = halves(by_cell(cells_ref.at[:, own * width :], left, width))
-    value = dot_split(basis, rest, NT)
-    value = jnp.concatenate([value, jnp.zeros((rank, ny - left * cells), F32)], axis=1)
+        out_ref[:, s] = dot_split(basis, slab_of(refs, s, width), NN).reshape(n, each, ny)
+    value = dot_split(basis, halves(by_cell(refs, own, left, width)), NT)
+    value = jnp.concatenate([value, jnp.zeros((rank, ny - value.shape[1]), F32)], axis=1)
     out_ref[:, own] = value.reshape(n, each, ny)
 
 
-def core(received, raw_t, own, left, width):
-    n, _, ny = received.shape
+def core(blocks, raw_t, me, own, left, width):
+    n, ny = len(blocks), blocks[0].shape[-1]
     return pl.pallas_call(
         functools.partial(core_kernel, own, left, width),
-        in_specs=[pl.BlockSpec(memory_space=pltpu.VMEM)] * 2,
+        in_specs=[pl.BlockSpec(memory_space=pltpu.SMEM)] + [pl.BlockSpec(memory_space=pltpu.VMEM)] * (n + 1),
         out_specs=pl.BlockSpec(memory_space=pltpu.VMEM),
         out_shape=jax.ShapeDtypeStruct((n, own + 1, raw_t.shape[0] // n, ny), F32),
         compiler_params=PARAMS,
-    )(received, raw_t)
+    )(me, raw_t, *blocks)
 
 
 def sum_over_devices(raw_t, devices):
@@ -174,11 +200,12 @@
     total = species * planes
     own, left = divmod(total, n)
     cells, each = ny // n, rank // n
-    slabs = field_data.reshape(total, width, ny)
-    send = pack(slabs, n, own, left)
-    received = lax.all_to_all(send, "fib", split_axis=0, concat_axis=0, tiled=True)
-    raw_t = sum_over_devices(raw_basis(received, start_block.T, own, left, width), devices)
-    core_send = core(received, raw_t, own, left, width)
+    me = lax.axis_index("fib").astype(jnp.int32).reshape(1)
+    blocks = pack(field_data.reshape(total * width, ny), me, n, own, left, width)
+    got = [lax.ppermute(block, "fib", pairs) for block, pairs in zip(blocks[1:], partners(n))]
+    blocks = [blocks[0], *got]
+    raw_t = sum_over_devices(raw_basis(blocks, start_block.T, me, own, left, width), devices)
+    core_send = core(blocks, raw_t, me, own, left, width)
     core_got = lax.all_to_all(core_send, "fib", split_axis=0, concat_axis=0, tiled=True)
     out_main = core_got[:, :own].reshape(n * own, each, ny)
     out_rest = core_got[:, own, :, : left * cells].reshape(n, each, left, cells)

time: 72.7 us -> 71.3 us (0.981)
  blocking collectives: 64.3 us -> 34.3 us
  waiting for transfers between devices: 0 us -> 19.3 us
  starting transfers between devices: 0 us -> 9.26 us
    all_to_all x1 -> x0, blocking collectives: 32.4 us -> none  [shards(): lax.all_to_all(send, 'fib', split_axis=0, concat_axis=0, tiled=True)]
    ppermute x0 -> x7, waiting for transfers between devices: none -> 19.3 us  [shards(): lax.ppermute(block, 'fib', pairs)]
    ppermute x0 -> x7, starting transfers between devices: none -> 9.26 us  [shards(): lax.ppermute(block, 'fib', pairs)]
    all_to_all x1, blocking collectives: 12.2 us -> 14.5 us  [sum_over_devices(): lax.all_to_all(parts, ('fib', 'blk'), split_axis=0, concat_axis=0, tiled=...]
  transfers between devices with their start and end apart: 0 -> 7, of which waited for: 0 -> 3; matrix products, arithmetic and copies ran while one was open for 0% -> 0% of each run, Pallas kernels for 0% -> 0%
where the time goes in v3:
time: 71.3 us; the launch traced here: 71.1 us
  blocking collectives  34.3 us (48%)
  waiting for transfers between devices  19.3 us (27%)
  starting transfers between devices  9.26 us (13%)
  Pallas kernels  5.66 us (8%)
  local copies, waits for them, and re-layouts  1.85 us (3%)
  other arithmetic  0.76 us (1%)
    ppermute x7, waiting for transfers between devices, shards(): lax.ppermute(block, 'fib', pairs)  19.3 us
    all_to_all x1, blocking collectives, sum_over_devices(): lax.all_to_all(parts, ('fib', 'blk'), split_axis=0, concat_axis=0, tiled=...  14.5 us
    all_to_all x1, blocking collectives, sum_over_devices(): lax.all_to_all(mine, ('fib', 'blk'), split_axis=0, concat_axis=0, tiled=T...  10.1 us
    all_to_all x1, blocking collectives, shards(): lax.all_to_all(core_send, 'fib', split_axis=0, concat_axis=0, tiled=True)  9.66 us
    ppermute x7, starting transfers between devices, shards(): lax.ppermute(block, 'fib', pairs)  9.26 us
    pallas_call x1, Pallas kernels, core(): pl.pallas_call(functools.partial(core_kernel, own, left, width), in_specs...  3.21 us
    pallas_call x1, Pallas kernels, raw_basis(): pl.pallas_call(functools.partial(raw_kernel, own, left, width), in_specs=...  2.03 us
    unnamed x4, local copies, waits for them, and re-layouts  1.61 us
  transfers between devices with their start and end apart: 7, of which 3 were waited for; matrix products, arithmetic and copies ran while one was open for 0% of the time, Pallas kernels for 0%

profile of v3, /device:TPU:0, one launch (start us, length us, event | category | flops | bytes accessed | tf_op | source)
XLA Modules:
  0.0 71.1 jit_solution(2573480883104967987)
XLA Ops:
  0.0 0.0 copy-start
  0.0 1.6 %copy-done = f32[33,2,64,128]{3,2,1,0:T(8,128)S(1)} copy-done((f32[33,2,64,128]{3,2,1,0:T(8,128)S(1)}, f32[33,2,64,128]{3,2,1,0:T(8,128)}, u32[]{:S(2)}) %copy-start) | copy-done | bytes 2162712
  1.6 0.0 copy-start.1
  1.6 0.4 shard_map.28
  2.0 0.5 collective-permute-start
  2.6 2.6 %collective-permute-start.1 = (f32[528,128]{1,0:T(8,128)S(1)}, f32[528,128]{1,0:T(8,128)S(1)}, u32[]{:S(2)}, u32[]{:S(2)}) collective-permute-start(f32[528,128]{1,0:T(8,128)S(1)} %get-tuple-element.15), channel_id=1, source_target_pairs={{0,8},{4,12},{8,0},{12,4},{16,24},{20,28},{24,16},{28,20},{1,9},{5... | collective-permute-start | bytes 811016 | tf_op jit(solution)/shard_map/ppermute | solution.py:205
  5.1 0.1 collective-permute-start.2
  5.2 1.8 %collective-permute-start.3 = (f32[528,128]{1,0:T(8,128)S(1)}, f32[528,128]{1,0:T(8,128)S(1)}, u32[]{:S(2)}, u32[]{:S(2)}) collective-permute-start(f32[528,128]{1,0:T(8,128)S(1)} %get-tuple-element.17), channel_id=1, source_target_pairs={{0,16},{4,20},{8,24},{12,28},{16,0},{20,4},{24,8},{28,12},{1,17},{... | collective-permute-start | bytes 811016 | tf_op jit(solution)/shard_map/ppermute | solution.py:205
  7.0 0.0 collective-permute-start.4
  7.0 0.0 collective-permute-done.refs_1_
  7.0 2.6 %collective-permute-start.5 = (f32[528,128]{1,0:T(8,128)S(1)}, f32[528,128]{1,0:T(8,128)S(1)}, u32[]{:S(2)}, u32[]{:S(2)}) collective-permute-start(f32[528,128]{1,0:T(8,128)S(1)} %get-tuple-element.19), channel_id=1, source_target_pairs={{0,24},{4,28},{8,16},{12,20},{16,8},{20,12},{24,0},{28,4},{1,25},{... | collective-permute-start | bytes 811016 | tf_op jit(solution)/shard_map/ppermute | solution.py:205
  9.6 2.9 %collective-permute-done.1.refs_2_ = f32[528,128]{1,0:T(8,128)S(1)} collective-permute-done((f32[528,128]{1,0:T(8,128)S(1)}, f32[528,128]{1,0:T(8,128)S(1)}, u32[]{:S(2)}, u32[]{:S(2)}) %collective-permute-start.1) | collective-permute-done | bytes 270368 | tf_op jit(solution)/shard_map/ppermute | solution.py:205
  12.5 1.7 %collective-permute-start.6 = (f32[528,128]{1,0:T(8,128)S(1)}, f32[528,128]{1,0:T(8,128)S(1)}, u32[]{:S(2)}, u32[]{:S(2)}) collective-permute-start(f32[528,128]{1,0:T(8,128)S(1)} %get-tuple-element.20), channel_id=1, source_target_pairs={{0,28},{4,24},{8,20},{12,16},{16,12},{20,8},{24,4},{28,0},{1,29},{... | collective-permute-start | bytes 811016 | tf_op jit(solution)/shard_map/ppermute | solution.py:205
  14.2 3.5 %collective-permute-done.2.refs_3_ = f32[528,128]{1,0:T(8,128)S(1)} collective-permute-done((f32[528,128]{1,0:T(8,128)S(1)}, f32[528,128]{1,0:T(8,128)S(1)}, u32[]{:S(2)}, u32[]{:S(2)}) %collective-permute-start.2) | collective-permute-done | bytes 270368 | tf_op jit(solution)/shard_map/ppermute | solution.py:205
  17.7 0.0 collective-permute-done.3.refs_4_
  17.7 12.8 %collective-permute-done.4.refs_5_ = f32[528,128]{1,0:T(8,128)S(1)} collective-permute-done((f32[528,128]{1,0:T(8,128)S(1)}, f32[528,128]{1,0:T(8,128)S(1)}, u32[]{:S(2)}, u32[]{:S(2)}) %collective-permute-start.4) | collective-permute-done | bytes 270368 | tf_op jit(solution)/shard_map/ppermute | solution.py:205
  30.6 0.0 collective-permute-done.5.refs_6_
  30.6 0.0 collective-permute-done.6.refs_7_
  30.6 0.0 copy-done.1
  30.6 2.0 %shard_map.29 = f32[64,512]{1,0:T(8,128)S(1)} custom-call(s32[1]{0:T(128)} %bitcast.me_ref, f32[64,512]{1,0:T(8,128)S(1)} %bitcast.25, f32[528,128]{1,0:T(8,128)S(1)} %get-tuple-element.13.refs_0_, f32[528,128]{1,0:T(8,128)S(1)} %collective-permute-done.refs_1_, f32[528,128]{1,0:T(8,128)S(1)} %collective-permute-done.1.refs_2_, ...), custom_call_target="tpu_custom_call" | custom-call | tf_op jit(solution)/shard_map/pallas_call | solution.py:115
  32.6 14.5 %all_to_all.15 = f32[32,1,8,128]{3,2,1,0:T(8,128)S(1)} all-to-all(f32[32,1,8,128]{3,2,1,0:T(8,128)S(1)} %bitcast.24), channel_id=1, replica_groups=mesh['fib'=8,'blk'=4] {'fib','blk'}, dimensions={0} | all-to-all | bytes 262144 | tf_op jit(solution)/shard_map/all_to_all | solution.py:191
  47.2 10.1 %all_to_all.16 = f32[32,1,8,128]{3,2,1,0:T(8,128)S(1)} all-to-all(f32[32,1,8,128]{3,2,1,0:T(8,128)S(1)} %broadcast_in_dim.2), channel_id=1, replica_groups=mesh['fib'=8,'blk'=4] {'fib','blk'}, dimensions={0} | all-to-all | bytes 262144 | tf_op jit(solution)/shard_map/all_to_all | solution.py:193
  57.3 3.2 %shard_map.30 = f32[8,9,8,128]{3,2,1,0:T(8,128)S(1)} custom-call(s32[1]{0:T(128)} %bitcast.me_ref, f32[64,512]{1,0:T(8,128)S(1)} %bitcast.23, f32[528,128]{1,0:T(8,128)S(1)} %get-tuple-element.13.refs_0_, f32[528,128]{1,0:T(8,128)S(1)} %collective-permute-done.refs_1_, f32[528,128]{1,0:T(8,128)S(1)} %collective-permute-done.1.refs_2_, ...), custom_call_target="tpu_custom_call" | custom-call | tf_op jit(solution)/shard_map/pallas_call | solution.py:175
  60.5 9.7 %all_to_all.17 = f32[8,9,8,128]{3,2,1,0:T(8,128)S(1)} all-to-all(f32[8,9,8,128]{3,2,1,0:T(8,128)S(1)} %shard_map.30), channel_id=1, replica_groups=mesh['fib'=8,'blk'=4] {'fib'}, dimensions={0} | all-to-all | bytes 589824 | tf_op jit(solution)/shard_map/all_to_all | solution.py:209
  70.2 0.1 reshape_squeeze.3
  70.3 0.1 reshape.39
  70.4 0.7 %pad_maximum_fusion = f32[66,8,128]{2,1,0:T(8,128)} fusion(f32[2,8,128]{2,1,0:T(8,128)S(1)} %reshape.39, f32[64,8,128]{2,1,0:T(8,128)S(1)} %bitcast.26), kind=kLoop, calls=%fused_computation | loop fusion | flops 67584 | bytes 540672 | tf_op jit(solution)/shard_map/concatenate | solution.py:213
  (5 shorter events, 0.1 us)
Async XLA Ops:
  0.0 1.6 %copy-start = (f32[33,2,64,128]{3,2,1,0:T(8,128)S(1)}, f32[33,2,64,128]{3,2,1,0:T(8,128)}, u32[]{:S(2)}) copy-start(f32[33,2,64,128]{3,2,1,0:T(8,128)} %param.2) | copy-start | bytes 6488068
  1.6 29.0 %copy-start.1 = (f32[512,64]{0,1:T(8,128)S(1)}, f32[512,64]{0,1:T(8,128)}, u32[]{:S(2)}) copy-start(f32[512,64]{0,1:T(8,128)} %param.3) | copy-start | bytes 393220
  2.0 4.9 %collective-permute-start = (f32[528,128]{1,0:T(8,128)S(1)}, f32[528,128]{1,0:T(8,128)S(1)}, u32[]{:S(2)}, u32[]{:S(2)}) collective-permute-start(f32[528,128]{1,0:T(8,128)S(1)} %get-tuple-element.14), channel_id=1, source_target_pairs={{0,4},{4,0},{8,12},{12,8},{16,20},{20,16},{24,28},{28,24},{1,5},{5... | collective-permute-start | bytes 811016 | tf_op jit(solution)/shard_map/ppermute | solution.py:205
  2.6 9.9 %collective-permute-start.1 = (f32[528,128]{1,0:T(8,128)S(1)}, f32[528,128]{1,0:T(8,128)S(1)}, u32[]{:S(2)}, u32[]{:S(2)}) collective-permute-start(f32[528,128]{1,0:T(8,128)S(1)} %get-tuple-element.15), channel_id=1, source_target_pairs={{0,8},{4,12},{8,0},{12,4},{16,24},{20,28},{24,16},{28,20},{1,9},{5... | collective-permute-start | bytes 811016 | tf_op jit(solution)/shard_map/ppermute | solution.py:205
  5.1 12.6 %collective-permute-start.2 = (f32[528,128]{1,0:T(8,128)S(1)}, f32[528,128]{1,0:T(8,128)S(1)}, u32[]{:S(2)}, u32[]{:S(2)}) collective-permute-start(f32[528,128]{1,0:T(8,128)S(1)} %get-tuple-element.16), channel_id=1, source_target_pairs={{0,12},{4,8},{8,4},{12,0},{16,28},{20,24},{24,20},{28,16},{1,13},{... | collective-permute-start | bytes 811016 | tf_op jit(solution)/shard_map/ppermute | solution.py:205
  5.2 12.5 %collective-permute-start.3 = (f32[528,128]{1,0:T(8,128)S(1)}, f32[528,128]{1,0:T(8,128)S(1)}, u32[]{:S(2)}, u32[]{:S(2)}) collective-permute-start(f32[528,128]{1,0:T(8,128)S(1)} %get-tuple-element.17), channel_id=1, source_target_pairs={{0,16},{4,20},{8,24},{12,28},{16,0},{20,4},{24,8},{28,12},{1,17},{... | collective-permute-start | bytes 811016 | tf_op jit(solution)/shard_map/ppermute | solution.py:205
  7.0 23.6 %collective-permute-start.4 = (f32[528,128]{1,0:T(8,128)S(1)}, f32[528,128]{1,0:T(8,128)S(1)}, u32[]{:S(2)}, u32[]{:S(2)}) collective-permute-start(f32[528,128]{1,0:T(8,128)S(1)} %get-tuple-element.18), channel_id=1, source_target_pairs={{0,20},{4,16},{8,28},{12,24},{16,4},{20,0},{24,12},{28,8},{1,21},{... | collective-permute-start | bytes 811016 | tf_op jit(solution)/shard_map/ppermute | solution.py:205
  7.0 23.6 %collective-permute-start.5 = (f32[528,128]{1,0:T(8,128)S(1)}, f32[528,128]{1,0:T(8,128)S(1)}, u32[]{:S(2)}, u32[]{:S(2)}) collective-permute-start(f32[528,128]{1,0:T(8,128)S(1)} %get-tuple-element.19), channel_id=1, source_target_pairs={{0,24},{4,28},{8,16},{12,20},{16,8},{20,12},{24,0},{28,4},{1,25},{... | collective-permute-start | bytes 811016 | tf_op jit(solution)/shard_map/ppermute | solution.py:205
  12.5 18.1 %collective-permute-start.6 = (f32[528,128]{1,0:T(8,128)S(1)}, f32[528,128]{1,0:T(8,128)S(1)}, u32[]{:S(2)}, u32[]{:S(2)}) collective-permute-start(f32[528,128]{1,0:T(8,128)S(1)} %get-tuple-element.20), channel_id=1, source_target_pairs={{0,28},{4,24},{8,20},{12,16},{16,12},{20,8},{24,4},{28,0},{1,29},{... | collective-permute-start | bytes 811016 | tf_op jit(solution)/shard_map/ppermute | solution.py:205

commit v4 on v0

v4 whole, which is shorter than its diff:
```python
import functools

import jax
import jax.numpy as jnp
from jax import lax
from jax.experimental import pallas as pl
from jax.experimental.pallas import tpu as pltpu
from jax.sharding import PartitionSpec as P

F32, BF16 = jnp.float32, jnp.bfloat16
HIGHEST = lax.Precision.HIGHEST
NN = (((1,), (0,)), ((), ()))
NT = (((1,), (1,)), ((), ()))
PARAMS = pltpu.CompilerParams(vmem_limit_bytes=40 * 1024 * 1024)
VMEM = pl.BlockSpec(memory_space=pltpu.VMEM)
SMEM = pl.BlockSpec(memory_space=pltpu.SMEM)
HBM = pl.BlockSpec(memory_space=pltpu.HBM)


def halves(value):
    high = value.astype(BF16)
    return high, (value - high.astype(F32)).astype(BF16)


def stack(value):
    return jnp.concatenate(halves(value), axis=0)


def dot(left, right, dims):
    return lax.dot_general(left, right, dims, preferred_element_type=F32)


def dot_split(left, right, dims):
    rows = left.shape[0] // 2
    right_high, right_low = right
    both = dot(left, right_high, dims)
    return both[:rows] + both[rows:] + dot(left[:rows], right_low, dims)


def reorder(value, me, n, axis):
    width = value.shape[axis] // n
    bit = 1
    while bit < n:
        parts = [lax.slice_in_dim(value, i * bit * width, (i + 1) * bit * width, axis=axis) for i in range(n // bit)]
        swapped = jnp.concatenate([parts[i ^ 1] for i in range(n // bit)], axis=axis)
        value = jnp.where((me & bit) != 0, swapped, value)
        bit *= 2
    return value


def exchange(value, axis, mask, size):
    return lax.ppermute(value, axis, [(i, i ^ mask) for i in range(size)])


def pack_kernel(chips, first, last, own, left, width, me_ref, rows_ref, *refs):
    blocks, refs = refs[:chips], refs[chips:]
    ny = rows_ref.shape[1]
    chip = lax.div(me_ref[0], 2)
    sems = refs[-1]
    count = (last - first) * width
    if left:
        turned, rest = refs[:2]
        rest_copy = pltpu.make_async_copy(rows_ref.at[pl.ds(chips * own * width, left * width)], rest, sems.at[chips])
        rest_copy.start()
    copies = []
    for k, block in enumerate(blocks):
        at = pl.multiple_of(((chip ^ k) * own + first) * width, 8)
        copies.append(pltpu.make_async_copy(rows_ref.at[pl.ds(at, count)], block.at[pl.ds(0, count)], sems.at[k]))
        copies[-1].start()
    if left:
        cells = ny // chips
        rest_copy.wait()
        turned[:, : left * width] = rest[...].T
        for k, block in enumerate(blocks):
            block[count:] = turned[pl.ds(pl.multiple_of((chip ^ k) * cells, cells), cells), :]
    for copy in copies:
        copy.wait()


def pack(rows, me, chips, first, last, own, left, width):
    ny = rows.shape[1]
    high = (last - first) * width + (ny // chips if left else 0)
    scratch = [pltpu.VMEM((ny, ny), F32), pltpu.VMEM((left * width, ny), F32)] if left else []
    return pl.pallas_call(
        functools.partial(pack_kernel, chips, first, last, own, left, width),
        in_specs=[SMEM, HBM],
        out_specs=[VMEM] * chips,
        out_shape=[jax.ShapeDtypeStruct((high, ny), F32)] * chips,
        scratch_shapes=scratch + [pltpu.SemaphoreType.DMA((chips + 1,))],
        compiler_params=PARAMS,
    )(me, rows)


def slabs_of(refs, count, width):
    ny = refs[0].shape[1]
    for s in range(0, count, 2):
        pair = range(s, min(s + 2, count))
        columns = [jnp.concatenate([ref[q * width : (q + 1) * width] for ref in refs], axis=0) for q in pair]
        yield s * ny, (s + len(columns)) * ny, halves(jnp.concatenate(columns, axis=1))


def rest_of(refs, count, left, width):
    blocks = [ref[count * width :] for ref in refs]
    slabs = [[block[:, k * width : (k + 1) * width] for block in blocks] for k in range(left)]
    return halves(jnp.concatenate([jnp.concatenate(parts, axis=1) for parts in slabs], axis=0))


def widen(value, lanes):
    return jnp.concatenate([value, jnp.zeros((value.shape[0], lanes - value.shape[1]), F32)], axis=1)


def project_kernel(count, left, width, me_ref, start_ref, *refs):
    refs, out_ref = refs[:-1], refs[-1]
    chips, me, ny = len(refs), me_ref[0], refs[0].shape[1]
    parts = [start_ref[:, i * width : (i + 1) * width] for i in range(2 * chips)]
    odd = (me & 1) != 0
    start = jnp.where(odd, jnp.concatenate(parts[1::2], axis=1), jnp.concatenate(parts[::2], axis=1))
    start = stack(reorder(start, lax.div(me, 2), chips, 1))
    for at, to, slab in slabs_of(refs, count, width):
        out_ref[:, at:to] = dot_split(start, slab, NN)
    if left:
        out_ref[:, count * ny :] = widen(dot_split(start, rest_of(refs, count, left, width), NT), ny)


def project(blocks, start_t, me, count, left, width):
    ny = blocks[0].shape[1]
    return pl.pallas_call(
        functools.partial(project_kernel, count, left, width),
        in_specs=[SMEM] + [VMEM] * (1 + len(blocks)),
        out_specs=VMEM,
        out_shape=jax.ShapeDtypeStruct((start_t.shape[0], (count + (left > 0)) * ny), F32),
        compiler_params=PARAMS,
    )(me, start_t, *blocks)


def raw_kernel(count, left, width, more, last, me_ref, mine_ref, other_ref, *refs):
    refs, out_ref = refs[:-1], refs[-1]
    if more:
        refs, total = refs[:-1], refs[-1][...]
    else:
        total = jnp.zeros(out_ref.shape, F32)
    ny = refs[0].shape[1]
    for at, to, slab in slabs_of(refs, count, width):
        total += dot_split(stack(mine_ref[:, at:to] + other_ref[:, at:to]), slab, NT)
    if left:
        rest = rest_of(refs, count, left, width)
        lanes = slice(count * ny, count * ny + rest[0].shape[0])
        total += dot_split(stack(mine_ref[:, lanes] + other_ref[:, lanes]), rest, NN)
    if last:
        total = reorder(total, lax.div(me_ref[0], 2), len(refs), 1)
    out_ref[...] = total


def raw_part(blocks, mine, other, before, me, count, left, width, last):
    more = [] if before is None else [before]
    return pl.pallas_call(
        functools.partial(raw_kernel, count, left, width, bool(more), last),
        in_specs=[SMEM] + [VMEM] * (2 + len(blocks) + len(more)),
        out_specs=VMEM,
        out_shape=jax.ShapeDtypeStruct((mine.shape[0], len(blocks) * width), F32),
        compiler_params=PARAMS,
    )(me, mine, other, *blocks, *more)


def sum_over(value, axis, low, size):
    while low < size:
        masks = [low] if 2 * low >= size else [low, 2 * low, 3 * low]
        got = [exchange(value, axis, mask, size) for mask in masks]
        for term in got:
            value = value + term
        low *= len(masks) + 1
    return value


def gram_kernel(raw_ref, out_ref):
    raw = raw_ref[...]
    out_ref[...] = lax.dot_general(raw, raw, NT, precision=HIGHEST, preferred_element_type=F32)


def gram_part(raw):
    return pl.pallas_call(
        gram_kernel,
        in_specs=[VMEM],
        out_specs=VMEM,
        out_shape=jax.ShapeDtypeStruct((raw.shape[0], raw.shape[0]), F32),
        compiler_params=PARAMS,
    )(raw)


def inverse_factor(gram):
    rank = gram.shape[0]
    row = lax.broadcasted_iota(jnp.int32, (rank, rank), 0)
    col = lax.broadcasted_iota(jnp.int32, (rank, rank), 1)
    table = jnp.concatenate([gram, jnp.where(row == col, 1.0, 0.0).astype(F32)], axis=1)
    rows = [table[8 * b : 8 * b + 8] for b in range(rank // 8)]
    wide = rows[0].shape
    sub = lax.broadcasted_iota(jnp.int32, wide, 0)

    def spread(value, k):
        return jnp.broadcast_to(value[k : k + 1], wide)

    inverse = []
    for b in range(len(rows)):
        columns = [
            [jnp.broadcast_to(block[:, 8 * b + k : 8 * b + k + 1], wide) for k in range(8)] for block in rows[b:]
        ]
        pivots = jnp.ones(wide, F32)
        for k in range(8):
            pivot = spread(columns[0][k], k)
            pivots = jnp.where(sub == k, pivot, pivots)
            scale = 1.0 / pivot
            scaled = spread(rows[b], k) * scale
            ahead = [spread(columns[0][m], k) * scale for m in range(k + 1, 8)]
            for i, column in enumerate(columns):
                factor = jnp.where(sub > k, column[k], 0.0) if i == 0 else column[k]
                for m in range(k + 1, 8):
                    column[m] = column[m] - factor * ahead[m - k - 1]
                rows[b + i] = rows[b + i] - factor * scaled
        inverse.append(rows[b][:, rank:] * lax.rsqrt(pivots[:, rank:]))
    return jnp.concatenate(inverse, axis=0)


def core_kernel(counts, left, width, me_ref, mine_ref, other_ref, raw_ref, *refs):
    refs, (keep_ref, send_ref) = refs[:-2], refs[-2:]
    chips = keep_ref.shape[0]
    rank, (each, ny) = raw_ref.shape[0], keep_ref.shape[-2:]
    me = me_ref[0]
    inverse = inverse_factor(mine_ref[...] + other_ref[...])
    inverse = reorder(inverse, me, 2 * chips, 0)
    raw = reorder(raw_ref[...], lax.div(me, 2), chips, 1)
    basis = stack(lax.dot_general(inverse, raw, NN, precision=HIGHEST, preferred_element_type=F32))

    def put(slab, value):
        for k in range(chips):
            keep_ref[k, slab] = value[2 * k * each : (2 * k + 1) * each]
            send_ref[k, slab] = value[(2 * k + 1) * each : (2 * k + 2) * each]

    done = 0
    for c, count in enumerate(counts):
        blocks = refs[c * chips : (c + 1) * chips]
        for at, to, slab in slabs_of(blocks, count, width):
            value = dot_split(basis, slab, NN)
            for lane in range(0, to - at, ny):
                put(done + (at + lane) // ny, value[:, lane : lane + ny])
        done += count
    put(done, widen(dot_split(basis, rest_of(blocks, count, left, width), NT), ny))


def core(blocks, mine, other, raw, me, counts, left, width, each):
    chips, ny = len(blocks) // len(counts), blocks[0].shape[1]
    shape = jax.ShapeDtypeStruct((chips, sum(counts) + 1, each, ny), F32)
    return pl.pallas_call(
        functools.partial(core_kernel, counts, left, width),
        in_specs=[SMEM] + [VMEM] * (3 + len(blocks)),
        out_specs=[VMEM] * 2,
        out_shape=[shape] * 2,
        compiler_params=PARAMS,
    )(me, mine, other, raw, *blocks)


def add_kernel(keep_ref, got_ref, *outs):
    for k, out in enumerate(outs):
        out[...] = keep_ref[k] + got_ref[k]


def add_parts(keep, got):
    chips = keep.shape[0]
    return pl.pallas_call(
        add_kernel,
        in_specs=[VMEM] * 2,
        out_specs=[VMEM] * chips,
        out_shape=[jax.ShapeDtypeStruct(keep.shape[1:], F32)] * chips,
        compiler_params=PARAMS,
    )(keep, got)


def place_kernel(own, left, cells, me_ref, *refs):
    refs, (out_ref, rest, sems) = refs[:-3], refs[-3:]
    chips = len(refs)
    chip = lax.div(me_ref[0], 2)
    copies = []
    for k, ref in enumerate(refs):
        to = out_ref.at[pl.ds((chip ^ k) * own, own)]
        copies.append(pltpu.make_async_copy(ref.at[pl.ds(0, own)], to, sems.at[k]))
        copies[-1].start()
    for k in range(left):
        parts = [ref[own][:, k * cells : (k + 1) * cells] for ref in refs]
        rest[k] = reorder(jnp.concatenate(parts, axis=1), chip, chips, 1)
    copies.append(pltpu.make_async_copy(rest, out_ref.at[pl.ds(chips * own, left)], sems.at[chips]))
    copies[-1].start()
    for copy in copies:
        copy.wait()


def place(parts, me, own, left):
    chips = len(parts)
    _, each, ny = parts[0].shape
    return pl.pallas_call(
        functools.partial(place_kernel, own, left, ny // chips),
        in_specs=[SMEM] + [VMEM] * chips,
        out_specs=HBM,
        out_shape=jax.ShapeDtypeStruct((chips * own + left, each, ny), F32),
        scratch_shapes=[pltpu.VMEM((left, each, ny), F32), pltpu.SemaphoreType.DMA((chips + 1,))],
        compiler_params=PARAMS,
    )(me, *parts)


def shards(n, layers, field_data, start_block):
    species, planes, width, ny = field_data.shape
    chips, each = n // 2, start_block.shape[1] // n
    total = species * planes
    own, left = divmod(total, chips)
    counts = [own - own // 2, own // 2]
    me = lax.axis_index("fib").astype(jnp.int32).reshape(1)
    rows = field_data.reshape(total * width, ny)
    start_t = start_block.T
    blocks, raw, first = [], None, 0
    for c, count in enumerate(counts):
        rest = left if c == len(counts) - 1 else 0
        sent = pack(rows, me, chips, first, first + count, own, rest, width)
        part = [sent[0]] + [exchange(sent[k], "fib", 2 * k, n) for k in range(1, chips)]
        mine = project(part, start_t, me, count, rest, width)
        other = exchange(mine, "fib", 1, n)
        raw = raw_part(part, mine, other, raw, me, count, rest, width, c == len(counts) - 1)
        blocks += part
        first += count
    raw = sum_over(sum_over(raw, "fib", 2, n), "blk", 1, layers)
    gram = gram_part(raw)
    keep, send = core(blocks, gram, exchange(gram, "fib", 1, n), raw, me, counts, left, width, each)
    parts = add_parts(keep, exchange(send, "fib", 1, n))
    parts = [parts[0]] + [exchange(parts[k], "fib", 2 * k, n) for k in range(1, chips)]
    return place(parts, me, own, left).reshape(species, planes, each, ny)


def solution(mesh):
    n, layers = mesh.shape["fib"], mesh.shape["blk"]
    in_specs = (P(None, "blk", "fib", None), P())
    out_specs = P(None, "blk", "fib", None)
    return jax.shard_map(
        functools.partial(shards, n, layers), mesh=mesh, in_specs=in_specs, out_specs=out_specs, check_vma=False
    )
```

time: 253 us -> 63.9 us (0.25)
  waiting for transfers between devices: 129 us -> 32.7 us
  blocking collectives: 42.8 us -> 0 us
  local copies, waits for them, and re-layouts: 34.3 us -> 1.61 us
  starting transfers between devices: 0.01 us -> 23.1 us
  other arithmetic: 20.9 us -> 0.03 us
  between operations: 13.5 us -> 0.11 us
  matrix products: 11.3 us -> 0 us
  Pallas kernels: 0 us -> 6.22 us
    psum x1 -> x0, waiting for transfers between devices: 129 us -> none  [shards(): gram_total = lax.psum(local_gram, ('fib', 'blk'))]
    all_to_all x2 -> x0, blocking collectives: 42.8 us -> none  [the longest x1 32.4 us: shards(): lax.all_to_all(field_data, 'fib', split_axis=3, concat_axis=2, tiled=True)]
    ppermute x0 -> x19, waiting for transfers between devices: none -> 32.7 us  [exchange(): return lax.ppermute(value, axis, [(i, i ^ mask) for i in range(size)])]
    ppermute x0 -> x19, starting transfers between devices: none -> 23.1 us  [exchange(): return lax.ppermute(value, axis, [(i, i ^ mask) for i in range(size)])]
    unnamed x7 -> x4, local copies, waits for them, and re-layouts: 20.9 us -> 1.61 us
    all_to_all x6 -> x0, local copies, waits for them, and re-layouts: 12.2 us -> none  [the longest x4 11.1 us: shards(): lax.all_to_all(field_data, 'fib', split_axis=3, concat_axis=2, tiled=True)]
    another operation x5 -> x0, other arithmetic: 12.2 us -> none  [the longest x3 6.6 us: shards(): lower_factor = jnp.linalg.cholesky(inner_block)]
    dot_general x4 -> x0, matrix products: 11 us -> none  [the longest x1 5.37 us: shards(): lax.dot_general(unfolded, unfolded, contract_rows, precision=highest)]
  transfers between devices with their start and end apart: 1 -> 19, of which waited for: 1 -> 15; matrix products, arithmetic and copies ran while one was open for 0% -> 0% of each run, Pallas kernels for 0% -> 2%
where the time goes in v4:
time: 63.9 us; the launch traced here: 63.8 us
  waiting for transfers between devices  32.7 us (51%)
  starting transfers between devices  23.1 us (36%)
  Pallas kernels  6.22 us (10%)
  local copies, waits for them, and re-layouts  1.61 us (3%)
    ppermute x19, waiting for transfers between devices, exchange(): return lax.ppermute(value, axis, [(i, i ^ mask) for i in range(size)])  32.7 us
    ppermute x19, starting transfers between devices, exchange(): return lax.ppermute(value, axis, [(i, i ^ mask) for i in range(size)])  23.1 us
    pallas_call x1, Pallas kernels, core(): pl.pallas_call(functools.partial(core_kernel, counts, left, width), in_sp...  2.79 us
    unnamed x4, local copies, waits for them, and re-layouts  1.61 us
  transfers between devices with their start and end apart: 19, of which 15 were waited for; matrix products, arithmetic and copies ran while one was open for 0% of the time, Pallas kernels for 2%

profile of v4, /device:TPU:0, one launch (start us, length us, event | category | flops | bytes accessed | tf_op | source)
XLA Modules:
  0.0 63.8 jit_solution(8174699262923549038)
XLA Ops:
  0.0 1.6 %copy-done = f32[33,2,64,128]{3,2,1,0:T(8,128)S(1)} copy-done((f32[33,2,64,128]{3,2,1,0:T(8,128)S(1)}, f32[33,2,64,128]{3,2,1,0:T(8,128)}, u32[]{:S(2)}) %copy-start) | copy-done | bytes 2162712
  1.9 3.0 %collective-permute-start = (f32[544,128]{1,0:T(8,128)S(1)}, f32[544,128]{1,0:T(8,128)S(1)}, u32[]{:S(2)}, u32[]{:S(2)}) collective-permute-start(f32[544,128]{1,0:T(8,128)S(1)} %get-tuple-element.20), channel_id=1, source_target_pairs={{0,8},{4,12},{8,0},{12,4},{16,24},{20,28},{24,16},{28,20},{1,9},{5... | collective-permute-start | bytes 835592 | tf_op jit(solution)/shard_map/ppermute | solution.py:52
  4.9 1.5 %collective-permute-start.1 = (f32[544,128]{1,0:T(8,128)S(1)}, f32[544,128]{1,0:T(8,128)S(1)}, u32[]{:S(2)}, u32[]{:S(2)}) collective-permute-start(f32[544,128]{1,0:T(8,128)S(1)} %get-tuple-element.21), channel_id=1, source_target_pairs={{0,16},{4,20},{8,24},{12,28},{16,0},{20,4},{24,8},{28,12},{1,17},{... | collective-permute-start | bytes 835592 | tf_op jit(solution)/shard_map/ppermute | solution.py:52
  6.6 2.0 %collective-permute-start.4 = (f32[512,128]{1,0:T(8,128)S(1)}, f32[512,128]{1,0:T(8,128)S(1)}, u32[]{:S(2)}, u32[]{:S(2)}) collective-permute-start(f32[512,128]{1,0:T(8,128)S(1)} %get-tuple-element.24), channel_id=1, source_target_pairs={{0,8},{4,12},{8,0},{12,4},{16,24},{20,28},{24,16},{28,20},{1,9},{5... | collective-permute-start | bytes 786440 | tf_op jit(solution)/shard_map/ppermute | solution.py:52
  8.6 1.5 %collective-permute-start.5 = (f32[512,128]{1,0:T(8,128)S(1)}, f32[512,128]{1,0:T(8,128)S(1)}, u32[]{:S(2)}, u32[]{:S(2)}) collective-permute-start(f32[512,128]{1,0:T(8,128)S(1)} %get-tuple-element.25), channel_id=1, source_target_pairs={{0,16},{4,20},{8,24},{12,28},{16,0},{20,4},{24,8},{28,12},{1,17},{... | collective-permute-start | bytes 786440 | tf_op jit(solution)/shard_map/ppermute | solution.py:52
  10.1 2.3 %collective-permute-done.refs_1_.refs_5_ = f32[544,128]{1,0:T(8,128)S(1)} collective-permute-done((f32[544,128]{1,0:T(8,128)S(1)}, f32[544,128]{1,0:T(8,128)S(1)}, u32[]{:S(2)}, u32[]{:S(2)}) %collective-permute-start) | collective-permute-done | bytes 278560 | tf_op jit(solution)/shard_map/ppermute | solution.py:52
  12.4 3.0 %collective-permute-start.6 = (f32[512,128]{1,0:T(8,128)S(1)}, f32[512,128]{1,0:T(8,128)S(1)}, u32[]{:S(2)}, u32[]{:S(2)}) collective-permute-start(f32[512,128]{1,0:T(8,128)S(1)} %get-tuple-element.26), channel_id=1, source_target_pairs={{0,24},{4,28},{8,16},{12,20},{16,8},{20,12},{24,0},{28,4},{1,25},{... | collective-permute-start | bytes 786440 | tf_op jit(solution)/shard_map/ppermute | solution.py:52
  15.4 5.0 %collective-permute-done.1.refs_2_.refs_6_ = f32[544,128]{1,0:T(8,128)S(1)} collective-permute-done((f32[544,128]{1,0:T(8,128)S(1)}, f32[544,128]{1,0:T(8,128)S(1)}, u32[]{:S(2)}, u32[]{:S(2)}) %collective-permute-start.1) | collective-permute-done | bytes 278560 | tf_op jit(solution)/shard_map/ppermute | solution.py:52
  21.0 3.0 %collective-permute-done.4.refs_1_ = f32[512,128]{1,0:T(8,128)S(1)} collective-permute-done((f32[512,128]{1,0:T(8,128)S(1)}, f32[512,128]{1,0:T(8,128)S(1)}, u32[]{:S(2)}, u32[]{:S(2)}) %collective-permute-start.4) | collective-permute-done | bytes 262176 | tf_op jit(solution)/shard_map/ppermute | solution.py:52
  24.0 6.2 %collective-permute-done.5.refs_2_ = f32[512,128]{1,0:T(8,128)S(1)} collective-permute-done((f32[512,128]{1,0:T(8,128)S(1)}, f32[512,128]{1,0:T(8,128)S(1)}, u32[]{:S(2)}, u32[]{:S(2)}) %collective-permute-start.5) | collective-permute-done | bytes 262176 | tf_op jit(solution)/shard_map/ppermute | solution.py:52
  30.8 1.5 %collective-permute-done.7.other_ref = f32[64,1024]{1,0:T(8,128)S(1)} collective-permute-done((f32[64,1024]{1,0:T(8,128)S(1)}, f32[64,1024]{1,0:T(8,128)S(1)}, u32[]{:S(2)}, u32[]{:S(2)}) %collective-permute-start.7) | collective-permute-done | bytes 262176 | tf_op jit(solution)/shard_map/ppermute | solution.py:52
  32.8 0.6 shard_map.33
  33.4 1.6 %collective-permute-start.10 = (f32[64,256]{1,0:T(8,128)S(1)}, f32[64,256]{1,0:T(8,128)S(1)}, u32[]{:S(2)}, u32[]{:S(2)}) collective-permute-start(f32[64,256]{1,0:T(8,128)S(1)} %shard_map.33), channel_id=1, source_target_pairs={{0,24},{4,28},{8,16},{12,20},{16,8},{20,12},{24,0},{28,4},{1,25},{... | collective-permute-start | bytes 196616 | tf_op jit(solution)/shard_map/ppermute | solution.py:52
  34.9 1.3 %collective-permute-start.9 = (f32[64,256]{1,0:T(8,128)S(1)}, f32[64,256]{1,0:T(8,128)S(1)}, u32[]{:S(2)}, u32[]{:S(2)}) collective-permute-start(f32[64,256]{1,0:T(8,128)S(1)} %shard_map.33), channel_id=1, source_target_pairs={{0,16},{4,20},{8,24},{12,28},{16,0},{20,4},{24,8},{28,12},{1,17},{... | collective-permute-start | bytes 196616 | tf_op jit(solution)/shard_map/ppermute | solution.py:52
  36.2 0.7 %collective-permute-start.8 = (f32[64,256]{1,0:T(8,128)S(1)}, f32[64,256]{1,0:T(8,128)S(1)}, u32[]{:S(2)}, u32[]{:S(2)}) collective-permute-start(f32[64,256]{1,0:T(8,128)S(1)} %shard_map.33), channel_id=1, source_target_pairs={{0,8},{4,12},{8,0},{12,4},{16,24},{20,28},{24,16},{28,20},{1,9},{5... | collective-permute-start | bytes 196616 | tf_op jit(solution)/shard_map/ppermute | solution.py:52
  36.9 1.8 %collective-permute-done.10 = f32[64,256]{1,0:T(8,128)S(1)} collective-permute-done((f32[64,256]{1,0:T(8,128)S(1)}, f32[64,256]{1,0:T(8,128)S(1)}, u32[]{:S(2)}, u32[]{:S(2)}) %collective-permute-start.10) | collective-permute-done | bytes 65568 | tf_op jit(solution)/shard_map/ppermute | solution.py:52
  38.7 1.2 %collective-permute-done.9 = f32[64,256]{1,0:T(8,128)S(1)} collective-permute-done((f32[64,256]{1,0:T(8,128)S(1)}, f32[64,256]{1,0:T(8,128)S(1)}, u32[]{:S(2)}, u32[]{:S(2)}) %collective-permute-start.9) | collective-permute-done | bytes 65568 | tf_op jit(solution)/shard_map/ppermute | solution.py:52
  39.9 0.6 collective-permute-done.8
  40.5 3.7 %collective-permute-start.13 = (f32[64,256]{1,0:T(8,128)S(1)}, f32[64,256]{1,0:T(8,128)S(1)}, u32[]{:S(2)}, u32[]{:S(2)}) collective-permute-start(f32[64,256]{1,0:T(8,128)S(1)} %add_add_fusion.1), channel_id=1, source_target_pairs={{0,3},{1,2},{2,1},{3,0},{4,7},{5,6},{6,5},{7,4},{8,11},{9,10},{10,... | collective-permute-start | bytes 196616 | tf_op jit(solution)/shard_map/ppermute | solution.py:52
  44.1 0.8 %collective-permute-start.11 = (f32[64,256]{1,0:T(8,128)S(1)}, f32[64,256]{1,0:T(8,128)S(1)}, u32[]{:S(2)}, u32[]{:S(2)}) collective-permute-start(f32[64,256]{1,0:T(8,128)S(1)} %add_add_fusion.1), channel_id=1, source_target_pairs={{0,1},{1,0},{2,3},{3,2},{4,5},{5,4},{6,7},{7,6},{8,9},{9,8},{10,11... | collective-permute-start | bytes 196616 | tf_op jit(solution)/shard_map/ppermute | solution.py:52
  44.9 2.3 %collective-permute-done.13 = f32[64,256]{1,0:T(8,128)S(1)} collective-permute-done((f32[64,256]{1,0:T(8,128)S(1)}, f32[64,256]{1,0:T(8,128)S(1)}, u32[]{:S(2)}, u32[]{:S(2)}) %collective-permute-start.13) | collective-permute-done | bytes 65568 | tf_op jit(solution)/shard_map/ppermute | solution.py:52
  47.2 2.2 %collective-permute-done.12 = f32[64,256]{1,0:T(8,128)S(1)} collective-permute-done((f32[64,256]{1,0:T(8,128)S(1)}, f32[64,256]{1,0:T(8,128)S(1)}, u32[]{:S(2)}, u32[]{:S(2)}) %collective-permute-start.12) | collective-permute-done | bytes 65568 | tf_op jit(solution)/shard_map/ppermute | solution.py:52
  49.7 1.2 %collective-permute-done.14.other_ref = f32[64,64]{1,0:T(8,128)S(1)} collective-permute-done((f32[64,64]{1,0:T(8,128)S(1)}, f32[64,64]{1,0:T(8,128)S(1)}, u32[]{:S(2)}, u32[]{:S(2)}) %collective-permute-start.14) | collective-permute-done | bytes 16416 | tf_op jit(solution)/shard_map/ppermute | solution.py:52
  50.9 2.8 %shard_map.35 = (f32[4,17,8,128]{3,2,1,0:T(8,128)S(1)}, f32[4,17,8,128]{3,2,1,0:T(8,128)S(1)}) custom-call(s32[1]{0:T(128)} %bitcast.me_ref, f32[64,64]{1,0:T(8,128)S(1)} %shard_map.34.mine_ref, f32[64,64]{1,0:T(8,128)S(1)} %collective-permute-done.14.other_ref, f32[64,256]{1,0:T(8,128)S(1)} %add_add_fusion.raw_ref, ...), custom_call_target="tpu_custom_call" | custom-call | tf_op jit(solution)/shard_map/pallas_call | solution.py:252
  53.9 1.4 %collective-permute-done.15.got_ref = f32[4,17,8,128]{3,2,1,0:T(8,128)S(1)} collective-permute-done((f32[4,17,8,128]{3,2,1,0:T(8,128)S(1)}, f32[4,17,8,128]{3,2,1,0:T(8,128)S(1)}, u32[]{:S(2)}, u32[]{:S(2)}) %collective-permute-start.15) | collective-permute-done | bytes 278560 | tf_op jit(solution)/shard_map/ppermute | solution.py:52
  55.4 1.1 %collective-permute-start.16 = (f32[17,8,128]{2,1,0:T(8,128)S(1)}, f32[17,8,128]{2,1,0:T(8,128)S(1)}, u32[]{:S(2)}, u32[]{:S(2)}) collective-permute-start(f32[17,8,128]{2,1,0:T(8,128)S(1)} %get-tuple-element.30), channel_id=1, source_target_pairs={{0,8},{4,12},{8,0},{12,4},{16,24},{20,28},{24,16},{28,20},{1,9},{5... | collective-permute-start | bytes 208904 | tf_op jit(solution)/shard_map/ppermute | solution.py:52
  56.5 1.2 %collective-permute-start.17 = (f32[17,8,128]{2,1,0:T(8,128)S(1)}, f32[17,8,128]{2,1,0:T(8,128)S(1)}, u32[]{:S(2)}, u32[]{:S(2)}) collective-permute-start(f32[17,8,128]{2,1,0:T(8,128)S(1)} %get-tuple-element.31), channel_id=1, source_target_pairs={{0,16},{4,20},{8,24},{12,28},{16,0},{20,4},{24,8},{28,12},{1,17},{... | collective-permute-start | bytes 208904 | tf_op jit(solution)/shard_map/ppermute | solution.py:52
  57.7 1.2 %collective-permute-start.18 = (f32[17,8,128]{2,1,0:T(8,128)S(1)}, f32[17,8,128]{2,1,0:T(8,128)S(1)}, u32[]{:S(2)}, u32[]{:S(2)}) collective-permute-start(f32[17,8,128]{2,1,0:T(8,128)S(1)} %get-tuple-element.32), channel_id=1, source_target_pairs={{0,24},{4,28},{8,16},{12,20},{16,8},{20,12},{24,0},{28,4},{1,25},{... | collective-permute-start | bytes 208904 | tf_op jit(solution)/shard_map/ppermute | solution.py:52
  58.9 0.8 %collective-permute-done.16.refs_1_ = f32[17,8,128]{2,1,0:T(8,128)S(1)} collective-permute-done((f32[17,8,128]{2,1,0:T(8,128)S(1)}, f32[17,8,128]{2,1,0:T(8,128)S(1)}, u32[]{:S(2)}, u32[]{:S(2)}) %collective-permute-start.16) | collective-permute-done | bytes 69664 | tf_op jit(solution)/shard_map/ppermute | solution.py:52
  59.7 1.1 %collective-permute-done.17.refs_2_ = f32[17,8,128]{2,1,0:T(8,128)S(1)} collective-permute-done((f32[17,8,128]{2,1,0:T(8,128)S(1)}, f32[17,8,128]{2,1,0:T(8,128)S(1)}, u32[]{:S(2)}, u32[]{:S(2)}) %collective-permute-start.17) | collective-permute-done | bytes 69664 | tf_op jit(solution)/shard_map/ppermute | solution.py:52
  60.8 2.1 %collective-permute-done.18.refs_3_ = f32[17,8,128]{2,1,0:T(8,128)S(1)} collective-permute-done((f32[17,8,128]{2,1,0:T(8,128)S(1)}, f32[17,8,128]{2,1,0:T(8,128)S(1)}, u32[]{:S(2)}, u32[]{:S(2)}) %collective-permute-start.18) | collective-permute-done | bytes 69664 | tf_op jit(solution)/shard_map/ppermute | solution.py:52
  62.9 0.9 %shard_map.37 = f32[66,8,128]{2,1,0:T(8,128)} custom-call(s32[1]{0:T(128)} %bitcast.me_ref, f32[17,8,128]{2,1,0:T(8,128)S(1)} %get-tuple-element.29.refs_0_, f32[17,8,128]{2,1,0:T(8,128)S(1)} %collective-permute-done.16.refs_1_, f32[17,8,128]{2,1,0:T(8,128)S(1)} %collective-permute-done.17.refs_2_, f32[17,8,128]{2,1,0:T(8,128)S(1)} %collective-permute-done.18.refs_3_), custom_call_target="tpu_custom_call" | custom-call | tf_op jit(solution)/shard_map/pallas_call | solution.py:298
  (22 shorter events, 2.5 us)
Async XLA Ops:
  0.0 1.6 %copy-start = (f32[33,2,64,128]{3,2,1,0:T(8,128)S(1)}, f32[33,2,64,128]{3,2,1,0:T(8,128)}, u32[]{:S(2)}) copy-start(f32[33,2,64,128]{3,2,1,0:T(8,128)} %param.2) | copy-start | bytes 6488068
  1.6 18.9 %copy-start.1 = (f32[512,64]{0,1:T(8,128)S(1)}, f32[512,64]{0,1:T(8,128)}, u32[]{:S(2)}) copy-start(f32[512,64]{0,1:T(8,128)} %param.3) | copy-start | bytes 393220
  1.9 10.5 %collective-permute-start = (f32[544,128]{1,0:T(8,128)S(1)}, f32[544,128]{1,0:T(8,128)S(1)}, u32[]{:S(2)}, u32[]{:S(2)}) collective-permute-start(f32[544,128]{1,0:T(8,128)S(1)} %get-tuple-element.20), channel_id=1, source_target_pairs={{0,8},{4,12},{8,0},{12,4},{16,24},{20,28},{24,16},{28,20},{1,9},{5... | collective-permute-start | bytes 835592 | tf_op jit(solution)/shard_map/ppermute | solution.py:52
  4.9 15.6 %collective-permute-start.1 = (f32[544,128]{1,0:T(8,128)S(1)}, f32[544,128]{1,0:T(8,128)S(1)}, u32[]{:S(2)}, u32[]{:S(2)}) collective-permute-start(f32[544,128]{1,0:T(8,128)S(1)} %get-tuple-element.21), channel_id=1, source_target_pairs={{0,16},{4,20},{8,24},{12,28},{16,0},{20,4},{24,8},{28,12},{1,17},{... | collective-permute-start | bytes 835592 | tf_op jit(solution)/shard_map/ppermute | solution.py:52
  6.4 14.0 %collective-permute-start.2 = (f32[544,128]{1,0:T(8,128)S(1)}, f32[544,128]{1,0:T(8,128)S(1)}, u32[]{:S(2)}, u32[]{:S(2)}) collective-permute-start(f32[544,128]{1,0:T(8,128)S(1)} %get-tuple-element.22), channel_id=1, source_target_pairs={{0,24},{4,28},{8,16},{12,20},{16,8},{20,12},{24,0},{28,4},{1,25},{... | collective-permute-start | bytes 835592 | tf_op jit(solution)/shard_map/ppermute | solution.py:52
  6.6 17.4 %collective-permute-start.4 = (f32[512,128]{1,0:T(8,128)S(1)}, f32[512,128]{1,0:T(8,128)S(1)}, u32[]{:S(2)}, u32[]{:S(2)}) collective-permute-start(f32[512,128]{1,0:T(8,128)S(1)} %get-tuple-element.24), channel_id=1, source_target_pairs={{0,8},{4,12},{8,0},{12,4},{16,24},{20,28},{24,16},{28,20},{1,9},{5... | collective-permute-start | bytes 786440 | tf_op jit(solution)/shard_map/ppermute | solution.py:52
  8.6 21.6 %collective-permute-start.5 = (f32[512,128]{1,0:T(8,128)S(1)}, f32[512,128]{1,0:T(8,128)S(1)}, u32[]{:S(2)}, u32[]{:S(2)}) collective-permute-start(f32[512,128]{1,0:T(8,128)S(1)} %get-tuple-element.25), channel_id=1, source_target_pairs={{0,16},{4,20},{8,24},{12,28},{16,0},{20,4},{24,8},{28,12},{1,17},{... | collective-permute-start | bytes 786440 | tf_op jit(solution)/shard_map/ppermute | solution.py:52
  12.4 17.8 %collective-permute-start.6 = (f32[512,128]{1,0:T(8,128)S(1)}, f32[512,128]{1,0:T(8,128)S(1)}, u32[]{:S(2)}, u32[]{:S(2)}) collective-permute-start(f32[512,128]{1,0:T(8,128)S(1)} %get-tuple-element.26), channel_id=1, source_target_pairs={{0,24},{4,28},{8,16},{12,20},{16,8},{20,12},{24,0},{28,4},{1,25},{... | collective-permute-start | bytes 786440 | tf_op jit(solution)/shard_map/ppermute | solution.py:52
  20.9 11.8 %collective-permute-start.3 = (f32[64,1152]{1,0:T(8,128)S(1)}, f32[64,1152]{1,0:T(8,128)S(1)}, u32[]{:S(2)}, u32[]{:S(2)}) collective-permute-start(f32[64,1152]{1,0:T(8,128)S(1)} %shard_map.29.mine_ref), channel_id=1, source_target_pairs={{0,4},{4,0},{8,12},{12,8},{16,20},{20,16},{24,28},{28,24},{1,5},{5... | collective-permute-start | bytes 884744 | tf_op jit(solution)/shard_map/ppermute | solution.py:52
  30.7 1.6 %collective-permute-start.7 = (f32[64,1024]{1,0:T(8,128)S(1)}, f32[64,1024]{1,0:T(8,128)S(1)}, u32[]{:S(2)}, u32[]{:S(2)}) collective-permute-start(f32[64,1024]{1,0:T(8,128)S(1)} %shard_map.31.mine_ref), channel_id=1, source_target_pairs={{0,4},{4,0},{8,12},{12,8},{16,20},{20,16},{24,28},{28,24},{1,5},{5... | collective-permute-start | bytes 786440 | tf_op jit(solution)/shard_map/ppermute | solution.py:52
  33.4 5.3 %collective-permute-start.10 = (f32[64,256]{1,0:T(8,128)S(1)}, f32[64,256]{1,0:T(8,128)S(1)}, u32[]{:S(2)}, u32[]{:S(2)}) collective-permute-start(f32[64,256]{1,0:T(8,128)S(1)} %shard_map.33), channel_id=1, source_target_pairs={{0,24},{4,28},{8,16},{12,20},{16,8},{20,12},{24,0},{28,4},{1,25},{... | collective-permute-start | bytes 196616 | tf_op jit(solution)/shard_map/ppermute | solution.py:52
  34.9 4.9 %collective-permute-start.9 = (f32[64,256]{1,0:T(8,128)S(1)}, f32[64,256]{1,0:T(8,128)S(1)}, u32[]{:S(2)}, u32[]{:S(2)}) collective-permute-start(f32[64,256]{1,0:T(8,128)S(1)} %shard_map.33), channel_id=1, source_target_pairs={{0,16},{4,20},{8,24},{12,28},{16,0},{20,4},{24,8},{28,12},{1,17},{... | collective-permute-start | bytes 196616 | tf_op jit(solution)/shard_map/ppermute | solution.py:52
  36.2 4.3 %collective-permute-start.8 = (f32[64,256]{1,0:T(8,128)S(1)}, f32[64,256]{1,0:T(8,128)S(1)}, u32[]{:S(2)}, u32[]{:S(2)}) collective-permute-start(f32[64,256]{1,0:T(8,128)S(1)} %shard_map.33), channel_id=1, source_target_pairs={{0,8},{4,12},{8,0},{12,4},{16,24},{20,28},{24,16},{28,20},{1,9},{5... | collective-permute-start | bytes 196616 | tf_op jit(solution)/shard_map/ppermute | solution.py:52
  40.5 6.8 %collective-permute-start.13 = (f32[64,256]{1,0:T(8,128)S(1)}, f32[64,256]{1,0:T(8,128)S(1)}, u32[]{:S(2)}, u32[]{:S(2)}) collective-permute-start(f32[64,256]{1,0:T(8,128)S(1)} %add_add_fusion.1), channel_id=1, source_target_pairs={{0,3},{1,2},{2,1},{3,0},{4,7},{5,6},{6,5},{7,4},{8,11},{9,10},{10,... | collective-permute-start | bytes 196616 | tf_op jit(solution)/shard_map/ppermute | solution.py:52
  44.1 5.3 %collective-permute-start.12 = (f32[64,256]{1,0:T(8,128)S(1)}, f32[64,256]{1,0:T(8,128)S(1)}, u32[]{:S(2)}, u32[]{:S(2)}) collective-permute-start(f32[64,256]{1,0:T(8,128)S(1)} %add_add_fusion.1), channel_id=1, source_target_pairs={{0,2},{1,3},{2,0},{3,1},{4,6},{5,7},{6,4},{7,5},{8,10},{9,11},{10,... | collective-permute-start | bytes 196616 | tf_op jit(solution)/shard_map/ppermute | solution.py:52
  44.1 5.3 %collective-permute-start.11 = (f32[64,256]{1,0:T(8,128)S(1)}, f32[64,256]{1,0:T(8,128)S(1)}, u32[]{:S(2)}, u32[]{:S(2)}) collective-permute-start(f32[64,256]{1,0:T(8,128)S(1)} %add_add_fusion.1), channel_id=1, source_target_pairs={{0,1},{1,0},{2,3},{3,2},{4,5},{5,4},{6,7},{7,6},{8,9},{9,8},{10,11... | collective-permute-start | bytes 196616 | tf_op jit(solution)/shard_map/ppermute | solution.py:52
  49.6 1.3 %collective-permute-start.14 = (f32[64,64]{1,0:T(8,128)S(1)}, f32[64,64]{1,0:T(8,128)S(1)}, u32[]{:S(2)}, u32[]{:S(2)}) collective-permute-start(f32[64,64]{1,0:T(8,128)S(1)} %shard_map.34.mine_ref), channel_id=1, source_target_pairs={{0,4},{4,0},{8,12},{12,8},{16,20},{20,16},{24,28},{28,24},{1,5},{5... | collective-permute-start | bytes 49160 | tf_op jit(solution)/shard_map/ppermute | solution.py:52
  53.7 1.6 %collective-permute-start.15 = (f32[4,17,8,128]{3,2,1,0:T(8,128)S(1)}, f32[4,17,8,128]{3,2,1,0:T(8,128)S(1)}, u32[]{:S(2)}, u32[]{:S(2)}) collective-permute-start(f32[4,17,8,128]{3,2,1,0:T(8,128)S(1)} %get-tuple-element.28), channel_id=1, source_target_pairs={{0,4},{4,0},{8,12},{12,8},{16,20},{20,16},{24,28},{28,24},{1,5},{5... | collective-permute-start | bytes 835592 | tf_op jit(solution)/shard_map/ppermute | solution.py:52
  55.4 4.4 %collective-permute-start.16 = (f32[17,8,128]{2,1,0:T(8,128)S(1)}, f32[17,8,128]{2,1,0:T(8,128)S(1)}, u32[]{:S(2)}, u32[]{:S(2)}) collective-permute-start(f32[17,8,128]{2,1,0:T(8,128)S(1)} %get-tuple-element.30), channel_id=1, source_target_pairs={{0,8},{4,12},{8,0},{12,4},{16,24},{20,28},{24,16},{28,20},{1,9},{5... | collective-permute-start | bytes 208904 | tf_op jit(solution)/shard_map/ppermute | solution.py:52
  56.5 4.3 %collective-permute-start.17 = (f32[17,8,128]{2,1,0:T(8,128)S(1)}, f32[17,8,128]{2,1,0:T(8,128)S(1)}, u32[]{:S(2)}, u32[]{:S(2)}) collective-permute-start(f32[17,8,128]{2,1,0:T(8,128)S(1)} %get-tuple-element.31), channel_id=1, source_target_pairs={{0,16},{4,20},{8,24},{12,28},{16,0},{20,4},{24,8},{28,12},{1,17},{... | collective-permute-start | bytes 208904 | tf_op jit(solution)/shard_map/ppermute | solution.py:52
  57.7 5.2 %collective-permute-start.18 = (f32[17,8,128]{2,1,0:T(8,128)S(1)}, f32[17,8,128]{2,1,0:T(8,128)S(1)}, u32[]{:S(2)}, u32[]{:S(2)}) collective-permute-start(f32[17,8,128]{2,1,0:T(8,128)S(1)} %get-tuple-element.32), channel_id=1, source_target_pairs={{0,24},{4,28},{8,16},{12,20},{16,8},{20,12},{24,0},{28,4},{1,25},{... | collective-permute-start | bytes 208904 | tf_op jit(solution)/shard_map/ppermute | solution.py:52

commit v5 on v4

--- a/solution.py
+++ b/solution.py
@@ -52,7 +52,8 @@
     return lax.ppermute(value, axis, [(i, i ^ mask) for i in range(size)])
 
 
-def pack_kernel(chips, first, last, own, left, width, me_ref, rows_ref, *refs):
+def pack_kernel(chips, first, last, own, left, width, me_ref, rows_ref, after, *refs):
+    del after
     blocks, refs = refs[:chips], refs[chips:]
     ny = rows_ref.shape[1]
     chip = lax.div(me_ref[0], 2)
@@ -77,18 +78,18 @@
         copy.wait()
 
 
-def pack(rows, me, chips, first, last, own, left, width):
+def pack(rows, me, after, chips, first, last, own, left, width):
     ny = rows.shape[1]
     high = (last - first) * width + (ny // chips if left else 0)
     scratch = [pltpu.VMEM((ny, ny), F32), pltpu.VMEM((left * width, ny), F32)] if left else []
     return pl.pallas_call(
         functools.partial(pack_kernel, chips, first, last, own, left, width),
-        in_specs=[SMEM, HBM],
+        in_specs=[SMEM, HBM, pl.BlockSpec(memory_space=pl.ANY)],
         out_specs=[VMEM] * chips,
         out_shape=[jax.ShapeDtypeStruct((high, ny), F32)] * chips,
         scratch_shapes=scratch + [pltpu.SemaphoreType.DMA((chips + 1,))],
         compiler_params=PARAMS,
-    )(me, rows)
+    )(me, pltpu.with_memory_space_constraint(rows, pltpu.HBM), after)
 
 
 def slabs_of(refs, count, width):
@@ -110,56 +111,66 @@
 
 
 def project_kernel(count, left, width, me_ref, start_ref, *refs):
-    refs, out_ref = refs[:-1], refs[-1]
-    chips, me, ny = len(refs), me_ref[0], refs[0].shape[1]
+    chips, me = (start_ref.shape[1] // width) // 2, me_ref[0]
+    refs, (out_ref, high_ref, low_ref, *rest_refs) = refs[:chips], refs[chips:]
+    ny = refs[0].shape[1]
     parts = [start_ref[:, i * width : (i + 1) * width] for i in range(2 * chips)]
     odd = (me & 1) != 0
     start = jnp.where(odd, jnp.concatenate(parts[1::2], axis=1), jnp.concatenate(parts[::2], axis=1))
     start = stack(reorder(start, lax.div(me, 2), chips, 1))
     for at, to, slab in slabs_of(refs, count, width):
         out_ref[:, at:to] = dot_split(start, slab, NN)
-    if left:
-        out_ref[:, count * ny :] = widen(dot_split(start, rest_of(refs, count, left, width), NT), ny)
-
-
-def project(blocks, start_t, me, count, left, width):
-    ny = blocks[0].shape[1]
-    return pl.pallas_call(
-        functools.partial(project_kernel, count, left, width),
-        in_specs=[SMEM] + [VMEM] * (1 + len(blocks)),
-        out_specs=VMEM,
-        out_shape=jax.ShapeDtypeStruct((start_t.shape[0], (count + (left > 0)) * ny), F32),
-        compiler_params=PARAMS,
-    )(me, start_t, *blocks)
-
-
-def raw_kernel(count, left, width, more, last, me_ref, mine_ref, other_ref, *refs):
-    refs, out_ref = refs[:-1], refs[-1]
-    if more:
-        refs, total = refs[:-1], refs[-1][...]
-    else:
-        total = jnp.zeros(out_ref.shape, F32)
-    ny = refs[0].shape[1]
-    for at, to, slab in slabs_of(refs, count, width):
-        total += dot_split(stack(mine_ref[:, at:to] + other_ref[:, at:to]), slab, NT)
+        high_ref[at // (2 * ny), :, : to - at], low_ref[at // (2 * ny), :, : to - at] = slab
     if left:
         rest = rest_of(refs, count, left, width)
+        rest_refs[0][...], rest_refs[1][...] = rest
+        out_ref[:, count * ny :] = widen(dot_split(start, rest, NT), ny)
+
+
+def project(blocks, start_t, me, count, left, width):
+    chips, ny = len(blocks), blocks[0].shape[1]
+    pairs = jax.ShapeDtypeStruct(((count + 1) // 2, chips * width, 2 * ny), BF16)
+    rest = [jax.ShapeDtypeStruct((left * (ny // chips), chips * width), BF16)] * 2 if left else []
+    columns = jax.ShapeDtypeStruct((start_t.shape[0], (count + (left > 0)) * ny), F32)
+    return pl.pallas_call(
+        functools.partial(project_kernel, count, left, width),
+        in_specs=[SMEM] + [VMEM] * (1 + chips),
+        out_specs=[VMEM] * (3 + len(rest)),
+        out_shape=[columns, pairs, pairs] + rest,
+        compiler_params=PARAMS,
+    )(me, start_t, *blocks)
+
+
+def split_slabs(high_ref, low_ref, count, ny):
+    for s in range(0, count, 2):
+        to = min(s + 2, count)
+        lanes = slice(0, (to - s) * ny)
+        yield s * ny, to * ny, (high_ref[s // 2, :, lanes], low_ref[s // 2, :, lanes])
+
+
+def raw_kernel(count, ny, chips, last, me_ref, mine_ref, other_ref, high_ref, low_ref, *refs):
+    refs, out_ref = refs[:-1], refs[-1]
+    total = refs[0][...] if last else jnp.zeros(out_ref.shape, F32)
+    for at, to, slab in split_slabs(high_ref, low_ref, count, ny):
+        total += dot_split(stack(mine_ref[:, at:to] + other_ref[:, at:to]), slab, NT)
+    if last:
+        rest = (refs[1][...], refs[2][...])
         lanes = slice(count * ny, count * ny + rest[0].shape[0])
         total += dot_split(stack(mine_ref[:, lanes] + other_ref[:, lanes]), rest, NN)
-    if last:
-        total = reorder(total, lax.div(me_ref[0], 2), len(refs), 1)
+        total = reorder(total, lax.div(me_ref[0], 2), chips, 1)
     out_ref[...] = total
 
 
-def raw_part(blocks, mine, other, before, me, count, left, width, last):
-    more = [] if before is None else [before]
-    return pl.pallas_call(
-        functools.partial(raw_kernel, count, left, width, bool(more), last),
-        in_specs=[SMEM] + [VMEM] * (2 + len(blocks) + len(more)),
+def raw_part(mine, other, pairs, before, me, count, ny, chips):
+    last = before is not None
+    args = [me, mine, other, *pairs[:2]] + ([before, *pairs[2:]] if last else [])
+    return pl.pallas_call(
+        functools.partial(raw_kernel, count, ny, chips, last),
+        in_specs=[SMEM] + [VMEM] * (len(args) - 1),
         out_specs=VMEM,
-        out_shape=jax.ShapeDtypeStruct((mine.shape[0], len(blocks) * width), F32),
-        compiler_params=PARAMS,
-    )(me, mine, other, *blocks, *more)
+        out_shape=jax.ShapeDtypeStruct((mine.shape[0], pairs[0].shape[1]), F32),
+        compiler_params=PARAMS,
+    )(*args)
 
 
 def sum_over(value, axis, low, size):
@@ -209,21 +220,21 @@
             pivot = spread(columns[0][k], k)
             pivots = jnp.where(sub == k, pivot, pivots)
             scale = 1.0 / pivot
-            scaled = spread(rows[b], k) * scale
-            ahead = [spread(columns[0][m], k) * scale for m in range(k + 1, 8)]
+            across = spread(rows[b], k)
+            ahead = [spread(columns[0][m], k) for m in range(k + 1, 8)]
             for i, column in enumerate(columns):
                 factor = jnp.where(sub > k, column[k], 0.0) if i == 0 else column[k]
                 for m in range(k + 1, 8):
-                    column[m] = column[m] - factor * ahead[m - k - 1]
-                rows[b + i] = rows[b + i] - factor * scaled
+                    column[m] = column[m] - (factor * ahead[m - k - 1]) * scale
+                rows[b + i] = rows[b + i] - (factor * across) * scale
         inverse.append(rows[b][:, rank:] * lax.rsqrt(pivots[:, rank:]))
     return jnp.concatenate(inverse, axis=0)
 
 
-def core_kernel(counts, left, width, me_ref, mine_ref, other_ref, raw_ref, *refs):
+def core_kernel(counts, me_ref, mine_ref, other_ref, raw_ref, *refs):
     refs, (keep_ref, send_ref) = refs[:-2], refs[-2:]
     chips = keep_ref.shape[0]
-    rank, (each, ny) = raw_ref.shape[0], keep_ref.shape[-2:]
+    each, ny = keep_ref.shape[-2:]
     me = me_ref[0]
     inverse = inverse_factor(mine_ref[...] + other_ref[...])
     inverse = reorder(inverse, me, 2 * chips, 0)
@@ -237,25 +248,23 @@
 
     done = 0
     for c, count in enumerate(counts):
-        blocks = refs[c * chips : (c + 1) * chips]
-        for at, to, slab in slabs_of(blocks, count, width):
+        for at, to, slab in split_slabs(refs[2 * c], refs[2 * c + 1], count, ny):
             value = dot_split(basis, slab, NN)
             for lane in range(0, to - at, ny):
                 put(done + (at + lane) // ny, value[:, lane : lane + ny])
         done += count
-    put(done, widen(dot_split(basis, rest_of(blocks, count, left, width), NT), ny))
-
-
-def core(blocks, mine, other, raw, me, counts, left, width, each):
-    chips, ny = len(blocks) // len(counts), blocks[0].shape[1]
+    put(done, widen(dot_split(basis, (refs[-2][...], refs[-1][...]), NT), ny))
+
+
+def core(pairs, mine, other, raw, me, counts, chips, each, ny):
     shape = jax.ShapeDtypeStruct((chips, sum(counts) + 1, each, ny), F32)
     return pl.pallas_call(
-        functools.partial(core_kernel, counts, left, width),
-        in_specs=[SMEM] + [VMEM] * (3 + len(blocks)),
+        functools.partial(core_kernel, counts),
+        in_specs=[SMEM] + [VMEM] * (3 + len(pairs)),
         out_specs=[VMEM] * 2,
         out_shape=[shape] * 2,
         compiler_params=PARAMS,
-    )(me, mine, other, raw, *blocks)
+    )(me, mine, other, raw, *pairs)
 
 
 def add_kernel(keep_ref, got_ref, *outs):
@@ -310,23 +319,24 @@
     chips, each = n // 2, start_block.shape[1] // n
     total = species * planes
     own, left = divmod(total, chips)
-    counts = [own - own // 2, own // 2]
+    counts = [own * 5 // 8, own - own * 5 // 8]
     me = lax.axis_index("fib").astype(jnp.int32).reshape(1)
     rows = field_data.reshape(total * width, ny)
     start_t = start_block.T
-    blocks, raw, first = [], None, 0
+    pairs, raw, first, after = [], None, 0, me
     for c, count in enumerate(counts):
         rest = left if c == len(counts) - 1 else 0
-        sent = pack(rows, me, chips, first, first + count, own, rest, width)
+        sent = pack(rows, me, after, chips, first, first + count, own, rest, width)
         part = [sent[0]] + [exchange(sent[k], "fib", 2 * k, n) for k in range(1, chips)]
-        mine = project(part, start_t, me, count, rest, width)
+        mine, *split = project(part, start_t, me, count, rest, width)
         other = exchange(mine, "fib", 1, n)
-        raw = raw_part(part, mine, other, raw, me, count, rest, width, c == len(counts) - 1)
-        blocks += part
+        raw = raw_part(mine, other, split, raw, me, count, ny, chips)
+        pairs += split
         first += count
+        after = sent[0]
     raw = sum_over(sum_over(raw, "fib", 2, n), "blk", 1, layers)
     gram = gram_part(raw)
-    keep, send = core(blocks, gram, exchange(gram, "fib", 1, n), raw, me, counts, left, width, each)
+    keep, send = core(pairs, gram, exchange(gram, "fib", 1, n), raw, me, counts, chips, each, ny)
     parts = add_parts(keep, exchange(send, "fib", 1, n))
     parts = [parts[0]] + [exchange(parts[k], "fib", 2 * k, n) for k in range(1, chips)]
     return place(parts, me, own, left).reshape(species, planes, each, ny)

time: 63.9 us -> 62.5 us (0.978)
  Pallas kernels: 6.22 us -> 8.19 us
  waiting for transfers between devices: 32.7 us -> 30.9 us
  local copies, waits for them, and re-layouts: 1.61 us -> 0.01 us
    pallas_call x2, Pallas kernels: 0.42 us -> 2.64 us  [pack(): pl.pallas_call(functools.partial(pack_kernel, chips, first, last, own, le...]
    ppermute x19, waiting for transfers between devices: 32.7 us -> 30.9 us  [exchange(): return lax.ppermute(value, axis, [(i, i ^ mask) for i in range(size)])]
    unnamed x4 -> x2, local copies, waits for them, and re-layouts: 1.61 us -> 0.01 us
  transfers between devices with their start and end apart: 19 -> 19, of which waited for: 15 -> 15; matrix products, arithmetic and copies ran while one was open for 0% -> 0% of each run, Pallas kernels for 2% -> 4%
where the time goes in v5:
time: 62.5 us; the launch traced here: 62.3 us
  waiting for transfers between devices  30.9 us (49%)
  starting transfers between devices  23.1 us (37%)
  Pallas kernels  8.19 us (13%)
    ppermute x19, waiting for transfers between devices, exchange(): return lax.ppermute(value, axis, [(i, i ^ mask) for i in range(size)])  30.9 us
    ppermute x19, starting transfers between devices, exchange(): return lax.ppermute(value, axis, [(i, i ^ mask) for i in range(size)])  23.1 us
    pallas_call x2, Pallas kernels, pack(): pl.pallas_call(functools.partial(pack_kernel, chips, first, last, own, le...  2.64 us
    pallas_call x1, Pallas kernels, core(): pl.pallas_call(functools.partial(core_kernel, counts), in_specs=[SMEM] +...  2.52 us
  transfers between devices with their start and end apart: 19, of which 15 were waited for; matrix products, arithmetic and copies ran while one was open for 0% of the time, Pallas kernels for 4%

profile of v5, /device:TPU:0, one launch (start us, length us, event | category | flops | bytes accessed | tf_op | source)
XLA Modules:
  0.0 62.3 jit_solution(7380460988903735000)
XLA Ops:
  0.0 1.3 %shard_map.28 = (f32[640,128]{1,0:T(8,128)S(1)}, f32[640,128]{1,0:T(8,128)S(1)}, f32[640,128]{1,0:T(8,128)S(1)}, f32[640,128]{1,0:T(8,128)S(1)}) custom-call(s32[1]{0:T(128)} %bitcast.me_ref.after, f32[4224,128]{1,0:T(8,128)} %bitcast.6, s32[1]{0:T(128)} %bitcast.me_ref.after), custom_call_target="tpu_custom_call" | custom-call | tf_op jit(solution)/shard_map/pallas_call | solution.py:85
  1.4 3.0 %collective-permute-start.4 = (f32[640,128]{1,0:T(8,128)S(1)}, f32[640,128]{1,0:T(8,128)S(1)}, u32[]{:S(2)}, u32[]{:S(2)}) collective-permute-start(f32[640,128]{1,0:T(8,128)S(1)} %get-tuple-element.35), channel_id=1, source_target_pairs={{0,8},{4,12},{8,0},{12,4},{16,24},{20,28},{24,16},{28,20},{1,9},{5... | collective-permute-start | bytes 983048 | tf_op jit(solution)/shard_map/ppermute | solution.py:52
  4.4 1.5 %collective-permute-start.5 = (f32[640,128]{1,0:T(8,128)S(1)}, f32[640,128]{1,0:T(8,128)S(1)}, u32[]{:S(2)}, u32[]{:S(2)}) collective-permute-start(f32[640,128]{1,0:T(8,128)S(1)} %get-tuple-element.36), channel_id=1, source_target_pairs={{0,16},{4,20},{8,24},{12,28},{16,0},{20,4},{24,8},{28,12},{1,17},{... | collective-permute-start | bytes 983048 | tf_op jit(solution)/shard_map/ppermute | solution.py:52
  5.9 1.3 %shard_map.29 = (f32[416,128]{1,0:T(8,128)S(1)}, f32[416,128]{1,0:T(8,128)S(1)}, f32[416,128]{1,0:T(8,128)S(1)}, f32[416,128]{1,0:T(8,128)S(1)}) custom-call(s32[1]{0:T(128)} %bitcast.me_ref.after, f32[4224,128]{1,0:T(8,128)} %bitcast.7, f32[640,128]{1,0:T(8,128)S(1)} %get-tuple-element.27.after.refs_0_), custom_call_target="tpu_custom_call" | custom-call | tf_op jit(solution)/shard_map/pallas_call | solution.py:85
  7.2 2.0 %collective-permute-start = (f32[416,128]{1,0:T(8,128)S(1)}, f32[416,128]{1,0:T(8,128)S(1)}, u32[]{:S(2)}, u32[]{:S(2)}) collective-permute-start(f32[416,128]{1,0:T(8,128)S(1)} %get-tuple-element.29), channel_id=1, source_target_pairs={{0,8},{4,12},{8,0},{12,4},{16,24},{20,28},{24,16},{28,20},{1,9},{5... | collective-permute-start | bytes 638984 | tf_op jit(solution)/shard_map/ppermute | solution.py:52
  9.2 1.5 %collective-permute-start.1 = (f32[416,128]{1,0:T(8,128)S(1)}, f32[416,128]{1,0:T(8,128)S(1)}, u32[]{:S(2)}, u32[]{:S(2)}) collective-permute-start(f32[416,128]{1,0:T(8,128)S(1)} %get-tuple-element.30), channel_id=1, source_target_pairs={{0,16},{4,20},{8,24},{12,28},{16,0},{20,4},{24,8},{28,12},{1,17},{... | collective-permute-start | bytes 638984 | tf_op jit(solution)/shard_map/ppermute | solution.py:52
  10.7 2.2 %collective-permute-done.4.refs_1_ = f32[640,128]{1,0:T(8,128)S(1)} collective-permute-done((f32[640,128]{1,0:T(8,128)S(1)}, f32[640,128]{1,0:T(8,128)S(1)}, u32[]{:S(2)}, u32[]{:S(2)}) %collective-permute-start.4) | collective-permute-done | bytes 327712 | tf_op jit(solution)/shard_map/ppermute | solution.py:52
  12.9 3.0 %collective-permute-start.2 = (f32[416,128]{1,0:T(8,128)S(1)}, f32[416,128]{1,0:T(8,128)S(1)}, u32[]{:S(2)}, u32[]{:S(2)}) collective-permute-start(f32[416,128]{1,0:T(8,128)S(1)} %get-tuple-element.31), channel_id=1, source_target_pairs={{0,24},{4,28},{8,16},{12,20},{16,8},{20,12},{24,0},{28,4},{1,25},{... | collective-permute-start | bytes 638984 | tf_op jit(solution)/shard_map/ppermute | solution.py:52
  15.9 6.1 %collective-permute-done.5.refs_2_ = f32[640,128]{1,0:T(8,128)S(1)} collective-permute-done((f32[640,128]{1,0:T(8,128)S(1)}, f32[640,128]{1,0:T(8,128)S(1)}, u32[]{:S(2)}, u32[]{:S(2)}) %collective-permute-start.5) | collective-permute-done | bytes 327712 | tf_op jit(solution)/shard_map/ppermute | solution.py:52
  22.6 1.9 %collective-permute-done.refs_1_ = f32[416,128]{1,0:T(8,128)S(1)} collective-permute-done((f32[416,128]{1,0:T(8,128)S(1)}, f32[416,128]{1,0:T(8,128)S(1)}, u32[]{:S(2)}, u32[]{:S(2)}) %collective-permute-start) | collective-permute-done | bytes 213024 | tf_op jit(solution)/shard_map/ppermute | solution.py:52
  24.5 5.1 %collective-permute-done.1.refs_2_ = f32[416,128]{1,0:T(8,128)S(1)} collective-permute-done((f32[416,128]{1,0:T(8,128)S(1)}, f32[416,128]{1,0:T(8,128)S(1)}, u32[]{:S(2)}, u32[]{:S(2)}) %collective-permute-start.1) | collective-permute-done | bytes 213024 | tf_op jit(solution)/shard_map/ppermute | solution.py:52
  30.7 0.9 %collective-permute-done.3.other_ref = f32[64,896]{1,0:T(8,128)S(1)} collective-permute-done((f32[64,896]{1,0:T(8,128)S(1)}, f32[64,896]{1,0:T(8,128)S(1)}, u32[]{:S(2)}, u32[]{:S(2)}) %collective-permute-start.3) | collective-permute-done | bytes 229408 | tf_op jit(solution)/shard_map/ppermute | solution.py:52
  32.2 1.6 %collective-permute-start.10 = (f32[64,256]{1,0:T(8,128)S(1)}, f32[64,256]{1,0:T(8,128)S(1)}, u32[]{:S(2)}, u32[]{:S(2)}) collective-permute-start(f32[64,256]{1,0:T(8,128)S(1)} %shard_map.33), channel_id=1, source_target_pairs={{0,24},{4,28},{8,16},{12,20},{16,8},{20,12},{24,0},{28,4},{1,25},{... | collective-permute-start | bytes 196616 | tf_op jit(solution)/shard_map/ppermute | solution.py:52
  33.7 1.2 %collective-permute-start.9 = (f32[64,256]{1,0:T(8,128)S(1)}, f32[64,256]{1,0:T(8,128)S(1)}, u32[]{:S(2)}, u32[]{:S(2)}) collective-permute-start(f32[64,256]{1,0:T(8,128)S(1)} %shard_map.33), channel_id=1, source_target_pairs={{0,16},{4,20},{8,24},{12,28},{16,0},{20,4},{24,8},{28,12},{1,17},{... | collective-permute-start | bytes 196616 | tf_op jit(solution)/shard_map/ppermute | solution.py:52
  35.0 0.7 %collective-permute-start.8 = (f32[64,256]{1,0:T(8,128)S(1)}, f32[64,256]{1,0:T(8,128)S(1)}, u32[]{:S(2)}, u32[]{:S(2)}) collective-permute-start(f32[64,256]{1,0:T(8,128)S(1)} %shard_map.33), channel_id=1, source_target_pairs={{0,8},{4,12},{8,0},{12,4},{16,24},{20,28},{24,16},{28,20},{1,9},{5... | collective-permute-start | bytes 196616 | tf_op jit(solution)/shard_map/ppermute | solution.py:52
  35.7 1.8 %collective-permute-done.10 = f32[64,256]{1,0:T(8,128)S(1)} collective-permute-done((f32[64,256]{1,0:T(8,128)S(1)}, f32[64,256]{1,0:T(8,128)S(1)}, u32[]{:S(2)}, u32[]{:S(2)}) %collective-permute-start.10) | collective-permute-done | bytes 65568 | tf_op jit(solution)/shard_map/ppermute | solution.py:52
  37.5 1.2 %collective-permute-done.9 = f32[64,256]{1,0:T(8,128)S(1)} collective-permute-done((f32[64,256]{1,0:T(8,128)S(1)}, f32[64,256]{1,0:T(8,128)S(1)}, u32[]{:S(2)}, u32[]{:S(2)}) %collective-permute-start.9) | collective-permute-done | bytes 65568 | tf_op jit(solution)/shard_map/ppermute | solution.py:52
  38.7 0.6 collective-permute-done.8
  39.2 3.7 %collective-permute-start.13 = (f32[64,256]{1,0:T(8,128)S(1)}, f32[64,256]{1,0:T(8,128)S(1)}, u32[]{:S(2)}, u32[]{:S(2)}) collective-permute-start(f32[64,256]{1,0:T(8,128)S(1)} %add_add_fusion.1), channel_id=1, source_target_pairs={{0,3},{1,2},{2,1},{3,0},{4,7},{5,6},{6,5},{7,4},{8,11},{9,10},{10,... | collective-permute-start | bytes 196616 | tf_op jit(solution)/shard_map/ppermute | solution.py:52
  42.9 0.8 %collective-permute-start.11 = (f32[64,256]{1,0:T(8,128)S(1)}, f32[64,256]{1,0:T(8,128)S(1)}, u32[]{:S(2)}, u32[]{:S(2)}) collective-permute-start(f32[64,256]{1,0:T(8,128)S(1)} %add_add_fusion.1), channel_id=1, source_target_pairs={{0,1},{1,0},{2,3},{3,2},{4,5},{5,4},{6,7},{7,6},{8,9},{9,8},{10,11... | collective-permute-start | bytes 196616 | tf_op jit(solution)/shard_map/ppermute | solution.py:52
  43.7 2.3 %collective-permute-done.13 = f32[64,256]{1,0:T(8,128)S(1)} collective-permute-done((f32[64,256]{1,0:T(8,128)S(1)}, f32[64,256]{1,0:T(8,128)S(1)}, u32[]{:S(2)}, u32[]{:S(2)}) %collective-permute-start.13) | collective-permute-done | bytes 65568 | tf_op jit(solution)/shard_map/ppermute | solution.py:52
  46.0 2.2 %collective-permute-done.12 = f32[64,256]{1,0:T(8,128)S(1)} collective-permute-done((f32[64,256]{1,0:T(8,128)S(1)}, f32[64,256]{1,0:T(8,128)S(1)}, u32[]{:S(2)}, u32[]{:S(2)}) %collective-permute-start.12) | collective-permute-done | bytes 65568 | tf_op jit(solution)/shard_map/ppermute | solution.py:52
  48.5 1.2 %collective-permute-done.14.other_ref = f32[64,64]{1,0:T(8,128)S(1)} collective-permute-done((f32[64,64]{1,0:T(8,128)S(1)}, f32[64,64]{1,0:T(8,128)S(1)}, u32[]{:S(2)}, u32[]{:S(2)}) %collective-permute-start.14) | collective-permute-done | bytes 16416 | tf_op jit(solution)/shard_map/ppermute | solution.py:52
  49.7 2.5 %shard_map.35 = (f32[4,17,8,128]{3,2,1,0:T(8,128)S(1)}, f32[4,17,8,128]{3,2,1,0:T(8,128)S(1)}) custom-call(s32[1]{0:T(128)} %bitcast.me_ref.after, f32[64,64]{1,0:T(8,128)S(1)} %shard_map.34.mine_ref, f32[64,64]{1,0:T(8,128)S(1)} %collective-permute-done.14.other_ref, f32[64,256]{1,0:T(8,128)S(1)} %add_add_fusion.raw_ref, ...), custom_call_target="tpu_custom_call" | custom-call | tf_op jit(solution)/shard_map/pallas_call | solution.py:261
  52.5 1.4 %collective-permute-done.15.got_ref = f32[4,17,8,128]{3,2,1,0:T(8,128)S(1)} collective-permute-done((f32[4,17,8,128]{3,2,1,0:T(8,128)S(1)}, f32[4,17,8,128]{3,2,1,0:T(8,128)S(1)}, u32[]{:S(2)}, u32[]{:S(2)}) %collective-permute-start.15) | collective-permute-done | bytes 278560 | tf_op jit(solution)/shard_map/ppermute | solution.py:52
  53.9 1.1 %collective-permute-start.16 = (f32[17,8,128]{2,1,0:T(8,128)S(1)}, f32[17,8,128]{2,1,0:T(8,128)S(1)}, u32[]{:S(2)}, u32[]{:S(2)}) collective-permute-start(f32[17,8,128]{2,1,0:T(8,128)S(1)} %get-tuple-element.46), channel_id=1, source_target_pairs={{0,8},{4,12},{8,0},{12,4},{16,24},{20,28},{24,16},{28,20},{1,9},{5... | collective-permute-start | bytes 208904 | tf_op jit(solution)/shard_map/ppermute | solution.py:52
  55.0 1.2 %collective-permute-start.17 = (f32[17,8,128]{2,1,0:T(8,128)S(1)}, f32[17,8,128]{2,1,0:T(8,128)S(1)}, u32[]{:S(2)}, u32[]{:S(2)}) collective-permute-start(f32[17,8,128]{2,1,0:T(8,128)S(1)} %get-tuple-element.47), channel_id=1, source_target_pairs={{0,16},{4,20},{8,24},{12,28},{16,0},{20,4},{24,8},{28,12},{1,17},{... | collective-permute-start | bytes 208904 | tf_op jit(solution)/shard_map/ppermute | solution.py:52
  56.2 1.2 %collective-permute-start.18 = (f32[17,8,128]{2,1,0:T(8,128)S(1)}, f32[17,8,128]{2,1,0:T(8,128)S(1)}, u32[]{:S(2)}, u32[]{:S(2)}) collective-permute-start(f32[17,8,128]{2,1,0:T(8,128)S(1)} %get-tuple-element.48), channel_id=1, source_target_pairs={{0,24},{4,28},{8,16},{12,20},{16,8},{20,12},{24,0},{28,4},{1,25},{... | collective-permute-start | bytes 208904 | tf_op jit(solution)/shard_map/ppermute | solution.py:52
  57.4 0.8 %collective-permute-done.16.refs_1_ = f32[17,8,128]{2,1,0:T(8,128)S(1)} collective-permute-done((f32[17,8,128]{2,1,0:T(8,128)S(1)}, f32[17,8,128]{2,1,0:T(8,128)S(1)}, u32[]{:S(2)}, u32[]{:S(2)}) %collective-permute-start.16) | collective-permute-done | bytes 69664 | tf_op jit(solution)/shard_map/ppermute | solution.py:52
  58.3 1.1 %collective-permute-done.17.refs_2_ = f32[17,8,128]{2,1,0:T(8,128)S(1)} collective-permute-done((f32[17,8,128]{2,1,0:T(8,128)S(1)}, f32[17,8,128]{2,1,0:T(8,128)S(1)}, u32[]{:S(2)}, u32[]{:S(2)}) %collective-permute-start.17) | collective-permute-done | bytes 69664 | tf_op jit(solution)/shard_map/ppermute | solution.py:52
  59.3 2.1 %collective-permute-done.18.refs_3_ = f32[17,8,128]{2,1,0:T(8,128)S(1)} collective-permute-done((f32[17,8,128]{2,1,0:T(8,128)S(1)}, f32[17,8,128]{2,1,0:T(8,128)S(1)}, u32[]{:S(2)}, u32[]{:S(2)}) %collective-permute-start.18) | collective-permute-done | bytes 69664 | tf_op jit(solution)/shard_map/ppermute | solution.py:52
  61.5 0.9 %shard_map.37 = f32[66,8,128]{2,1,0:T(8,128)} custom-call(s32[1]{0:T(128)} %bitcast.me_ref.after, f32[17,8,128]{2,1,0:T(8,128)S(1)} %get-tuple-element.45.refs_0_, f32[17,8,128]{2,1,0:T(8,128)S(1)} %collective-permute-done.16.refs_1_, f32[17,8,128]{2,1,0:T(8,128)S(1)} %collective-permute-done.17.refs_2_, f32[17,8,128]{2,1,0:T(8,128)S(1)} %collective-permute-done.18.refs_3_), custom_call_target="tpu_custom_call" | custom-call | tf_op jit(solution)/shard_map/pallas_call | solution.py:307
  (20 shorter events, 2.7 us)
Async XLA Ops:
  0.0 22.0 %copy-start = (f32[512,64]{0,1:T(8,128)S(1)}, f32[512,64]{0,1:T(8,128)}, u32[]{:S(2)}) copy-start(f32[512,64]{0,1:T(8,128)} %param.3) | copy-start | bytes 393220
  1.4 11.5 %collective-permute-start.4 = (f32[640,128]{1,0:T(8,128)S(1)}, f32[640,128]{1,0:T(8,128)S(1)}, u32[]{:S(2)}, u32[]{:S(2)}) collective-permute-start(f32[640,128]{1,0:T(8,128)S(1)} %get-tuple-element.35), channel_id=1, source_target_pairs={{0,8},{4,12},{8,0},{12,4},{16,24},{20,28},{24,16},{28,20},{1,9},{5... | collective-permute-start | bytes 983048 | tf_op jit(solution)/shard_map/ppermute | solution.py:52
  4.4 17.7 %collective-permute-start.5 = (f32[640,128]{1,0:T(8,128)S(1)}, f32[640,128]{1,0:T(8,128)S(1)}, u32[]{:S(2)}, u32[]{:S(2)}) collective-permute-start(f32[640,128]{1,0:T(8,128)S(1)} %get-tuple-element.36), channel_id=1, source_target_pairs={{0,16},{4,20},{8,24},{12,28},{16,0},{20,4},{24,8},{28,12},{1,17},{... | collective-permute-start | bytes 983048 | tf_op jit(solution)/shard_map/ppermute | solution.py:52
  5.9 16.1 %collective-permute-start.6 = (f32[640,128]{1,0:T(8,128)S(1)}, f32[640,128]{1,0:T(8,128)S(1)}, u32[]{:S(2)}, u32[]{:S(2)}) collective-permute-start(f32[640,128]{1,0:T(8,128)S(1)} %get-tuple-element.37), channel_id=1, source_target_pairs={{0,24},{4,28},{8,16},{12,20},{16,8},{20,12},{24,0},{28,4},{1,25},{... | collective-permute-start | bytes 983048 | tf_op jit(solution)/shard_map/ppermute | solution.py:52
  7.2 17.3 %collective-permute-start = (f32[416,128]{1,0:T(8,128)S(1)}, f32[416,128]{1,0:T(8,128)S(1)}, u32[]{:S(2)}, u32[]{:S(2)}) collective-permute-start(f32[416,128]{1,0:T(8,128)S(1)} %get-tuple-element.29), channel_id=1, source_target_pairs={{0,8},{4,12},{8,0},{12,4},{16,24},{20,28},{24,16},{28,20},{1,9},{5... | collective-permute-start | bytes 638984 | tf_op jit(solution)/shard_map/ppermute | solution.py:52
  9.2 20.5 %collective-permute-start.1 = (f32[416,128]{1,0:T(8,128)S(1)}, f32[416,128]{1,0:T(8,128)S(1)}, u32[]{:S(2)}, u32[]{:S(2)}) collective-permute-start(f32[416,128]{1,0:T(8,128)S(1)} %get-tuple-element.30), channel_id=1, source_target_pairs={{0,16},{4,20},{8,24},{12,28},{16,0},{20,4},{24,8},{28,12},{1,17},{... | collective-permute-start | bytes 638984 | tf_op jit(solution)/shard_map/ppermute | solution.py:52
  12.9 16.8 %collective-permute-start.2 = (f32[416,128]{1,0:T(8,128)S(1)}, f32[416,128]{1,0:T(8,128)S(1)}, u32[]{:S(2)}, u32[]{:S(2)}) collective-permute-start(f32[416,128]{1,0:T(8,128)S(1)} %get-tuple-element.31), channel_id=1, source_target_pairs={{0,24},{4,28},{8,16},{12,20},{16,8},{20,12},{24,0},{28,4},{1,25},{... | collective-permute-start | bytes 638984 | tf_op jit(solution)/shard_map/ppermute | solution.py:52
  22.6 7.7 %collective-permute-start.7 = (f32[64,1280]{1,0:T(8,128)S(1)}, f32[64,1280]{1,0:T(8,128)S(1)}, u32[]{:S(2)}, u32[]{:S(2)}) collective-permute-start(f32[64,1280]{1,0:T(8,128)S(1)} %get-tuple-element.38.mine_ref), channel_id=1, source_target_pairs={{0,4},{4,0},{8,12},{12,8},{16,20},{20,16},{24,28},{28,24},{1,5},{5... | collective-permute-start | bytes 983048 | tf_op jit(solution)/shard_map/ppermute | solution.py:52
  30.1 1.6 %collective-permute-start.3 = (f32[64,896]{1,0:T(8,128)S(1)}, f32[64,896]{1,0:T(8,128)S(1)}, u32[]{:S(2)}, u32[]{:S(2)}) collective-permute-start(f32[64,896]{1,0:T(8,128)S(1)} %get-tuple-element.32.mine_ref), channel_id=1, source_target_pairs={{0,4},{4,0},{8,12},{12,8},{16,20},{20,16},{24,28},{28,24},{1,5},{5... | collective-permute-start | bytes 688136 | tf_op jit(solution)/shard_map/ppermute | solution.py:52
  32.2 5.3 %collective-permute-start.10 = (f32[64,256]{1,0:T(8,128)S(1)}, f32[64,256]{1,0:T(8,128)S(1)}, u32[]{:S(2)}, u32[]{:S(2)}) collective-permute-start(f32[64,256]{1,0:T(8,128)S(1)} %shard_map.33), channel_id=1, source_target_pairs={{0,24},{4,28},{8,16},{12,20},{16,8},{20,12},{24,0},{28,4},{1,25},{... | collective-permute-start | bytes 196616 | tf_op jit(solution)/shard_map/ppermute | solution.py:52
  33.7 4.9 %collective-permute-start.9 = (f32[64,256]{1,0:T(8,128)S(1)}, f32[64,256]{1,0:T(8,128)S(1)}, u32[]{:S(2)}, u32[]{:S(2)}) collective-permute-start(f32[64,256]{1,0:T(8,128)S(1)} %shard_map.33), channel_id=1, source_target_pairs={{0,16},{4,20},{8,24},{12,28},{16,0},{20,4},{24,8},{28,12},{1,17},{... | collective-permute-start | bytes 196616 | tf_op jit(solution)/shard_map/ppermute | solution.py:52
  35.0 4.3 %collective-permute-start.8 = (f32[64,256]{1,0:T(8,128)S(1)}, f32[64,256]{1,0:T(8,128)S(1)}, u32[]{:S(2)}, u32[]{:S(2)}) collective-permute-start(f32[64,256]{1,0:T(8,128)S(1)} %shard_map.33), channel_id=1, source_target_pairs={{0,8},{4,12},{8,0},{12,4},{16,24},{20,28},{24,16},{28,20},{1,9},{5... | collective-permute-start | bytes 196616 | tf_op jit(solution)/shard_map/ppermute | solution.py:52
  39.2 6.8 %collective-permute-start.13 = (f32[64,256]{1,0:T(8,128)S(1)}, f32[64,256]{1,0:T(8,128)S(1)}, u32[]{:S(2)}, u32[]{:S(2)}) collective-permute-start(f32[64,256]{1,0:T(8,128)S(1)} %add_add_fusion.1), channel_id=1, source_target_pairs={{0,3},{1,2},{2,1},{3,0},{4,7},{5,6},{6,5},{7,4},{8,11},{9,10},{10,... | collective-permute-start | bytes 196616 | tf_op jit(solution)/shard_map/ppermute | solution.py:52
  42.9 5.3 %collective-permute-start.12 = (f32[64,256]{1,0:T(8,128)S(1)}, f32[64,256]{1,0:T(8,128)S(1)}, u32[]{:S(2)}, u32[]{:S(2)}) collective-permute-start(f32[64,256]{1,0:T(8,128)S(1)} %add_add_fusion.1), channel_id=1, source_target_pairs={{0,2},{1,3},{2,0},{3,1},{4,6},{5,7},{6,4},{7,5},{8,10},{9,11},{10,... | collective-permute-start | bytes 196616 | tf_op jit(solution)/shard_map/ppermute | solution.py:52
  42.9 5.3 %collective-permute-start.11 = (f32[64,256]{1,0:T(8,128)S(1)}, f32[64,256]{1,0:T(8,128)S(1)}, u32[]{:S(2)}, u32[]{:S(2)}) collective-permute-start(f32[64,256]{1,0:T(8,128)S(1)} %add_add_fusion.1), channel_id=1, source_target_pairs={{0,1},{1,0},{2,3},{3,2},{4,5},{5,4},{6,7},{7,6},{8,9},{9,8},{10,11... | collective-permute-start | bytes 196616 | tf_op jit(solution)/shard_map/ppermute | solution.py:52
  48.4 1.3 %collective-permute-start.14 = (f32[64,64]{1,0:T(8,128)S(1)}, f32[64,64]{1,0:T(8,128)S(1)}, u32[]{:S(2)}, u32[]{:S(2)}) collective-permute-start(f32[64,64]{1,0:T(8,128)S(1)} %shard_map.34.mine_ref), channel_id=1, source_target_pairs={{0,4},{4,0},{8,12},{12,8},{16,20},{20,16},{24,28},{28,24},{1,5},{5... | collective-permute-start | bytes 49160 | tf_op jit(solution)/shard_map/ppermute | solution.py:52
  52.2 1.6 %collective-permute-start.15 = (f32[4,17,8,128]{3,2,1,0:T(8,128)S(1)}, f32[4,17,8,128]{3,2,1,0:T(8,128)S(1)}, u32[]{:S(2)}, u32[]{:S(2)}) collective-permute-start(f32[4,17,8,128]{3,2,1,0:T(8,128)S(1)} %get-tuple-element.44), channel_id=1, source_target_pairs={{0,4},{4,0},{8,12},{12,8},{16,20},{20,16},{24,28},{28,24},{1,5},{5... | collective-permute-start | bytes 835592 | tf_op jit(solution)/shard_map/ppermute | solution.py:52
  53.9 4.4 %collective-permute-start.16 = (f32[17,8,128]{2,1,0:T(8,128)S(1)}, f32[17,8,128]{2,1,0:T(8,128)S(1)}, u32[]{:S(2)}, u32[]{:S(2)}) collective-permute-start(f32[17,8,128]{2,1,0:T(8,128)S(1)} %get-tuple-element.46), channel_id=1, source_target_pairs={{0,8},{4,12},{8,0},{12,4},{16,24},{20,28},{24,16},{28,20},{1,9},{5... | collective-permute-start | bytes 208904 | tf_op jit(solution)/shard_map/ppermute | solution.py:52
  55.0 4.3 %collective-permute-start.17 = (f32[17,8,128]{2,1,0:T(8,128)S(1)}, f32[17,8,128]{2,1,0:T(8,128)S(1)}, u32[]{:S(2)}, u32[]{:S(2)}) collective-permute-start(f32[17,8,128]{2,1,0:T(8,128)S(1)} %get-tuple-element.47), channel_id=1, source_target_pairs={{0,16},{4,20},{8,24},{12,28},{16,0},{20,4},{24,8},{28,12},{1,17},{... | collective-permute-start | bytes 208904 | tf_op jit(solution)/shard_map/ppermute | solution.py:52
  56.2 5.2 %collective-permute-start.18 = (f32[17,8,128]{2,1,0:T(8,128)S(1)}, f32[17,8,128]{2,1,0:T(8,128)S(1)}, u32[]{:S(2)}, u32[]{:S(2)}) collective-permute-start(f32[17,8,128]{2,1,0:T(8,128)S(1)} %get-tuple-element.48), channel_id=1, source_target_pairs={{0,24},{4,28},{8,16},{12,20},{16,8},{20,12},{24,0},{28,4},{1,25},{... | collective-permute-start | bytes 208904 | tf_op jit(solution)/shard_map/ppermute | solution.py:52

commit v6 on v5

--- a/solution.py
+++ b/solution.py
@@ -46,6 +46,18 @@
         value = jnp.where((me & bit) != 0, swapped, value)
         bit *= 2
     return value
+
+
+def far_first(masks):
+    return [masks[-1], *masks[:-1]]
+
+
+def for_order(blocks):
+    return [blocks[k] for k in [*far_first(range(1, len(blocks))), 0]]
+
+
+def in_order(refs):
+    return [refs[-1], *refs[1:-1], refs[0]]
 
 
 def exchange(value, axis, mask, size):
@@ -112,7 +124,7 @@
 
 def project_kernel(count, left, width, me_ref, start_ref, *refs):
     chips, me = (start_ref.shape[1] // width) // 2, me_ref[0]
-    refs, (out_ref, high_ref, low_ref, *rest_refs) = refs[:chips], refs[chips:]
+    refs, (out_ref, high_ref, low_ref, *rest_refs) = in_order(refs[:chips]), refs[chips:]
     ny = refs[0].shape[1]
     parts = [start_ref[:, i * width : (i + 1) * width] for i in range(2 * chips)]
     odd = (me & 1) != 0
@@ -138,7 +150,7 @@
         out_specs=[VMEM] * (3 + len(rest)),
         out_shape=[columns, pairs, pairs] + rest,
         compiler_params=PARAMS,
-    )(me, start_t, *blocks)
+    )(me, start_t, *for_order(blocks))
 
 
 def split_slabs(high_ref, low_ref, count, ny):
@@ -176,8 +188,8 @@
 def sum_over(value, axis, low, size):
     while low < size:
         masks = [low] if 2 * low >= size else [low, 2 * low, 3 * low]
-        got = [exchange(value, axis, mask, size) for mask in masks]
-        for term in got:
+        got = [exchange(value, axis, mask, size) for mask in far_first(masks)]
+        for term in reversed(got):
             value = value + term
         low *= len(masks) + 1
     return value
@@ -286,6 +298,7 @@
 def place_kernel(own, left, cells, me_ref, *refs):
     refs, (out_ref, rest, sems) = refs[:-3], refs[-3:]
     chips = len(refs)
+    refs = in_order(refs)
     chip = lax.div(me_ref[0], 2)
     copies = []
     for k, ref in enumerate(refs):
@@ -311,7 +324,7 @@
         out_shape=jax.ShapeDtypeStruct((chips * own + left, each, ny), F32),
         scratch_shapes=[pltpu.VMEM((left, each, ny), F32), pltpu.SemaphoreType.DMA((chips + 1,))],
         compiler_params=PARAMS,
-    )(me, *parts)
+    )(me, *for_order(parts))
 
 
 def shards(n, layers, field_data, start_block):

time: 62.5 us -> 61.4 us (0.982)
  starting transfers between devices: 23.1 us -> 22.1 us
    ppermute x19, starting transfers between devices: 23.1 us -> 22.1 us  [exchange(): return lax.ppermute(value, axis, [(i, i ^ mask) for i in range(size)])]
  transfers between devices with their start and end apart: 19 -> 19, of which waited for: 15 -> 16; matrix products, arithmetic and copies ran while one was open for 0% -> 0% of each run, Pallas kernels for 4% -> 5%
where the time goes in v6:
time: 61.4 us; the launch traced here: 61.3 us
  waiting for transfers between devices  30.9 us (50%)
  starting transfers between devices  22.1 us (36%)
  Pallas kernels  8.19 us (13%)
    ppermute x19, waiting for transfers between devices, exchange(): return lax.ppermute(value, axis, [(i, i ^ mask) for i in range(size)])  30.9 us
    ppermute x19, starting transfers between devices, exchange(): return lax.ppermute(value, axis, [(i, i ^ mask) for i in range(size)])  22.1 us
    pallas_call x2, Pallas kernels, pack(): pl.pallas_call(functools.partial(pack_kernel, chips, first, last, own, le...  2.64 us
    pallas_call x1, Pallas kernels, core(): pl.pallas_call(functools.partial(core_kernel, counts), in_specs=[SMEM] +...  2.52 us
  transfers between devices with their start and end apart: 19, of which 16 were waited for; matrix products, arithmetic and copies ran while one was open for 0% of the time, Pallas kernels for 5%

profile of v6, /device:TPU:0, one launch (start us, length us, event | category | flops | bytes accessed | tf_op | source)
XLA Modules:
  0.0 61.3 jit_solution(15752778393874073407)
XLA Ops:
  0.0 1.3 %shard_map.28 = (f32[640,128]{1,0:T(8,128)S(1)}, f32[640,128]{1,0:T(8,128)S(1)}, f32[640,128]{1,0:T(8,128)S(1)}, f32[640,128]{1,0:T(8,128)S(1)}) custom-call(s32[1]{0:T(128)} %bitcast.me_ref.after, f32[4224,128]{1,0:T(8,128)} %bitcast.6, s32[1]{0:T(128)} %bitcast.me_ref.after), custom_call_target="tpu_custom_call" | custom-call | tf_op jit(solution)/shard_map/pallas_call | solution.py:97
  1.4 4.0 %collective-permute-start.4 = (f32[640,128]{1,0:T(8,128)S(1)}, f32[640,128]{1,0:T(8,128)S(1)}, u32[]{:S(2)}, u32[]{:S(2)}) collective-permute-start(f32[640,128]{1,0:T(8,128)S(1)} %get-tuple-element.35), channel_id=1, source_target_pairs={{0,24},{4,28},{8,16},{12,20},{16,8},{20,12},{24,0},{28,4},{1,25},{... | collective-permute-start | bytes 983048 | tf_op jit(solution)/shard_map/ppermute | solution.py:64
  5.3 0.5 collective-permute-start.5
  6.0 1.3 %shard_map.29 = (f32[416,128]{1,0:T(8,128)S(1)}, f32[416,128]{1,0:T(8,128)S(1)}, f32[416,128]{1,0:T(8,128)S(1)}, f32[416,128]{1,0:T(8,128)S(1)}) custom-call(s32[1]{0:T(128)} %bitcast.me_ref.after, f32[4224,128]{1,0:T(8,128)} %bitcast.7, f32[640,128]{1,0:T(8,128)S(1)} %get-tuple-element.27.after.refs_3_), custom_call_target="tpu_custom_call" | custom-call | tf_op jit(solution)/shard_map/pallas_call | solution.py:97
  7.3 2.9 %collective-permute-start = (f32[416,128]{1,0:T(8,128)S(1)}, f32[416,128]{1,0:T(8,128)S(1)}, u32[]{:S(2)}, u32[]{:S(2)}) collective-permute-start(f32[416,128]{1,0:T(8,128)S(1)} %get-tuple-element.28), channel_id=1, source_target_pairs={{0,24},{4,28},{8,16},{12,20},{16,8},{20,12},{24,0},{28,4},{1,25},{... | collective-permute-start | bytes 638984 | tf_op jit(solution)/shard_map/ppermute | solution.py:64
  10.2 0.5 collective-permute-start.1
  10.7 3.2 %collective-permute-done.4.refs_0_ = f32[640,128]{1,0:T(8,128)S(1)} collective-permute-done((f32[640,128]{1,0:T(8,128)S(1)}, f32[640,128]{1,0:T(8,128)S(1)}, u32[]{:S(2)}, u32[]{:S(2)}) %collective-permute-start.4) | collective-permute-done | bytes 327712 | tf_op jit(solution)/shard_map/ppermute | solution.py:64
  13.9 2.0 %collective-permute-start.2 = (f32[416,128]{1,0:T(8,128)S(1)}, f32[416,128]{1,0:T(8,128)S(1)}, u32[]{:S(2)}, u32[]{:S(2)}) collective-permute-start(f32[416,128]{1,0:T(8,128)S(1)} %get-tuple-element.30), channel_id=1, source_target_pairs={{0,16},{4,20},{8,24},{12,28},{16,0},{20,4},{24,8},{28,12},{1,17},{... | collective-permute-start | bytes 638984 | tf_op jit(solution)/shard_map/ppermute | solution.py:64
  15.9 5.6 %collective-permute-done.5.refs_1_ = f32[640,128]{1,0:T(8,128)S(1)} collective-permute-done((f32[640,128]{1,0:T(8,128)S(1)}, f32[640,128]{1,0:T(8,128)S(1)}, u32[]{:S(2)}, u32[]{:S(2)}) %collective-permute-start.5) | collective-permute-done | bytes 327712 | tf_op jit(solution)/shard_map/ppermute | solution.py:64
  22.1 3.4 %collective-permute-done.refs_0_ = f32[416,128]{1,0:T(8,128)S(1)} collective-permute-done((f32[416,128]{1,0:T(8,128)S(1)}, f32[416,128]{1,0:T(8,128)S(1)}, u32[]{:S(2)}, u32[]{:S(2)}) %collective-permute-start) | collective-permute-done | bytes 213024 | tf_op jit(solution)/shard_map/ppermute | solution.py:64
  25.5 4.0 %collective-permute-done.1.refs_1_ = f32[416,128]{1,0:T(8,128)S(1)} collective-permute-done((f32[416,128]{1,0:T(8,128)S(1)}, f32[416,128]{1,0:T(8,128)S(1)}, u32[]{:S(2)}, u32[]{:S(2)}) %collective-permute-start.1) | collective-permute-done | bytes 213024 | tf_op jit(solution)/shard_map/ppermute | solution.py:64
  30.6 0.9 %collective-permute-done.3.other_ref = f32[64,896]{1,0:T(8,128)S(1)} collective-permute-done((f32[64,896]{1,0:T(8,128)S(1)}, f32[64,896]{1,0:T(8,128)S(1)}, u32[]{:S(2)}, u32[]{:S(2)}) %collective-permute-start.3) | collective-permute-done | bytes 229408 | tf_op jit(solution)/shard_map/ppermute | solution.py:64
  32.0 2.4 %collective-permute-start.10 = (f32[64,256]{1,0:T(8,128)S(1)}, f32[64,256]{1,0:T(8,128)S(1)}, u32[]{:S(2)}, u32[]{:S(2)}) collective-permute-start(f32[64,256]{1,0:T(8,128)S(1)} %shard_map.33), channel_id=1, source_target_pairs={{0,24},{4,28},{8,16},{12,20},{16,8},{20,12},{24,0},{28,4},{1,25},{... | collective-permute-start | bytes 196616 | tf_op jit(solution)/shard_map/ppermute | solution.py:64
  34.4 0.5 collective-permute-start.9
  34.9 0.7 %collective-permute-start.8 = (f32[64,256]{1,0:T(8,128)S(1)}, f32[64,256]{1,0:T(8,128)S(1)}, u32[]{:S(2)}, u32[]{:S(2)}) collective-permute-start(f32[64,256]{1,0:T(8,128)S(1)} %shard_map.33), channel_id=1, source_target_pairs={{0,16},{4,20},{8,24},{12,28},{16,0},{20,4},{24,8},{28,12},{1,17},{... | collective-permute-start | bytes 196616 | tf_op jit(solution)/shard_map/ppermute | solution.py:64
  35.5 2.1 %collective-permute-done.10 = f32[64,256]{1,0:T(8,128)S(1)} collective-permute-done((f32[64,256]{1,0:T(8,128)S(1)}, f32[64,256]{1,0:T(8,128)S(1)}, u32[]{:S(2)}, u32[]{:S(2)}) %collective-permute-start.10) | collective-permute-done | bytes 65568 | tf_op jit(solution)/shard_map/ppermute | solution.py:64
  37.6 1.0 %collective-permute-done.9 = f32[64,256]{1,0:T(8,128)S(1)} collective-permute-done((f32[64,256]{1,0:T(8,128)S(1)}, f32[64,256]{1,0:T(8,128)S(1)}, u32[]{:S(2)}, u32[]{:S(2)}) %collective-permute-start.9) | collective-permute-done | bytes 65568 | tf_op jit(solution)/shard_map/ppermute | solution.py:64
  38.6 0.5 collective-permute-done.8
  39.2 3.7 %collective-permute-start.13 = (f32[64,256]{1,0:T(8,128)S(1)}, f32[64,256]{1,0:T(8,128)S(1)}, u32[]{:S(2)}, u32[]{:S(2)}) collective-permute-start(f32[64,256]{1,0:T(8,128)S(1)} %add_add_fusion.1), channel_id=1, source_target_pairs={{0,3},{1,2},{2,1},{3,0},{4,7},{5,6},{6,5},{7,4},{8,11},{9,10},{10,... | collective-permute-start | bytes 196616 | tf_op jit(solution)/shard_map/ppermute | solution.py:64
  42.8 0.8 %collective-permute-start.11 = (f32[64,256]{1,0:T(8,128)S(1)}, f32[64,256]{1,0:T(8,128)S(1)}, u32[]{:S(2)}, u32[]{:S(2)}) collective-permute-start(f32[64,256]{1,0:T(8,128)S(1)} %add_add_fusion.1), channel_id=1, source_target_pairs={{0,2},{1,3},{2,0},{3,1},{4,6},{5,7},{6,4},{7,5},{8,10},{9,11},{10,... | collective-permute-start | bytes 196616 | tf_op jit(solution)/shard_map/ppermute | solution.py:64
  43.6 1.8 %collective-permute-done.13 = f32[64,256]{1,0:T(8,128)S(1)} collective-permute-done((f32[64,256]{1,0:T(8,128)S(1)}, f32[64,256]{1,0:T(8,128)S(1)}, u32[]{:S(2)}, u32[]{:S(2)}) %collective-permute-start.13) | collective-permute-done | bytes 65568 | tf_op jit(solution)/shard_map/ppermute | solution.py:64
  45.4 1.7 %collective-permute-done.12 = f32[64,256]{1,0:T(8,128)S(1)} collective-permute-done((f32[64,256]{1,0:T(8,128)S(1)}, f32[64,256]{1,0:T(8,128)S(1)}, u32[]{:S(2)}, u32[]{:S(2)}) %collective-permute-start.12) | collective-permute-done | bytes 65568 | tf_op jit(solution)/shard_map/ppermute | solution.py:64
  47.1 0.9 %collective-permute-done.11 = f32[64,256]{1,0:T(8,128)S(1)} collective-permute-done((f32[64,256]{1,0:T(8,128)S(1)}, f32[64,256]{1,0:T(8,128)S(1)}, u32[]{:S(2)}, u32[]{:S(2)}) %collective-permute-start.11) | collective-permute-done | bytes 65568 | tf_op jit(solution)/shard_map/ppermute | solution.py:64
  48.3 1.2 %collective-permute-done.14.other_ref = f32[64,64]{1,0:T(8,128)S(1)} collective-permute-done((f32[64,64]{1,0:T(8,128)S(1)}, f32[64,64]{1,0:T(8,128)S(1)}, u32[]{:S(2)}, u32[]{:S(2)}) %collective-permute-start.14) | collective-permute-done | bytes 16416 | tf_op jit(solution)/shard_map/ppermute | solution.py:64
  49.5 2.5 %shard_map.35 = (f32[4,17,8,128]{3,2,1,0:T(8,128)S(1)}, f32[4,17,8,128]{3,2,1,0:T(8,128)S(1)}) custom-call(s32[1]{0:T(128)} %bitcast.me_ref.after, f32[64,64]{1,0:T(8,128)S(1)} %shard_map.34.mine_ref, f32[64,64]{1,0:T(8,128)S(1)} %collective-permute-done.14.other_ref, f32[64,256]{1,0:T(8,128)S(1)} %add_add_fusion.raw_ref, ...), custom_call_target="tpu_custom_call" | custom-call | tf_op jit(solution)/shard_map/pallas_call | solution.py:273
  52.3 1.4 %collective-permute-done.15.got_ref = f32[4,17,8,128]{3,2,1,0:T(8,128)S(1)} collective-permute-done((f32[4,17,8,128]{3,2,1,0:T(8,128)S(1)}, f32[4,17,8,128]{3,2,1,0:T(8,128)S(1)}, u32[]{:S(2)}, u32[]{:S(2)}) %collective-permute-start.15) | collective-permute-done | bytes 278560 | tf_op jit(solution)/shard_map/ppermute | solution.py:64
  53.7 1.7 %collective-permute-start.16 = (f32[17,8,128]{2,1,0:T(8,128)S(1)}, f32[17,8,128]{2,1,0:T(8,128)S(1)}, u32[]{:S(2)}, u32[]{:S(2)}) collective-permute-start(f32[17,8,128]{2,1,0:T(8,128)S(1)} %get-tuple-element.45), channel_id=1, source_target_pairs={{0,24},{4,28},{8,16},{12,20},{16,8},{20,12},{24,0},{28,4},{1,25},{... | collective-permute-start | bytes 208904 | tf_op jit(solution)/shard_map/ppermute | solution.py:64
  55.4 0.6 collective-permute-start.17
  56.0 1.2 %collective-permute-start.18 = (f32[17,8,128]{2,1,0:T(8,128)S(1)}, f32[17,8,128]{2,1,0:T(8,128)S(1)}, u32[]{:S(2)}, u32[]{:S(2)}) collective-permute-start(f32[17,8,128]{2,1,0:T(8,128)S(1)} %get-tuple-element.47), channel_id=1, source_target_pairs={{0,16},{4,20},{8,24},{12,28},{16,0},{20,4},{24,8},{28,12},{1,17},{... | collective-permute-start | bytes 208904 | tf_op jit(solution)/shard_map/ppermute | solution.py:64
  57.2 2.1 %collective-permute-done.16.refs_0_ = f32[17,8,128]{2,1,0:T(8,128)S(1)} collective-permute-done((f32[17,8,128]{2,1,0:T(8,128)S(1)}, f32[17,8,128]{2,1,0:T(8,128)S(1)}, u32[]{:S(2)}, u32[]{:S(2)}) %collective-permute-start.16) | collective-permute-done | bytes 69664 | tf_op jit(solution)/shard_map/ppermute | solution.py:64
  59.8 0.7 %collective-permute-done.18.refs_2_ = f32[17,8,128]{2,1,0:T(8,128)S(1)} collective-permute-done((f32[17,8,128]{2,1,0:T(8,128)S(1)}, f32[17,8,128]{2,1,0:T(8,128)S(1)}, u32[]{:S(2)}, u32[]{:S(2)}) %collective-permute-start.18) | collective-permute-done | bytes 69664 | tf_op jit(solution)/shard_map/ppermute | solution.py:64
  60.4 0.9 %shard_map.37 = f32[66,8,128]{2,1,0:T(8,128)} custom-call(s32[1]{0:T(128)} %bitcast.me_ref.after, f32[17,8,128]{2,1,0:T(8,128)S(1)} %collective-permute-done.16.refs_0_, f32[17,8,128]{2,1,0:T(8,128)S(1)} %collective-permute-done.17.refs_1_, f32[17,8,128]{2,1,0:T(8,128)S(1)} %collective-permute-done.18.refs_2_, f32[17,8,128]{2,1,0:T(8,128)S(1)} %get-tuple-element.48.refs_3_), custom_call_target="tpu_custom_call" | custom-call | tf_op jit(solution)/shard_map/pallas_call | solution.py:320
  (20 shorter events, 3.1 us)
Async XLA Ops:
  0.0 21.5 %copy-start = (f32[512,64]{0,1:T(8,128)S(1)}, f32[512,64]{0,1:T(8,128)}, u32[]{:S(2)}) copy-start(f32[512,64]{0,1:T(8,128)} %param.3) | copy-start | bytes 393220
  1.4 12.5 %collective-permute-start.4 = (f32[640,128]{1,0:T(8,128)S(1)}, f32[640,128]{1,0:T(8,128)S(1)}, u32[]{:S(2)}, u32[]{:S(2)}) collective-permute-start(f32[640,128]{1,0:T(8,128)S(1)} %get-tuple-element.35), channel_id=1, source_target_pairs={{0,24},{4,28},{8,16},{12,20},{16,8},{20,12},{24,0},{28,4},{1,25},{... | collective-permute-start | bytes 983048 | tf_op jit(solution)/shard_map/ppermute | solution.py:64
  5.3 16.2 %collective-permute-start.5 = (f32[640,128]{1,0:T(8,128)S(1)}, f32[640,128]{1,0:T(8,128)S(1)}, u32[]{:S(2)}, u32[]{:S(2)}) collective-permute-start(f32[640,128]{1,0:T(8,128)S(1)} %get-tuple-element.36), channel_id=1, source_target_pairs={{0,8},{4,12},{8,0},{12,4},{16,24},{20,28},{24,16},{28,20},{1,9},{5... | collective-permute-start | bytes 983048 | tf_op jit(solution)/shard_map/ppermute | solution.py:64
  5.9 15.6 %collective-permute-start.6 = (f32[640,128]{1,0:T(8,128)S(1)}, f32[640,128]{1,0:T(8,128)S(1)}, u32[]{:S(2)}, u32[]{:S(2)}) collective-permute-start(f32[640,128]{1,0:T(8,128)S(1)} %get-tuple-element.37), channel_id=1, source_target_pairs={{0,16},{4,20},{8,24},{12,28},{16,0},{20,4},{24,8},{28,12},{1,17},{... | collective-permute-start | bytes 983048 | tf_op jit(solution)/shard_map/ppermute | solution.py:64
  7.3 18.3 %collective-permute-start = (f32[416,128]{1,0:T(8,128)S(1)}, f32[416,128]{1,0:T(8,128)S(1)}, u32[]{:S(2)}, u32[]{:S(2)}) collective-permute-start(f32[416,128]{1,0:T(8,128)S(1)} %get-tuple-element.28), channel_id=1, source_target_pairs={{0,24},{4,28},{8,16},{12,20},{16,8},{20,12},{24,0},{28,4},{1,25},{... | collective-permute-start | bytes 638984 | tf_op jit(solution)/shard_map/ppermute | solution.py:64
  10.2 19.3 %collective-permute-start.1 = (f32[416,128]{1,0:T(8,128)S(1)}, f32[416,128]{1,0:T(8,128)S(1)}, u32[]{:S(2)}, u32[]{:S(2)}) collective-permute-start(f32[416,128]{1,0:T(8,128)S(1)} %get-tuple-element.29), channel_id=1, source_target_pairs={{0,8},{4,12},{8,0},{12,4},{16,24},{20,28},{24,16},{28,20},{1,9},{5... | collective-permute-start | bytes 638984 | tf_op jit(solution)/shard_map/ppermute | solution.py:64
  13.9 15.6 %collective-permute-start.2 = (f32[416,128]{1,0:T(8,128)S(1)}, f32[416,128]{1,0:T(8,128)S(1)}, u32[]{:S(2)}, u32[]{:S(2)}) collective-permute-start(f32[416,128]{1,0:T(8,128)S(1)} %get-tuple-element.30), channel_id=1, source_target_pairs={{0,16},{4,20},{8,24},{12,28},{16,0},{20,4},{24,8},{28,12},{1,17},{... | collective-permute-start | bytes 638984 | tf_op jit(solution)/shard_map/ppermute | solution.py:64
  22.0 8.0 %collective-permute-start.7 = (f32[64,1280]{1,0:T(8,128)S(1)}, f32[64,1280]{1,0:T(8,128)S(1)}, u32[]{:S(2)}, u32[]{:S(2)}) collective-permute-start(f32[64,1280]{1,0:T(8,128)S(1)} %get-tuple-element.38.mine_ref), channel_id=1, source_target_pairs={{0,4},{4,0},{8,12},{12,8},{16,20},{20,16},{24,28},{28,24},{1,5},{5... | collective-permute-start | bytes 983048 | tf_op jit(solution)/shard_map/ppermute | solution.py:64
  30.0 1.6 %collective-permute-start.3 = (f32[64,896]{1,0:T(8,128)S(1)}, f32[64,896]{1,0:T(8,128)S(1)}, u32[]{:S(2)}, u32[]{:S(2)}) collective-permute-start(f32[64,896]{1,0:T(8,128)S(1)} %get-tuple-element.32.mine_ref), channel_id=1, source_target_pairs={{0,4},{4,0},{8,12},{12,8},{16,20},{20,16},{24,28},{28,24},{1,5},{5... | collective-permute-start | bytes 688136 | tf_op jit(solution)/shard_map/ppermute | solution.py:64
  32.0 5.6 %collective-permute-start.10 = (f32[64,256]{1,0:T(8,128)S(1)}, f32[64,256]{1,0:T(8,128)S(1)}, u32[]{:S(2)}, u32[]{:S(2)}) collective-permute-start(f32[64,256]{1,0:T(8,128)S(1)} %shard_map.33), channel_id=1, source_target_pairs={{0,24},{4,28},{8,16},{12,20},{16,8},{20,12},{24,0},{28,4},{1,25},{... | collective-permute-start | bytes 196616 | tf_op jit(solution)/shard_map/ppermute | solution.py:64
  34.4 4.3 %collective-permute-start.9 = (f32[64,256]{1,0:T(8,128)S(1)}, f32[64,256]{1,0:T(8,128)S(1)}, u32[]{:S(2)}, u32[]{:S(2)}) collective-permute-start(f32[64,256]{1,0:T(8,128)S(1)} %shard_map.33), channel_id=1, source_target_pairs={{0,8},{4,12},{8,0},{12,4},{16,24},{20,28},{24,16},{28,20},{1,9},{5... | collective-permute-start | bytes 196616 | tf_op jit(solution)/shard_map/ppermute | solution.py:64
  34.9 4.3 %collective-permute-start.8 = (f32[64,256]{1,0:T(8,128)S(1)}, f32[64,256]{1,0:T(8,128)S(1)}, u32[]{:S(2)}, u32[]{:S(2)}) collective-permute-start(f32[64,256]{1,0:T(8,128)S(1)} %shard_map.33), channel_id=1, source_target_pairs={{0,16},{4,20},{8,24},{12,28},{16,0},{20,4},{24,8},{28,12},{1,17},{... | collective-permute-start | bytes 196616 | tf_op jit(solution)/shard_map/ppermute | solution.py:64
  39.2 6.3 %collective-permute-start.13 = (f32[64,256]{1,0:T(8,128)S(1)}, f32[64,256]{1,0:T(8,128)S(1)}, u32[]{:S(2)}, u32[]{:S(2)}) collective-permute-start(f32[64,256]{1,0:T(8,128)S(1)} %add_add_fusion.1), channel_id=1, source_target_pairs={{0,3},{1,2},{2,1},{3,0},{4,7},{5,6},{6,5},{7,4},{8,11},{9,10},{10,... | collective-permute-start | bytes 196616 | tf_op jit(solution)/shard_map/ppermute | solution.py:64
  42.8 4.3 %collective-permute-start.12 = (f32[64,256]{1,0:T(8,128)S(1)}, f32[64,256]{1,0:T(8,128)S(1)}, u32[]{:S(2)}, u32[]{:S(2)}) collective-permute-start(f32[64,256]{1,0:T(8,128)S(1)} %add_add_fusion.1), channel_id=1, source_target_pairs={{0,1},{1,0},{2,3},{3,2},{4,5},{5,4},{6,7},{7,6},{8,9},{9,8},{10,11... | collective-permute-start | bytes 196616 | tf_op jit(solution)/shard_map/ppermute | solution.py:64
  42.8 5.2 %collective-permute-start.11 = (f32[64,256]{1,0:T(8,128)S(1)}, f32[64,256]{1,0:T(8,128)S(1)}, u32[]{:S(2)}, u32[]{:S(2)}) collective-permute-start(f32[64,256]{1,0:T(8,128)S(1)} %add_add_fusion.1), channel_id=1, source_target_pairs={{0,2},{1,3},{2,0},{3,1},{4,6},{5,7},{6,4},{7,5},{8,10},{9,11},{10,... | collective-permute-start | bytes 196616 | tf_op jit(solution)/shard_map/ppermute | solution.py:64
  48.2 1.3 %collective-permute-start.14 = (f32[64,64]{1,0:T(8,128)S(1)}, f32[64,64]{1,0:T(8,128)S(1)}, u32[]{:S(2)}, u32[]{:S(2)}) collective-permute-start(f32[64,64]{1,0:T(8,128)S(1)} %shard_map.34.mine_ref), channel_id=1, source_target_pairs={{0,4},{4,0},{8,12},{12,8},{16,20},{20,16},{24,28},{28,24},{1,5},{5... | collective-permute-start | bytes 49160 | tf_op jit(solution)/shard_map/ppermute | solution.py:64
  52.0 1.6 %collective-permute-start.15 = (f32[4,17,8,128]{3,2,1,0:T(8,128)S(1)}, f32[4,17,8,128]{3,2,1,0:T(8,128)S(1)}, u32[]{:S(2)}, u32[]{:S(2)}) collective-permute-start(f32[4,17,8,128]{3,2,1,0:T(8,128)S(1)} %get-tuple-element.44), channel_id=1, source_target_pairs={{0,4},{4,0},{8,12},{12,8},{16,20},{20,16},{24,28},{28,24},{1,5},{5... | collective-permute-start | bytes 835592 | tf_op jit(solution)/shard_map/ppermute | solution.py:64
  53.7 5.7 %collective-permute-start.16 = (f32[17,8,128]{2,1,0:T(8,128)S(1)}, f32[17,8,128]{2,1,0:T(8,128)S(1)}, u32[]{:S(2)}, u32[]{:S(2)}) collective-permute-start(f32[17,8,128]{2,1,0:T(8,128)S(1)} %get-tuple-element.45), channel_id=1, source_target_pairs={{0,24},{4,28},{8,16},{12,20},{16,8},{20,12},{24,0},{28,4},{1,25},{... | collective-permute-start | bytes 208904 | tf_op jit(solution)/shard_map/ppermute | solution.py:64
  55.4 4.4 %collective-permute-start.17 = (f32[17,8,128]{2,1,0:T(8,128)S(1)}, f32[17,8,128]{2,1,0:T(8,128)S(1)}, u32[]{:S(2)}, u32[]{:S(2)}) collective-permute-start(f32[17,8,128]{2,1,0:T(8,128)S(1)} %get-tuple-element.46), channel_id=1, source_target_pairs={{0,8},{4,12},{8,0},{12,4},{16,24},{20,28},{24,16},{28,20},{1,9},{5... | collective-permute-start | bytes 208904 | tf_op jit(solution)/shard_map/ppermute | solution.py:64
  56.0 4.4 %collective-permute-start.18 = (f32[17,8,128]{2,1,0:T(8,128)S(1)}, f32[17,8,128]{2,1,0:T(8,128)S(1)}, u32[]{:S(2)}, u32[]{:S(2)}) collective-permute-start(f32[17,8,128]{2,1,0:T(8,128)S(1)} %get-tuple-element.47), channel_id=1, source_target_pairs={{0,16},{4,20},{8,24},{12,28},{16,0},{20,4},{24,8},{28,12},{1,17},{... | collective-permute-start | bytes 208904 | tf_op jit(solution)/shard_map/ppermute | solution.py:64

commit v7 on v6

--- a/solution.py
+++ b/solution.py
@@ -64,9 +64,9 @@
     return lax.ppermute(value, axis, [(i, i ^ mask) for i in range(size)])
 
 
-def pack_kernel(chips, first, last, own, left, width, me_ref, rows_ref, after, *refs):
+def pack_kernel(ks, chips, first, last, own, left, width, me_ref, rows_ref, after, *refs):
     del after
-    blocks, refs = refs[:chips], refs[chips:]
+    blocks, refs = refs[: len(ks)], refs[len(ks) :]
     ny = rows_ref.shape[1]
     chip = lax.div(me_ref[0], 2)
     sems = refs[-1]
@@ -76,7 +76,7 @@
         rest_copy = pltpu.make_async_copy(rows_ref.at[pl.ds(chips * own * width, left * width)], rest, sems.at[chips])
         rest_copy.start()
     copies = []
-    for k, block in enumerate(blocks):
+    for k, block in zip(ks, blocks):
         at = pl.multiple_of(((chip ^ k) * own + first) * width, 8)
         copies.append(pltpu.make_async_copy(rows_ref.at[pl.ds(at, count)], block.at[pl.ds(0, count)], sems.at[k]))
         copies[-1].start()
@@ -84,21 +84,21 @@
         cells = ny // chips
         rest_copy.wait()
         turned[:, : left * width] = rest[...].T
-        for k, block in enumerate(blocks):
+        for k, block in zip(ks, blocks):
             block[count:] = turned[pl.ds(pl.multiple_of((chip ^ k) * cells, cells), cells), :]
     for copy in copies:
         copy.wait()
 
 
-def pack(rows, me, after, chips, first, last, own, left, width):
+def pack(rows, me, after, ks, chips, first, last, own, left, width):
     ny = rows.shape[1]
     high = (last - first) * width + (ny // chips if left else 0)
     scratch = [pltpu.VMEM((ny, ny), F32), pltpu.VMEM((left * width, ny), F32)] if left else []
     return pl.pallas_call(
-        functools.partial(pack_kernel, chips, first, last, own, left, width),
+        functools.partial(pack_kernel, ks, chips, first, last, own, left, width),
         in_specs=[SMEM, HBM, pl.BlockSpec(memory_space=pl.ANY)],
-        out_specs=[VMEM] * chips,
-        out_shape=[jax.ShapeDtypeStruct((high, ny), F32)] * chips,
+        out_specs=[VMEM] * len(ks),
+        out_shape=[jax.ShapeDtypeStruct((high, ny), F32)] * len(ks),
         scratch_shapes=scratch + [pltpu.SemaphoreType.DMA((chips + 1,))],
         compiler_params=PARAMS,
     )(me, pltpu.with_memory_space_constraint(rows, pltpu.HBM), after)
@@ -243,56 +243,65 @@
     return jnp.concatenate(inverse, axis=0)
 
 
-def core_kernel(counts, me_ref, mine_ref, other_ref, raw_ref, *refs):
-    refs, (keep_ref, send_ref) = refs[:-2], refs[-2:]
-    chips = keep_ref.shape[0]
-    each, ny = keep_ref.shape[-2:]
-    me = me_ref[0]
-    inverse = inverse_factor(mine_ref[...] + other_ref[...])
-    inverse = reorder(inverse, me, 2 * chips, 0)
-    raw = reorder(raw_ref[...], lax.div(me, 2), chips, 1)
-    basis = stack(lax.dot_general(inverse, raw, NN, precision=HIGHEST, preferred_element_type=F32))
-
-    def put(slab, value):
-        for k in range(chips):
-            keep_ref[k, slab] = value[2 * k * each : (2 * k + 1) * each]
-            send_ref[k, slab] = value[(2 * k + 1) * each : (2 * k + 2) * each]
-
+def factor_kernel(mine_ref, other_ref, out_ref):
+    out_ref[...] = inverse_factor(mine_ref[...] + other_ref[...])
+
+
+def factor(mine, other):
+    return pl.pallas_call(
+        factor_kernel,
+        in_specs=[VMEM] * 2,
+        out_specs=VMEM,
+        out_shape=jax.ShapeDtypeStruct(mine.shape, F32),
+        compiler_params=PARAMS,
+        cost_estimate=pl.CostEstimate(flops=10**10, bytes_accessed=1000, transcendentals=0),
+    )(mine, other)
+
+
+def mixed_kernel(counts, chips, ny, after, me_ref, raw_ref, *refs):
+    del after
+    refs, out_ref = refs[:-1], refs[-1]
+    raw = stack(reorder(raw_ref[...], lax.div(me_ref[0], 2), chips, 1))
     done = 0
     for c, count in enumerate(counts):
         for at, to, slab in split_slabs(refs[2 * c], refs[2 * c + 1], count, ny):
-            value = dot_split(basis, slab, NN)
-            for lane in range(0, to - at, ny):
-                put(done + (at + lane) // ny, value[:, lane : lane + ny])
-        done += count
-    put(done, widen(dot_split(basis, (refs[-2][...], refs[-1][...]), NT), ny))
-
-
-def core(pairs, mine, other, raw, me, counts, chips, each, ny):
-    shape = jax.ShapeDtypeStruct((chips, sum(counts) + 1, each, ny), F32)
-    return pl.pallas_call(
-        functools.partial(core_kernel, counts),
-        in_specs=[SMEM] + [VMEM] * (3 + len(pairs)),
-        out_specs=[VMEM] * 2,
-        out_shape=[shape] * 2,
-        compiler_params=PARAMS,
-    )(me, mine, other, raw, *pairs)
-
-
-def add_kernel(keep_ref, got_ref, *outs):
-    for k, out in enumerate(outs):
-        out[...] = keep_ref[k] + got_ref[k]
-
-
-def add_parts(keep, got):
-    chips = keep.shape[0]
-    return pl.pallas_call(
-        add_kernel,
-        in_specs=[VMEM] * 2,
+            out_ref[:, done + at : done + to] = dot_split(raw, slab, NN)
+        done += count * ny
+    out_ref[:, done:] = widen(dot_split(raw, (refs[-2][...], refs[-1][...]), NT), ny)
+
+
+def mixed(raw, pairs, me, after, counts, chips, ny):
+    return pl.pallas_call(
+        functools.partial(mixed_kernel, counts, chips, ny),
+        in_specs=[pl.BlockSpec(memory_space=pl.ANY), SMEM] + [VMEM] * (1 + len(pairs)),
+        out_specs=VMEM,
+        out_shape=jax.ShapeDtypeStruct((raw.shape[0], (sum(counts) + 1) * ny), F32),
+        compiler_params=PARAMS,
+    )(after, me, raw, *pairs)
+
+
+def core_kernel(chips, me_ref, inverse_ref, mine_ref, other_ref, *outs):
+    slabs, each, ny = outs[0].shape
+    inverse = reorder(inverse_ref[...], me_ref[0], 2 * chips, 0)
+    inverse = jnp.concatenate([inverse[2 * k * each : (2 * k + 1) * each] for k in range(chips)], axis=0)
+    for s in range(0, slabs, 2):
+        to = min(s + 2, slabs)
+        both = mine_ref[:, s * ny : to * ny] + other_ref[:, s * ny : to * ny]
+        value = lax.dot_general(inverse, both, NN, precision=HIGHEST, preferred_element_type=F32)
+        for k in range(chips):
+            for slab in range(s, to):
+                lanes = slice((slab - s) * ny, (slab - s + 1) * ny)
+                outs[k][slab] = value[k * each : (k + 1) * each, lanes]
+
+
+def core(inverse, mine, other, me, chips, each, ny):
+    return pl.pallas_call(
+        functools.partial(core_kernel, chips),
+        in_specs=[SMEM] + [VMEM] * 3,
         out_specs=[VMEM] * chips,
-        out_shape=[jax.ShapeDtypeStruct(keep.shape[1:], F32)] * chips,
-        compiler_params=PARAMS,
-    )(keep, got)
+        out_shape=[jax.ShapeDtypeStruct((mine.shape[1] // ny, each, ny), F32)] * chips,
+        compiler_params=PARAMS,
+    )(me, inverse, mine, other)
 
 
 def place_kernel(own, left, cells, me_ref, *refs):
@@ -336,21 +345,25 @@
     me = lax.axis_index("fib").astype(jnp.int32).reshape(1)
     rows = field_data.reshape(total * width, ny)
     start_t = start_block.T
-    pairs, raw, first, after = [], None, 0, me
-    for c, count in enumerate(counts):
-        rest = left if c == len(counts) - 1 else 0
-        sent = pack(rows, me, after, chips, first, first + count, own, rest, width)
-        part = [sent[0]] + [exchange(sent[k], "fib", 2 * k, n) for k in range(1, chips)]
-        mine, *split = project(part, start_t, me, count, rest, width)
+    bounds = [(0, counts[0], 0), (counts[0], own, left)]
+    near, far = [*range(1, chips - 1)], [chips - 1]
+    sent, after = [{}, {}], me
+    for c, ks in [(0, far), (0, [0, *near]), (1, [0, *near, *far])]:
+        got = pack(rows, me, after, ks, chips, *bounds[c][:2], own, bounds[c][2], width)
+        sent[c].update(zip(ks, got))
+        after = got[0]
+    pairs, raw = [], None
+    for c, (first, last, rest) in enumerate(bounds):
+        part = [sent[c][0]] + [exchange(sent[c][k], "fib", 2 * k, n) for k in range(1, chips)]
+        mine, *split = project(part, start_t, me, last - first, rest, width)
         other = exchange(mine, "fib", 1, n)
-        raw = raw_part(mine, other, split, raw, me, count, ny, chips)
+        raw = raw_part(mine, other, split, raw, me, last - first, ny, chips)
         pairs += split
-        first += count
-        after = sent[0]
     raw = sum_over(sum_over(raw, "fib", 2, n), "blk", 1, layers)
     gram = gram_part(raw)
-    keep, send = core(pairs, gram, exchange(gram, "fib", 1, n), raw, me, counts, chips, each, ny)
-    parts = add_parts(keep, exchange(send, "fib", 1, n))
+    sums = mixed(raw, pairs, me, gram, counts, chips, ny)
+    inverse = factor(gram, exchange(gram, "fib", 1, n))
+    parts = core(inverse, sums, exchange(sums, "fib", 1, n), me, chips, each, ny)
     parts = [parts[0]] + [exchange(parts[k], "fib", 2 * k, n) for k in range(1, chips)]
     return place(parts, me, own, left).reshape(species, planes, each, ny)
 

time: 61.4 us -> 59.2 us (0.964)
  waiting for transfers between devices: 30.9 us -> 27.1 us
  Pallas kernels: 8.19 us -> 9.25 us
    ppermute x19, waiting for transfers between devices: 30.9 us -> 27.1 us  [exchange(): return lax.ppermute(value, axis, [(i, i ^ mask) for i in range(size)])]
    pallas_call x4 -> x6, Pallas kernels: 5.19 us -> 6.25 us  [the longest x3 3.52 us: pack(): pl.pallas_call(functools.partial(pack_kernel, ks, chips, first, last, own...]
  transfers between devices with their start and end apart: 19 -> 19, of which waited for: 16 -> 15; matrix products, arithmetic and copies ran while one was open for 0% -> 0% of each run, Pallas kernels for 5% -> 11%
where the time goes in v7:
time: 59.2 us; the launch traced here: 59 us
  waiting for transfers between devices  27.1 us (46%)
  starting transfers between devices  22.5 us (38%)
  Pallas kernels  9.25 us (16%)
    ppermute x19, waiting for transfers between devices, exchange(): return lax.ppermute(value, axis, [(i, i ^ mask) for i in range(size)])  27.1 us
    ppermute x19, starting transfers between devices, exchange(): return lax.ppermute(value, axis, [(i, i ^ mask) for i in range(size)])  22.5 us
    pallas_call x3, Pallas kernels, pack(): pl.pallas_call(functools.partial(pack_kernel, ks, chips, first, last, own...  3.52 us
    pallas_call x1, Pallas kernels, factor(): pl.pallas_call(factor_kernel, in_specs=[VMEM] * 2, out_specs=VMEM, out_sh...  1.8 us
  transfers between devices with their start and end apart: 19, of which 15 were waited for; matrix products, arithmetic and copies ran while one was open for 0% of the time, Pallas kernels for 11%

profile of v7, /device:TPU:0, one launch (start us, length us, event | category | flops | bytes accessed | tf_op | source)
XLA Modules:
  0.0 59.0 jit_solution(16711085817876734273)
XLA Ops:
  0.0 1.0 %shard_map.28.after = f32[640,128]{1,0:T(8,128)S(1)} custom-call(s32[1]{0:T(128)} %bitcast.me_ref.after, f32[4224,128]{1,0:T(8,128)} %bitcast.6, s32[1]{0:T(128)} %bitcast.me_ref.after), custom_call_target="tpu_custom_call" | custom-call | tf_op jit(solution)/shard_map/pallas_call | solution.py:97
  1.0 4.0 %collective-permute-start.4 = (f32[640,128]{1,0:T(8,128)S(1)}, f32[640,128]{1,0:T(8,128)S(1)}, u32[]{:S(2)}, u32[]{:S(2)}) collective-permute-start(f32[640,128]{1,0:T(8,128)S(1)} %shard_map.28.after), channel_id=1, source_target_pairs={{0,24},{4,28},{8,16},{12,20},{16,8},{20,12},{24,0},{28,4},{1,25},{... | collective-permute-start | bytes 983048 | tf_op jit(solution)/shard_map/ppermute | solution.py:64
  5.0 1.2 %shard_map.29 = (f32[640,128]{1,0:T(8,128)S(1)}, f32[640,128]{1,0:T(8,128)S(1)}, f32[640,128]{1,0:T(8,128)S(1)}) custom-call(s32[1]{0:T(128)} %bitcast.me_ref.after, f32[4224,128]{1,0:T(8,128)} %bitcast.7, f32[640,128]{1,0:T(8,128)S(1)} %shard_map.28.after), custom_call_target="tpu_custom_call" | custom-call | tf_op jit(solution)/shard_map/pallas_call | solution.py:97
  6.2 0.6 %collective-permute-start.5 = (f32[640,128]{1,0:T(8,128)S(1)}, f32[640,128]{1,0:T(8,128)S(1)}, u32[]{:S(2)}, u32[]{:S(2)}) collective-permute-start(f32[640,128]{1,0:T(8,128)S(1)} %get-tuple-element.32), channel_id=1, source_target_pairs={{0,8},{4,12},{8,0},{12,4},{16,24},{20,28},{24,16},{28,20},{1,9},{5... | collective-permute-start | bytes 983048 | tf_op jit(solution)/shard_map/ppermute | solution.py:64
  6.9 1.3 %shard_map.30 = (f32[416,128]{1,0:T(8,128)S(1)}, f32[416,128]{1,0:T(8,128)S(1)}, f32[416,128]{1,0:T(8,128)S(1)}, f32[416,128]{1,0:T(8,128)S(1)}) custom-call(s32[1]{0:T(128)} %bitcast.me_ref.after, f32[4224,128]{1,0:T(8,128)} %bitcast.8, f32[640,128]{1,0:T(8,128)S(1)} %get-tuple-element.24.after.refs_3_), custom_call_target="tpu_custom_call" | custom-call | tf_op jit(solution)/shard_map/pallas_call | solution.py:97
  8.2 3.0 %collective-permute-start = (f32[416,128]{1,0:T(8,128)S(1)}, f32[416,128]{1,0:T(8,128)S(1)}, u32[]{:S(2)}, u32[]{:S(2)}) collective-permute-start(f32[416,128]{1,0:T(8,128)S(1)} %get-tuple-element.25), channel_id=1, source_target_pairs={{0,24},{4,28},{8,16},{12,20},{16,8},{20,12},{24,0},{28,4},{1,25},{... | collective-permute-start | bytes 638984 | tf_op jit(solution)/shard_map/ppermute | solution.py:64
  11.1 0.5 collective-permute-start.1
  11.7 1.9 %collective-permute-done.4.refs_0_ = f32[640,128]{1,0:T(8,128)S(1)} collective-permute-done((f32[640,128]{1,0:T(8,128)S(1)}, f32[640,128]{1,0:T(8,128)S(1)}, u32[]{:S(2)}, u32[]{:S(2)}) %collective-permute-start.4) | collective-permute-done | bytes 327712 | tf_op jit(solution)/shard_map/ppermute | solution.py:64
  13.6 2.0 %collective-permute-start.2 = (f32[416,128]{1,0:T(8,128)S(1)}, f32[416,128]{1,0:T(8,128)S(1)}, u32[]{:S(2)}, u32[]{:S(2)}) collective-permute-start(f32[416,128]{1,0:T(8,128)S(1)} %get-tuple-element.27), channel_id=1, source_target_pairs={{0,16},{4,20},{8,24},{12,28},{16,0},{20,4},{24,8},{28,12},{1,17},{... | collective-permute-start | bytes 638984 | tf_op jit(solution)/shard_map/ppermute | solution.py:64
  15.6 5.6 %collective-permute-done.5.refs_1_ = f32[640,128]{1,0:T(8,128)S(1)} collective-permute-done((f32[640,128]{1,0:T(8,128)S(1)}, f32[640,128]{1,0:T(8,128)S(1)}, u32[]{:S(2)}, u32[]{:S(2)}) %collective-permute-start.5) | collective-permute-done | bytes 327712 | tf_op jit(solution)/shard_map/ppermute | solution.py:64
  21.8 3.4 %collective-permute-done.refs_0_ = f32[416,128]{1,0:T(8,128)S(1)} collective-permute-done((f32[416,128]{1,0:T(8,128)S(1)}, f32[416,128]{1,0:T(8,128)S(1)}, u32[]{:S(2)}, u32[]{:S(2)}) %collective-permute-start) | collective-permute-done | bytes 213024 | tf_op jit(solution)/shard_map/ppermute | solution.py:64
  25.2 4.0 %collective-permute-done.1.refs_1_ = f32[416,128]{1,0:T(8,128)S(1)} collective-permute-done((f32[416,128]{1,0:T(8,128)S(1)}, f32[416,128]{1,0:T(8,128)S(1)}, u32[]{:S(2)}, u32[]{:S(2)}) %collective-permute-start.1) | collective-permute-done | bytes 213024 | tf_op jit(solution)/shard_map/ppermute | solution.py:64
  30.3 0.9 %collective-permute-done.3.other_ref = f32[64,896]{1,0:T(8,128)S(1)} collective-permute-done((f32[64,896]{1,0:T(8,128)S(1)}, f32[64,896]{1,0:T(8,128)S(1)}, u32[]{:S(2)}, u32[]{:S(2)}) %collective-permute-start.3) | collective-permute-done | bytes 229408 | tf_op jit(solution)/shard_map/ppermute | solution.py:64
  31.7 2.4 %collective-permute-start.10 = (f32[64,256]{1,0:T(8,128)S(1)}, f32[64,256]{1,0:T(8,128)S(1)}, u32[]{:S(2)}, u32[]{:S(2)}) collective-permute-start(f32[64,256]{1,0:T(8,128)S(1)} %shard_map.34), channel_id=1, source_target_pairs={{0,24},{4,28},{8,16},{12,20},{16,8},{20,12},{24,0},{28,4},{1,25},{... | collective-permute-start | bytes 196616 | tf_op jit(solution)/shard_map/ppermute | solution.py:64
  34.0 0.5 collective-permute-start.9
  34.6 0.7 %collective-permute-start.8 = (f32[64,256]{1,0:T(8,128)S(1)}, f32[64,256]{1,0:T(8,128)S(1)}, u32[]{:S(2)}, u32[]{:S(2)}) collective-permute-start(f32[64,256]{1,0:T(8,128)S(1)} %shard_map.34), channel_id=1, source_target_pairs={{0,16},{4,20},{8,24},{12,28},{16,0},{20,4},{24,8},{28,12},{1,17},{... | collective-permute-start | bytes 196616 | tf_op jit(solution)/shard_map/ppermute | solution.py:64
  35.2 2.1 %collective-permute-done.10 = f32[64,256]{1,0:T(8,128)S(1)} collective-permute-done((f32[64,256]{1,0:T(8,128)S(1)}, f32[64,256]{1,0:T(8,128)S(1)}, u32[]{:S(2)}, u32[]{:S(2)}) %collective-permute-start.10) | collective-permute-done | bytes 65568 | tf_op jit(solution)/shard_map/ppermute | solution.py:64
  37.3 1.0 %collective-permute-done.9 = f32[64,256]{1,0:T(8,128)S(1)} collective-permute-done((f32[64,256]{1,0:T(8,128)S(1)}, f32[64,256]{1,0:T(8,128)S(1)}, u32[]{:S(2)}, u32[]{:S(2)}) %collective-permute-start.9) | collective-permute-done | bytes 65568 | tf_op jit(solution)/shard_map/ppermute | solution.py:64
  38.3 0.5 collective-permute-done.8
  38.9 3.7 %collective-permute-start.13 = (f32[64,256]{1,0:T(8,128)S(1)}, f32[64,256]{1,0:T(8,128)S(1)}, u32[]{:S(2)}, u32[]{:S(2)}) collective-permute-start(f32[64,256]{1,0:T(8,128)S(1)} %add_add_fusion.1), channel_id=1, source_target_pairs={{0,3},{1,2},{2,1},{3,0},{4,7},{5,6},{6,5},{7,4},{8,11},{9,10},{10,... | collective-permute-start | bytes 196616 | tf_op jit(solution)/shard_map/ppermute | solution.py:64
  42.5 0.8 %collective-permute-start.11 = (f32[64,256]{1,0:T(8,128)S(1)}, f32[64,256]{1,0:T(8,128)S(1)}, u32[]{:S(2)}, u32[]{:S(2)}) collective-permute-start(f32[64,256]{1,0:T(8,128)S(1)} %add_add_fusion.1), channel_id=1, source_target_pairs={{0,2},{1,3},{2,0},{3,1},{4,6},{5,7},{6,4},{7,5},{8,10},{9,11},{10,... | collective-permute-start | bytes 196616 | tf_op jit(solution)/shard_map/ppermute | solution.py:64
  43.3 1.8 %collective-permute-done.13 = f32[64,256]{1,0:T(8,128)S(1)} collective-permute-done((f32[64,256]{1,0:T(8,128)S(1)}, f32[64,256]{1,0:T(8,128)S(1)}, u32[]{:S(2)}, u32[]{:S(2)}) %collective-permute-start.13) | collective-permute-done | bytes 65568 | tf_op jit(solution)/shard_map/ppermute | solution.py:64
  45.1 1.7 %collective-permute-done.12 = f32[64,256]{1,0:T(8,128)S(1)} collective-permute-done((f32[64,256]{1,0:T(8,128)S(1)}, f32[64,256]{1,0:T(8,128)S(1)}, u32[]{:S(2)}, u32[]{:S(2)}) %collective-permute-start.12) | collective-permute-done | bytes 65568 | tf_op jit(solution)/shard_map/ppermute | solution.py:64
  46.8 0.9 %collective-permute-done.11 = f32[64,256]{1,0:T(8,128)S(1)} collective-permute-done((f32[64,256]{1,0:T(8,128)S(1)}, f32[64,256]{1,0:T(8,128)S(1)}, u32[]{:S(2)}, u32[]{:S(2)}) %collective-permute-start.11) | collective-permute-done | bytes 65568 | tf_op jit(solution)/shard_map/ppermute | solution.py:64
  48.5 0.6 collective-permute-start.15
  49.2 1.8 %shard_map.36.inverse_ref = f32[64,64]{1,0:T(8,128)S(1)} custom-call(f32[64,64]{1,0:T(8,128)S(1)} %shard_map.35.mine_ref.after, f32[64,64]{1,0:T(8,128)S(1)} %collective-permute-done.14.other_ref), custom_call_target="tpu_custom_call" | custom-call | flops 10000000000 | bytes 1000 | tf_op jit(solution)/shard_map/pallas_call | solution.py:251
  51.4 1.7 %collective-permute-start.16 = (f32[17,8,128]{2,1,0:T(8,128)S(1)}, f32[17,8,128]{2,1,0:T(8,128)S(1)}, u32[]{:S(2)}, u32[]{:S(2)}) collective-permute-start(f32[17,8,128]{2,1,0:T(8,128)S(1)} %get-tuple-element.39), channel_id=1, source_target_pairs={{0,24},{4,28},{8,16},{12,20},{16,8},{20,12},{24,0},{28,4},{1,25},{... | collective-permute-start | bytes 208904 | tf_op jit(solution)/shard_map/ppermute | solution.py:64
  53.1 0.6 %collective-permute-start.17 = (f32[17,8,128]{2,1,0:T(8,128)S(1)}, f32[17,8,128]{2,1,0:T(8,128)S(1)}, u32[]{:S(2)}, u32[]{:S(2)}) collective-permute-start(f32[17,8,128]{2,1,0:T(8,128)S(1)} %get-tuple-element.40), channel_id=1, source_target_pairs={{0,8},{4,12},{8,0},{12,4},{16,24},{20,28},{24,16},{28,20},{1,9},{5... | collective-permute-start | bytes 208904 | tf_op jit(solution)/shard_map/ppermute | solution.py:64
  53.7 1.2 %collective-permute-start.18 = (f32[17,8,128]{2,1,0:T(8,128)S(1)}, f32[17,8,128]{2,1,0:T(8,128)S(1)}, u32[]{:S(2)}, u32[]{:S(2)}) collective-permute-start(f32[17,8,128]{2,1,0:T(8,128)S(1)} %get-tuple-element.41), channel_id=1, source_target_pairs={{0,16},{4,20},{8,24},{12,28},{16,0},{20,4},{24,8},{28,12},{1,17},{... | collective-permute-start | bytes 208904 | tf_op jit(solution)/shard_map/ppermute | solution.py:64
  55.0 2.1 %collective-permute-done.16.refs_0_ = f32[17,8,128]{2,1,0:T(8,128)S(1)} collective-permute-done((f32[17,8,128]{2,1,0:T(8,128)S(1)}, f32[17,8,128]{2,1,0:T(8,128)S(1)}, u32[]{:S(2)}, u32[]{:S(2)}) %collective-permute-start.16) | collective-permute-done | bytes 69664 | tf_op jit(solution)/shard_map/ppermute | solution.py:64
  57.5 0.7 %collective-permute-done.18.refs_2_ = f32[17,8,128]{2,1,0:T(8,128)S(1)} collective-permute-done((f32[17,8,128]{2,1,0:T(8,128)S(1)}, f32[17,8,128]{2,1,0:T(8,128)S(1)}, u32[]{:S(2)}, u32[]{:S(2)}) %collective-permute-start.18) | collective-permute-done | bytes 69664 | tf_op jit(solution)/shard_map/ppermute | solution.py:64
  58.1 0.9 %shard_map.39 = f32[66,8,128]{2,1,0:T(8,128)} custom-call(s32[1]{0:T(128)} %bitcast.me_ref.after, f32[17,8,128]{2,1,0:T(8,128)S(1)} %collective-permute-done.16.refs_0_, f32[17,8,128]{2,1,0:T(8,128)S(1)} %collective-permute-done.17.refs_1_, f32[17,8,128]{2,1,0:T(8,128)S(1)} %collective-permute-done.18.refs_2_, f32[17,8,128]{2,1,0:T(8,128)S(1)} %get-tuple-element.42.refs_3_), custom_call_target="tpu_custom_call" | custom-call | tf_op jit(solution)/shard_map/pallas_call | solution.py:329
  (22 shorter events, 3.9 us)
Async XLA Ops:
  1.0 20.1 %copy-start = (f32[512,64]{0,1:T(8,128)S(1)}, f32[512,64]{0,1:T(8,128)}, u32[]{:S(2)}) copy-start(f32[512,64]{0,1:T(8,128)} %param.3) | copy-start | bytes 393220
  1.0 12.5 %collective-permute-start.4 = (f32[640,128]{1,0:T(8,128)S(1)}, f32[640,128]{1,0:T(8,128)S(1)}, u32[]{:S(2)}, u32[]{:S(2)}) collective-permute-start(f32[640,128]{1,0:T(8,128)S(1)} %shard_map.28.after), channel_id=1, source_target_pairs={{0,24},{4,28},{8,16},{12,20},{16,8},{20,12},{24,0},{28,4},{1,25},{... | collective-permute-start | bytes 983048 | tf_op jit(solution)/shard_map/ppermute | solution.py:64
  6.2 15.0 %collective-permute-start.5 = (f32[640,128]{1,0:T(8,128)S(1)}, f32[640,128]{1,0:T(8,128)S(1)}, u32[]{:S(2)}, u32[]{:S(2)}) collective-permute-start(f32[640,128]{1,0:T(8,128)S(1)} %get-tuple-element.32), channel_id=1, source_target_pairs={{0,8},{4,12},{8,0},{12,4},{16,24},{20,28},{24,16},{28,20},{1,9},{5... | collective-permute-start | bytes 983048 | tf_op jit(solution)/shard_map/ppermute | solution.py:64
  6.8 14.4 %collective-permute-start.6 = (f32[640,128]{1,0:T(8,128)S(1)}, f32[640,128]{1,0:T(8,128)S(1)}, u32[]{:S(2)}, u32[]{:S(2)}) collective-permute-start(f32[640,128]{1,0:T(8,128)S(1)} %get-tuple-element.33), channel_id=1, source_target_pairs={{0,16},{4,20},{8,24},{12,28},{16,0},{20,4},{24,8},{28,12},{1,17},{... | collective-permute-start | bytes 983048 | tf_op jit(solution)/shard_map/ppermute | solution.py:64
  8.2 17.0 %collective-permute-start = (f32[416,128]{1,0:T(8,128)S(1)}, f32[416,128]{1,0:T(8,128)S(1)}, u32[]{:S(2)}, u32[]{:S(2)}) collective-permute-start(f32[416,128]{1,0:T(8,128)S(1)} %get-tuple-element.25), channel_id=1, source_target_pairs={{0,24},{4,28},{8,16},{12,20},{16,8},{20,12},{24,0},{28,4},{1,25},{... | collective-permute-start | bytes 638984 | tf_op jit(solution)/shard_map/ppermute | solution.py:64
  11.1 18.1 %collective-permute-start.1 = (f32[416,128]{1,0:T(8,128)S(1)}, f32[416,128]{1,0:T(8,128)S(1)}, u32[]{:S(2)}, u32[]{:S(2)}) collective-permute-start(f32[416,128]{1,0:T(8,128)S(1)} %get-tuple-element.26), channel_id=1, source_target_pairs={{0,8},{4,12},{8,0},{12,4},{16,24},{20,28},{24,16},{28,20},{1,9},{5... | collective-permute-start | bytes 638984 | tf_op jit(solution)/shard_map/ppermute | solution.py:64
  13.6 15.6 %collective-permute-start.2 = (f32[416,128]{1,0:T(8,128)S(1)}, f32[416,128]{1,0:T(8,128)S(1)}, u32[]{:S(2)}, u32[]{:S(2)}) collective-permute-start(f32[416,128]{1,0:T(8,128)S(1)} %get-tuple-element.27), channel_id=1, source_target_pairs={{0,16},{4,20},{8,24},{12,28},{16,0},{20,4},{24,8},{28,12},{1,17},{... | collective-permute-start | bytes 638984 | tf_op jit(solution)/shard_map/ppermute | solution.py:64
  21.7 8.0 %collective-permute-start.7 = (f32[64,1280]{1,0:T(8,128)S(1)}, f32[64,1280]{1,0:T(8,128)S(1)}, u32[]{:S(2)}, u32[]{:S(2)}) collective-permute-start(f32[64,1280]{1,0:T(8,128)S(1)} %get-tuple-element.34.mine_ref), channel_id=1, source_target_pairs={{0,4},{4,0},{8,12},{12,8},{16,20},{20,16},{24,28},{28,24},{1,5},{5... | collective-permute-start | bytes 983048 | tf_op jit(solution)/shard_map/ppermute | solution.py:64
  29.6 1.6 %collective-permute-start.3 = (f32[64,896]{1,0:T(8,128)S(1)}, f32[64,896]{1,0:T(8,128)S(1)}, u32[]{:S(2)}, u32[]{:S(2)}) collective-permute-start(f32[64,896]{1,0:T(8,128)S(1)} %get-tuple-element.29.mine_ref), channel_id=1, source_target_pairs={{0,4},{4,0},{8,12},{12,8},{16,20},{20,16},{24,28},{28,24},{1,5},{5... | collective-permute-start | bytes 688136 | tf_op jit(solution)/shard_map/ppermute | solution.py:64
  31.7 5.6 %collective-permute-start.10 = (f32[64,256]{1,0:T(8,128)S(1)}, f32[64,256]{1,0:T(8,128)S(1)}, u32[]{:S(2)}, u32[]{:S(2)}) collective-permute-start(f32[64,256]{1,0:T(8,128)S(1)} %shard_map.34), channel_id=1, source_target_pairs={{0,24},{4,28},{8,16},{12,20},{16,8},{20,12},{24,0},{28,4},{1,25},{... | collective-permute-start | bytes 196616 | tf_op jit(solution)/shard_map/ppermute | solution.py:64
  34.0 4.3 %collective-permute-start.9 = (f32[64,256]{1,0:T(8,128)S(1)}, f32[64,256]{1,0:T(8,128)S(1)}, u32[]{:S(2)}, u32[]{:S(2)}) collective-permute-start(f32[64,256]{1,0:T(8,128)S(1)} %shard_map.34), channel_id=1, source_target_pairs={{0,8},{4,12},{8,0},{12,4},{16,24},{20,28},{24,16},{28,20},{1,9},{5... | collective-permute-start | bytes 196616 | tf_op jit(solution)/shard_map/ppermute | solution.py:64
  34.6 4.3 %collective-permute-start.8 = (f32[64,256]{1,0:T(8,128)S(1)}, f32[64,256]{1,0:T(8,128)S(1)}, u32[]{:S(2)}, u32[]{:S(2)}) collective-permute-start(f32[64,256]{1,0:T(8,128)S(1)} %shard_map.34), channel_id=1, source_target_pairs={{0,16},{4,20},{8,24},{12,28},{16,0},{20,4},{24,8},{28,12},{1,17},{... | collective-permute-start | bytes 196616 | tf_op jit(solution)/shard_map/ppermute | solution.py:64
  38.9 6.3 %collective-permute-start.13 = (f32[64,256]{1,0:T(8,128)S(1)}, f32[64,256]{1,0:T(8,128)S(1)}, u32[]{:S(2)}, u32[]{:S(2)}) collective-permute-start(f32[64,256]{1,0:T(8,128)S(1)} %add_add_fusion.1), channel_id=1, source_target_pairs={{0,3},{1,2},{2,1},{3,0},{4,7},{5,6},{6,5},{7,4},{8,11},{9,10},{10,... | collective-permute-start | bytes 196616 | tf_op jit(solution)/shard_map/ppermute | solution.py:64
  42.5 4.3 %collective-permute-start.12 = (f32[64,256]{1,0:T(8,128)S(1)}, f32[64,256]{1,0:T(8,128)S(1)}, u32[]{:S(2)}, u32[]{:S(2)}) collective-permute-start(f32[64,256]{1,0:T(8,128)S(1)} %add_add_fusion.1), channel_id=1, source_target_pairs={{0,1},{1,0},{2,3},{3,2},{4,5},{5,4},{6,7},{7,6},{8,9},{9,8},{10,11... | collective-permute-start | bytes 196616 | tf_op jit(solution)/shard_map/ppermute | solution.py:64
  42.5 5.2 %collective-permute-start.11 = (f32[64,256]{1,0:T(8,128)S(1)}, f32[64,256]{1,0:T(8,128)S(1)}, u32[]{:S(2)}, u32[]{:S(2)}) collective-permute-start(f32[64,256]{1,0:T(8,128)S(1)} %add_add_fusion.1), channel_id=1, source_target_pairs={{0,2},{1,3},{2,0},{3,1},{4,6},{5,7},{6,4},{7,5},{8,10},{9,11},{10,... | collective-permute-start | bytes 196616 | tf_op jit(solution)/shard_map/ppermute | solution.py:64
  47.9 1.3 %collective-permute-start.14 = (f32[64,64]{1,0:T(8,128)S(1)}, f32[64,64]{1,0:T(8,128)S(1)}, u32[]{:S(2)}, u32[]{:S(2)}) collective-permute-start(f32[64,64]{1,0:T(8,128)S(1)} %shard_map.35.mine_ref.after), channel_id=1, source_target_pairs={{0,4},{4,0},{8,12},{12,8},{16,20},{20,16},{24,28},{28,24},{1,5},{5... | collective-permute-start | bytes 49160 | tf_op jit(solution)/shard_map/ppermute | solution.py:64
  48.5 2.5 %collective-permute-start.15 = (f32[64,2176]{1,0:T(8,128)S(1)}, f32[64,2176]{1,0:T(8,128)S(1)}, u32[]{:S(2)}, u32[]{:S(2)}) collective-permute-start(f32[64,2176]{1,0:T(8,128)S(1)} %shard_map.37.mine_ref), channel_id=1, source_target_pairs={{0,4},{4,0},{8,12},{12,8},{16,20},{20,16},{24,28},{28,24},{1,5},{5... | collective-permute-start | bytes 1671176 | tf_op jit(solution)/shard_map/ppermute | solution.py:64
  51.4 5.7 %collective-permute-start.16 = (f32[17,8,128]{2,1,0:T(8,128)S(1)}, f32[17,8,128]{2,1,0:T(8,128)S(1)}, u32[]{:S(2)}, u32[]{:S(2)}) collective-permute-start(f32[17,8,128]{2,1,0:T(8,128)S(1)} %get-tuple-element.39), channel_id=1, source_target_pairs={{0,24},{4,28},{8,16},{12,20},{16,8},{20,12},{24,0},{28,4},{1,25},{... | collective-permute-start | bytes 208904 | tf_op jit(solution)/shard_map/ppermute | solution.py:64
  53.1 4.4 %collective-permute-start.17 = (f32[17,8,128]{2,1,0:T(8,128)S(1)}, f32[17,8,128]{2,1,0:T(8,128)S(1)}, u32[]{:S(2)}, u32[]{:S(2)}) collective-permute-start(f32[17,8,128]{2,1,0:T(8,128)S(1)} %get-tuple-element.40), channel_id=1, source_target_pairs={{0,8},{4,12},{8,0},{12,4},{16,24},{20,28},{24,16},{28,20},{1,9},{5... | collective-permute-start | bytes 208904 | tf_op jit(solution)/shard_map/ppermute | solution.py:64
  53.7 4.4 %collective-permute-start.18 = (f32[17,8,128]{2,1,0:T(8,128)S(1)}, f32[17,8,128]{2,1,0:T(8,128)S(1)}, u32[]{:S(2)}, u32[]{:S(2)}) collective-permute-start(f32[17,8,128]{2,1,0:T(8,128)S(1)} %get-tuple-element.41), channel_id=1, source_target_pairs={{0,16},{4,20},{8,24},{12,28},{16,0},{20,4},{24,8},{28,12},{1,17},{... | collective-permute-start | bytes 208904 | tf_op jit(solution)/shard_map/ppermute | solution.py:64

commit v8 on v7

--- a/solution.py
+++ b/solution.py
@@ -160,24 +160,26 @@
         yield s * ny, to * ny, (high_ref[s // 2, :, lanes], low_ref[s // 2, :, lanes])
 
 
-def raw_kernel(count, ny, chips, last, me_ref, mine_ref, other_ref, high_ref, low_ref, *refs):
+def raw_kernel(count, ny, chips, more, rest, last, me_ref, mine_ref, other_ref, high_ref, low_ref, *refs):
     refs, out_ref = refs[:-1], refs[-1]
-    total = refs[0][...] if last else jnp.zeros(out_ref.shape, F32)
+    total = refs[0][...] if more else jnp.zeros(out_ref.shape, F32)
     for at, to, slab in split_slabs(high_ref, low_ref, count, ny):
         total += dot_split(stack(mine_ref[:, at:to] + other_ref[:, at:to]), slab, NT)
+    if rest:
+        halves_of_rest = (refs[-2][...], refs[-1][...])
+        lanes = slice(count * ny, count * ny + halves_of_rest[0].shape[0])
+        total += dot_split(stack(mine_ref[:, lanes] + other_ref[:, lanes]), halves_of_rest, NN)
     if last:
-        rest = (refs[1][...], refs[2][...])
-        lanes = slice(count * ny, count * ny + rest[0].shape[0])
-        total += dot_split(stack(mine_ref[:, lanes] + other_ref[:, lanes]), rest, NN)
         total = reorder(total, lax.div(me_ref[0], 2), chips, 1)
     out_ref[...] = total
 
 
-def raw_part(mine, other, pairs, before, me, count, ny, chips):
-    last = before is not None
-    args = [me, mine, other, *pairs[:2]] + ([before, *pairs[2:]] if last else [])
-    return pl.pallas_call(
-        functools.partial(raw_kernel, count, ny, chips, last),
+def raw_part(mine, other, split, before, me, count, ny, chips, last):
+    pairs, rest = split[:2], split[2:]
+    more = [] if before is None else [before]
+    args = [me, mine, other, *pairs, *more, *rest]
+    return pl.pallas_call(
+        functools.partial(raw_kernel, count, ny, chips, bool(more), bool(rest), last),
         in_specs=[SMEM] + [VMEM] * (len(args) - 1),
         out_specs=VMEM,
         out_shape=jax.ShapeDtypeStruct((mine.shape[0], pairs[0].shape[1]), F32),
@@ -215,31 +217,42 @@
     row = lax.broadcasted_iota(jnp.int32, (rank, rank), 0)
     col = lax.broadcasted_iota(jnp.int32, (rank, rank), 1)
     table = jnp.concatenate([gram, jnp.where(row == col, 1.0, 0.0).astype(F32)], axis=1)
-    rows = [table[8 * b : 8 * b + 8] for b in range(rank // 8)]
+    count = rank // 8
+    rows = [table[8 * b : 8 * b + 8] for b in range(count)]
     wide = rows[0].shape
     sub = lax.broadcasted_iota(jnp.int32, wide, 0)
 
     def spread(value, k):
         return jnp.broadcast_to(value[k : k + 1], wide)
 
+    def panel(i, b):
+        return [jnp.broadcast_to(rows[i][:, 8 * b + k : 8 * b + k + 1], wide) for k in range(8)]
+
     inverse = []
-    for b in range(len(rows)):
-        columns = [
-            [jnp.broadcast_to(block[:, 8 * b + k : 8 * b + k + 1], wide) for k in range(8)] for block in rows[b:]
-        ]
+    head = panel(0, 0)
+    for b in range(count):
+        below = {i: panel(i, b) for i in range(b + 1, count)}
+        side, following = (panel(b, b + 1), panel(b + 1, b + 1)) if below else ([], [])
         pivots = jnp.ones(wide, F32)
         for k in range(8):
-            pivot = spread(columns[0][k], k)
+            pivot = spread(head[k], k)
             pivots = jnp.where(sub == k, pivot, pivots)
             scale = 1.0 / pivot
-            across = spread(rows[b], k)
-            ahead = [spread(columns[0][m], k) for m in range(k + 1, 8)]
-            for i, column in enumerate(columns):
-                factor = jnp.where(sub > k, column[k], 0.0) if i == 0 else column[k]
-                for m in range(k + 1, 8):
-                    column[m] = column[m] - (factor * ahead[m - k - 1]) * scale
-                rows[b + i] = rows[b + i] - (factor * across) * scale
+            factor = jnp.where(sub > k, head[k], 0.0)
+            ahead = [spread(column, k) for column in head[k + 1 :]]
+            head[k + 1 :] = [column - (factor * term) * scale for column, term in zip(head[k + 1 :], ahead)]
+            factor = factor * scale
+            across, beyond = spread(rows[b], k), [spread(column, k) for column in side]
+            rows[b] = rows[b] - factor * across
+            side = [column - factor * term for column, term in zip(side, beyond)]
+            for i, columns in below.items():
+                factor = columns[k] * scale
+                columns[k + 1 :] = [column - factor * term for column, term in zip(columns[k + 1 :], ahead)]
+                rows[i] = rows[i] - factor * across
+                if i == b + 1:
+                    following = [column - factor * term for column, term in zip(following, beyond)]
         inverse.append(rows[b][:, rank:] * lax.rsqrt(pivots[:, rank:]))
+        head = following
     return jnp.concatenate(inverse, axis=0)
 
 
@@ -341,27 +354,32 @@
     chips, each = n // 2, start_block.shape[1] // n
     total = species * planes
     own, left = divmod(total, chips)
-    counts = [own * 5 // 8, own - own * 5 // 8]
+    counts = [own * 3 // 8, own * 3 // 8]
+    counts.append(own - sum(counts))
     me = lax.axis_index("fib").astype(jnp.int32).reshape(1)
     rows = field_data.reshape(total * width, ny)
     start_t = start_block.T
-    bounds = [(0, counts[0], 0), (counts[0], own, left)]
+    bounds, first = [], 0
+    for c, count in enumerate(counts):
+        bounds.append((first, first + count, left if c == 1 else 0))
+        first += count
     near, far = [*range(1, chips - 1)], [chips - 1]
-    sent, after = [{}, {}], me
-    for c, ks in [(0, far), (0, [0, *near]), (1, [0, *near, *far])]:
+    sent, after = [{} for _ in counts], me
+    for c, ks in [(0, far), (0, [0, *near]), (1, [0, *near, *far]), (2, [0, *near, *far])]:
         got = pack(rows, me, after, ks, chips, *bounds[c][:2], own, bounds[c][2], width)
         sent[c].update(zip(ks, got))
         after = got[0]
-    pairs, raw = [], None
+    pairs, rests, raw = [], [], None
     for c, (first, last, rest) in enumerate(bounds):
         part = [sent[c][0]] + [exchange(sent[c][k], "fib", 2 * k, n) for k in range(1, chips)]
         mine, *split = project(part, start_t, me, last - first, rest, width)
         other = exchange(mine, "fib", 1, n)
-        raw = raw_part(mine, other, split, raw, me, last - first, ny, chips)
-        pairs += split
+        raw = raw_part(mine, other, split, raw, me, last - first, ny, chips, last == own)
+        pairs += split[:2]
+        rests += split[2:]
     raw = sum_over(sum_over(raw, "fib", 2, n), "blk", 1, layers)
     gram = gram_part(raw)
-    sums = mixed(raw, pairs, me, gram, counts, chips, ny)
+    sums = mixed(raw, pairs + rests, me, gram, counts, chips, ny)
     inverse = factor(gram, exchange(gram, "fib", 1, n))
     parts = core(inverse, sums, exchange(sums, "fib", 1, n), me, chips, each, ny)
     parts = [parts[0]] + [exchange(parts[k], "fib", 2 * k, n) for k in range(1, chips)]

time: 59.2 us -> 58.6 us (0.990)
  waiting for transfers between devices: 27.1 us -> 23.5 us
  starting transfers between devices: 22.5 us -> 24.5 us
  Pallas kernels: 9.25 us -> 10.2 us
    ppermute x19 -> x23, waiting for transfers between devices: 27.1 us -> 23.5 us  [exchange(): return lax.ppermute(value, axis, [(i, i ^ mask) for i in range(size)])]
    ppermute x19 -> x23, starting transfers between devices: 22.5 us -> 24.5 us  [exchange(): return lax.ppermute(value, axis, [(i, i ^ mask) for i in range(size)])]
    pallas_call x3 -> x4, Pallas kernels: 3.52 us -> 4.59 us  [pack(): pl.pallas_call(functools.partial(pack_kernel, ks, chips, first, last, own...]
  transfers between devices with their start and end apart: 19 -> 23, of which waited for: 15 -> 19; matrix products, arithmetic and copies ran while one was open for 0% -> 0% of each run, Pallas kernels for 11% -> 13%
where the time goes in v8:
time: 58.6 us; the launch traced here: 58.4 us
  starting transfers between devices  24.5 us (42%)
  waiting for transfers between devices  23.5 us (40%)
  Pallas kernels  10.2 us (17%)
    ppermute x23, starting transfers between devices, exchange(): return lax.ppermute(value, axis, [(i, i ^ mask) for i in range(size)])  24.5 us
    ppermute x23, waiting for transfers between devices, exchange(): return lax.ppermute(value, axis, [(i, i ^ mask) for i in range(size)])  23.5 us
    pallas_call x4, Pallas kernels, pack(): pl.pallas_call(functools.partial(pack_kernel, ks, chips, first, last, own...  4.59 us
    pallas_call x1, Pallas kernels, factor(): pl.pallas_call(factor_kernel, in_specs=[VMEM] * 2, out_specs=VMEM, out_sh...  1.41 us
  transfers between devices with their start and end apart: 23, of which 19 were waited for; matrix products, arithmetic and copies ran while one was open for 0% of the time, Pallas kernels for 13%

profile of v8, /device:TPU:0, one launch (start us, length us, event | category | flops | bytes accessed | tf_op | source)
XLA Modules:
  0.0 58.4 jit_solution(8082105817784980499)
XLA Ops:
  0.0 1.0 %shard_map.28.after = f32[384,128]{1,0:T(8,128)S(1)} custom-call(s32[1]{0:T(128)} %bitcast.me_ref.after, f32[4224,128]{1,0:T(8,128)} %bitcast.7, s32[1]{0:T(128)} %bitcast.me_ref.after), custom_call_target="tpu_custom_call" | custom-call | tf_op jit(solution)/shard_map/pallas_call | solution.py:97
  1.0 4.0 %collective-permute-start.8 = (f32[384,128]{1,0:T(8,128)S(1)}, f32[384,128]{1,0:T(8,128)S(1)}, u32[]{:S(2)}, u32[]{:S(2)}) collective-permute-start(f32[384,128]{1,0:T(8,128)S(1)} %shard_map.28.after), channel_id=1, source_target_pairs={{0,24},{4,28},{8,16},{12,20},{16,8},{20,12},{24,0},{28,4},{1,25},{... | collective-permute-start | bytes 589832 | tf_op jit(solution)/shard_map/ppermute | solution.py:64
  4.9 1.2 %shard_map.29 = (f32[384,128]{1,0:T(8,128)S(1)}, f32[384,128]{1,0:T(8,128)S(1)}, f32[384,128]{1,0:T(8,128)S(1)}) custom-call(s32[1]{0:T(128)} %bitcast.me_ref.after, f32[4224,128]{1,0:T(8,128)} %bitcast.8, f32[384,128]{1,0:T(8,128)S(1)} %shard_map.28.after), custom_call_target="tpu_custom_call" | custom-call | tf_op jit(solution)/shard_map/pallas_call | solution.py:97
  6.1 1.3 %shard_map.30 = (f32[416,128]{1,0:T(8,128)S(1)}, f32[416,128]{1,0:T(8,128)S(1)}, f32[416,128]{1,0:T(8,128)S(1)}, f32[416,128]{1,0:T(8,128)S(1)}) custom-call(s32[1]{0:T(128)} %bitcast.me_ref.after, f32[4224,128]{1,0:T(8,128)} %bitcast.9, f32[384,128]{1,0:T(8,128)S(1)} %get-tuple-element.31.after.refs_3_), custom_call_target="tpu_custom_call" | custom-call | tf_op jit(solution)/shard_map/pallas_call | solution.py:97
  7.5 1.9 %collective-permute-start.5 = (f32[416,128]{1,0:T(8,128)S(1)}, f32[416,128]{1,0:T(8,128)S(1)}, u32[]{:S(2)}, u32[]{:S(2)}) collective-permute-start(f32[416,128]{1,0:T(8,128)S(1)} %get-tuple-element.41), channel_id=1, source_target_pairs={{0,8},{4,12},{8,0},{12,4},{16,24},{20,28},{24,16},{28,20},{1,9},{5... | collective-permute-start | bytes 638984 | tf_op jit(solution)/shard_map/ppermute | solution.py:64
  9.5 1.5 %collective-permute-start.6 = (f32[416,128]{1,0:T(8,128)S(1)}, f32[416,128]{1,0:T(8,128)S(1)}, u32[]{:S(2)}, u32[]{:S(2)}) collective-permute-start(f32[416,128]{1,0:T(8,128)S(1)} %get-tuple-element.42), channel_id=1, source_target_pairs={{0,16},{4,20},{8,24},{12,28},{16,0},{20,4},{24,8},{28,12},{1,17},{... | collective-permute-start | bytes 638984 | tf_op jit(solution)/shard_map/ppermute | solution.py:64
  11.0 0.5 collective-permute-start.9
  12.0 1.1 %shard_map.31 = (f32[256,128]{1,0:T(8,128)S(1)}, f32[256,128]{1,0:T(8,128)S(1)}, f32[256,128]{1,0:T(8,128)S(1)}, f32[256,128]{1,0:T(8,128)S(1)}) custom-call(s32[1]{0:T(128)} %bitcast.me_ref.after, f32[4224,128]{1,0:T(8,128)} %bitcast.10, f32[416,128]{1,0:T(8,128)S(1)} %get-tuple-element.32.after.refs_3_), custom_call_target="tpu_custom_call" | custom-call | tf_op jit(solution)/shard_map/pallas_call | solution.py:97
  13.1 3.5 %collective-permute-done.4.refs_0_ = f32[416,128]{1,0:T(8,128)S(1)} collective-permute-done((f32[416,128]{1,0:T(8,128)S(1)}, f32[416,128]{1,0:T(8,128)S(1)}, u32[]{:S(2)}, u32[]{:S(2)}) %collective-permute-start.4) | collective-permute-done | bytes 213024 | tf_op jit(solution)/shard_map/ppermute | solution.py:64
  16.6 1.6 %collective-permute-start = (f32[256,128]{1,0:T(8,128)S(1)}, f32[256,128]{1,0:T(8,128)S(1)}, u32[]{:S(2)}, u32[]{:S(2)}) collective-permute-start(f32[256,128]{1,0:T(8,128)S(1)} %get-tuple-element.33), channel_id=1, source_target_pairs={{0,24},{4,28},{8,16},{12,20},{16,8},{20,12},{24,0},{28,4},{1,25},{... | collective-permute-start | bytes 393224 | tf_op jit(solution)/shard_map/ppermute | solution.py:64
  18.2 2.0 %collective-permute-done.5.refs_1_ = f32[416,128]{1,0:T(8,128)S(1)} collective-permute-done((f32[416,128]{1,0:T(8,128)S(1)}, f32[416,128]{1,0:T(8,128)S(1)}, u32[]{:S(2)}, u32[]{:S(2)}) %collective-permute-start.5) | collective-permute-done | bytes 213024 | tf_op jit(solution)/shard_map/ppermute | solution.py:64
  20.2 1.6 %collective-permute-start.1 = (f32[256,128]{1,0:T(8,128)S(1)}, f32[256,128]{1,0:T(8,128)S(1)}, u32[]{:S(2)}, u32[]{:S(2)}) collective-permute-start(f32[256,128]{1,0:T(8,128)S(1)} %get-tuple-element.34), channel_id=1, source_target_pairs={{0,8},{4,12},{8,0},{12,4},{16,24},{20,28},{24,16},{28,20},{1,9},{5... | collective-permute-start | bytes 393224 | tf_op jit(solution)/shard_map/ppermute | solution.py:64
  22.7 1.7 %collective-permute-done.9.refs_1_ = f32[384,128]{1,0:T(8,128)S(1)} collective-permute-done((f32[384,128]{1,0:T(8,128)S(1)}, f32[384,128]{1,0:T(8,128)S(1)}, u32[]{:S(2)}, u32[]{:S(2)}) %collective-permute-start.9) | collective-permute-done | bytes 196640 | tf_op jit(solution)/shard_map/ppermute | solution.py:64
  24.5 0.9 %collective-permute-done.10.refs_2_ = f32[384,128]{1,0:T(8,128)S(1)} collective-permute-done((f32[384,128]{1,0:T(8,128)S(1)}, f32[384,128]{1,0:T(8,128)S(1)}, u32[]{:S(2)}, u32[]{:S(2)}) %collective-permute-start.10) | collective-permute-done | bytes 196640 | tf_op jit(solution)/shard_map/ppermute | solution.py:64
  25.9 2.4 %collective-permute-done.refs_0_ = f32[256,128]{1,0:T(8,128)S(1)} collective-permute-done((f32[256,128]{1,0:T(8,128)S(1)}, f32[256,128]{1,0:T(8,128)S(1)}, u32[]{:S(2)}, u32[]{:S(2)}) %collective-permute-start) | collective-permute-done | bytes 131104 | tf_op jit(solution)/shard_map/ppermute | solution.py:64
  28.3 0.8 %collective-permute-done.1.refs_1_ = f32[256,128]{1,0:T(8,128)S(1)} collective-permute-done((f32[256,128]{1,0:T(8,128)S(1)}, f32[256,128]{1,0:T(8,128)S(1)}, u32[]{:S(2)}, u32[]{:S(2)}) %collective-permute-start.1) | collective-permute-done | bytes 131104 | tf_op jit(solution)/shard_map/ppermute | solution.py:64
  31.6 2.0 %collective-permute-start.14 = (f32[64,256]{1,0:T(8,128)S(1)}, f32[64,256]{1,0:T(8,128)S(1)}, u32[]{:S(2)}, u32[]{:S(2)}) collective-permute-start(f32[64,256]{1,0:T(8,128)S(1)} %shard_map.37), channel_id=1, source_target_pairs={{0,24},{4,28},{8,16},{12,20},{16,8},{20,12},{24,0},{28,4},{1,25},{... | collective-permute-start | bytes 196616 | tf_op jit(solution)/shard_map/ppermute | solution.py:64
  34.1 1.0 %collective-permute-start.12 = (f32[64,256]{1,0:T(8,128)S(1)}, f32[64,256]{1,0:T(8,128)S(1)}, u32[]{:S(2)}, u32[]{:S(2)}) collective-permute-start(f32[64,256]{1,0:T(8,128)S(1)} %shard_map.37), channel_id=1, source_target_pairs={{0,16},{4,20},{8,24},{12,28},{16,0},{20,4},{24,8},{28,12},{1,17},{... | collective-permute-start | bytes 196616 | tf_op jit(solution)/shard_map/ppermute | solution.py:64
  35.2 2.4 %collective-permute-done.14 = f32[64,256]{1,0:T(8,128)S(1)} collective-permute-done((f32[64,256]{1,0:T(8,128)S(1)}, f32[64,256]{1,0:T(8,128)S(1)}, u32[]{:S(2)}, u32[]{:S(2)}) %collective-permute-start.14) | collective-permute-done | bytes 65568 | tf_op jit(solution)/shard_map/ppermute | solution.py:64
  38.4 3.7 %collective-permute-start.17 = (f32[64,256]{1,0:T(8,128)S(1)}, f32[64,256]{1,0:T(8,128)S(1)}, u32[]{:S(2)}, u32[]{:S(2)}) collective-permute-start(f32[64,256]{1,0:T(8,128)S(1)} %add_add_fusion.1), channel_id=1, source_target_pairs={{0,3},{1,2},{2,1},{3,0},{4,7},{5,6},{6,5},{7,4},{8,11},{9,10},{10,... | collective-permute-start | bytes 196616 | tf_op jit(solution)/shard_map/ppermute | solution.py:64
  42.1 0.8 %collective-permute-start.15 = (f32[64,256]{1,0:T(8,128)S(1)}, f32[64,256]{1,0:T(8,128)S(1)}, u32[]{:S(2)}, u32[]{:S(2)}) collective-permute-start(f32[64,256]{1,0:T(8,128)S(1)} %add_add_fusion.1), channel_id=1, source_target_pairs={{0,2},{1,3},{2,0},{3,1},{4,6},{5,7},{6,4},{7,5},{8,10},{9,11},{10,... | collective-permute-start | bytes 196616 | tf_op jit(solution)/shard_map/ppermute | solution.py:64
  42.9 1.8 %collective-permute-done.17 = f32[64,256]{1,0:T(8,128)S(1)} collective-permute-done((f32[64,256]{1,0:T(8,128)S(1)}, f32[64,256]{1,0:T(8,128)S(1)}, u32[]{:S(2)}, u32[]{:S(2)}) %collective-permute-start.17) | collective-permute-done | bytes 65568 | tf_op jit(solution)/shard_map/ppermute | solution.py:64
  44.7 1.9 %collective-permute-done.16 = f32[64,256]{1,0:T(8,128)S(1)} collective-permute-done((f32[64,256]{1,0:T(8,128)S(1)}, f32[64,256]{1,0:T(8,128)S(1)}, u32[]{:S(2)}, u32[]{:S(2)}) %collective-permute-start.16) | collective-permute-done | bytes 65568 | tf_op jit(solution)/shard_map/ppermute | solution.py:64
  46.6 0.7 %collective-permute-done.15 = f32[64,256]{1,0:T(8,128)S(1)} collective-permute-done((f32[64,256]{1,0:T(8,128)S(1)}, f32[64,256]{1,0:T(8,128)S(1)}, u32[]{:S(2)}, u32[]{:S(2)}) %collective-permute-start.15) | collective-permute-done | bytes 65568 | tf_op jit(solution)/shard_map/ppermute | solution.py:64
  48.1 0.6 collective-permute-start.19
  48.8 1.4 %shard_map.39.inverse_ref = f32[64,64]{1,0:T(8,128)S(1)} custom-call(f32[64,64]{1,0:T(8,128)S(1)} %shard_map.38.mine_ref.after, f32[64,64]{1,0:T(8,128)S(1)} %collective-permute-done.18.other_ref), custom_call_target="tpu_custom_call" | custom-call | flops 10000000000 | bytes 1000 | tf_op jit(solution)/shard_map/pallas_call | solution.py:264
  50.6 1.7 %collective-permute-start.20 = (f32[17,8,128]{2,1,0:T(8,128)S(1)}, f32[17,8,128]{2,1,0:T(8,128)S(1)}, u32[]{:S(2)}, u32[]{:S(2)}) collective-permute-start(f32[17,8,128]{2,1,0:T(8,128)S(1)} %get-tuple-element.53), channel_id=1, source_target_pairs={{0,24},{4,28},{8,16},{12,20},{16,8},{20,12},{24,0},{28,4},{1,25},{... | collective-permute-start | bytes 208904 | tf_op jit(solution)/shard_map/ppermute | solution.py:64
  52.4 0.9 %collective-permute-start.21 = (f32[17,8,128]{2,1,0:T(8,128)S(1)}, f32[17,8,128]{2,1,0:T(8,128)S(1)}, u32[]{:S(2)}, u32[]{:S(2)}) collective-permute-start(f32[17,8,128]{2,1,0:T(8,128)S(1)} %get-tuple-element.54), channel_id=1, source_target_pairs={{0,8},{4,12},{8,0},{12,4},{16,24},{20,28},{24,16},{28,20},{1,9},{5... | collective-permute-start | bytes 208904 | tf_op jit(solution)/shard_map/ppermute | solution.py:64
  53.2 1.0 %collective-permute-start.22 = (f32[17,8,128]{2,1,0:T(8,128)S(1)}, f32[17,8,128]{2,1,0:T(8,128)S(1)}, u32[]{:S(2)}, u32[]{:S(2)}) collective-permute-start(f32[17,8,128]{2,1,0:T(8,128)S(1)} %get-tuple-element.55), channel_id=1, source_target_pairs={{0,16},{4,20},{8,24},{12,28},{16,0},{20,4},{24,8},{28,12},{1,17},{... | collective-permute-start | bytes 208904 | tf_op jit(solution)/shard_map/ppermute | solution.py:64
  54.2 2.2 %collective-permute-done.20.refs_0_ = f32[17,8,128]{2,1,0:T(8,128)S(1)} collective-permute-done((f32[17,8,128]{2,1,0:T(8,128)S(1)}, f32[17,8,128]{2,1,0:T(8,128)S(1)}, u32[]{:S(2)}, u32[]{:S(2)}) %collective-permute-start.20) | collective-permute-done | bytes 69664 | tf_op jit(solution)/shard_map/ppermute | solution.py:64
  56.4 0.7 %collective-permute-done.21.refs_1_ = f32[17,8,128]{2,1,0:T(8,128)S(1)} collective-permute-done((f32[17,8,128]{2,1,0:T(8,128)S(1)}, f32[17,8,128]{2,1,0:T(8,128)S(1)}, u32[]{:S(2)}, u32[]{:S(2)}) %collective-permute-start.21) | collective-permute-done | bytes 69664 | tf_op jit(solution)/shard_map/ppermute | solution.py:64
  57.5 0.9 %shard_map.42 = f32[66,8,128]{2,1,0:T(8,128)} custom-call(s32[1]{0:T(128)} %bitcast.me_ref.after, f32[17,8,128]{2,1,0:T(8,128)S(1)} %collective-permute-done.20.refs_0_, f32[17,8,128]{2,1,0:T(8,128)S(1)} %collective-permute-done.21.refs_1_, f32[17,8,128]{2,1,0:T(8,128)S(1)} %collective-permute-done.22.refs_2_, f32[17,8,128]{2,1,0:T(8,128)S(1)} %get-tuple-element.56.refs_3_), custom_call_target="tpu_custom_call" | custom-call | tf_op jit(solution)/shard_map/pallas_call | solution.py:342
  (33 shorter events, 7.4 us)
Async XLA Ops:
  1.0 10.6 %collective-permute-start.8 = (f32[384,128]{1,0:T(8,128)S(1)}, f32[384,128]{1,0:T(8,128)S(1)}, u32[]{:S(2)}, u32[]{:S(2)}) collective-permute-start(f32[384,128]{1,0:T(8,128)S(1)} %shard_map.28.after), channel_id=1, source_target_pairs={{0,24},{4,28},{8,16},{12,20},{16,8},{20,12},{24,0},{28,4},{1,25},{... | collective-permute-start | bytes 589832 | tf_op jit(solution)/shard_map/ppermute | solution.py:64
  6.1 16.2 %copy-start = (f32[512,64]{0,1:T(8,128)S(1)}, f32[512,64]{0,1:T(8,128)}, u32[]{:S(2)}) copy-start(f32[512,64]{0,1:T(8,128)} %param.3) | copy-start | bytes 393220
  7.5 9.2 %collective-permute-start.4 = (f32[416,128]{1,0:T(8,128)S(1)}, f32[416,128]{1,0:T(8,128)S(1)}, u32[]{:S(2)}, u32[]{:S(2)}) collective-permute-start(f32[416,128]{1,0:T(8,128)S(1)} %get-tuple-element.40), channel_id=1, source_target_pairs={{0,24},{4,28},{8,16},{12,20},{16,8},{20,12},{24,0},{28,4},{1,25},{... | collective-permute-start | bytes 638984 | tf_op jit(solution)/shard_map/ppermute | solution.py:64
  7.5 12.7 %collective-permute-start.5 = (f32[416,128]{1,0:T(8,128)S(1)}, f32[416,128]{1,0:T(8,128)S(1)}, u32[]{:S(2)}, u32[]{:S(2)}) collective-permute-start(f32[416,128]{1,0:T(8,128)S(1)} %get-tuple-element.41), channel_id=1, source_target_pairs={{0,8},{4,12},{8,0},{12,4},{16,24},{20,28},{24,16},{28,20},{1,9},{5... | collective-permute-start | bytes 638984 | tf_op jit(solution)/shard_map/ppermute | solution.py:64
  9.5 12.4 %collective-permute-start.6 = (f32[416,128]{1,0:T(8,128)S(1)}, f32[416,128]{1,0:T(8,128)S(1)}, u32[]{:S(2)}, u32[]{:S(2)}) collective-permute-start(f32[416,128]{1,0:T(8,128)S(1)} %get-tuple-element.42), channel_id=1, source_target_pairs={{0,16},{4,20},{8,24},{12,28},{16,0},{20,4},{24,8},{28,12},{1,17},{... | collective-permute-start | bytes 638984 | tf_op jit(solution)/shard_map/ppermute | solution.py:64
  11.0 13.5 %collective-permute-start.9 = (f32[384,128]{1,0:T(8,128)S(1)}, f32[384,128]{1,0:T(8,128)S(1)}, u32[]{:S(2)}, u32[]{:S(2)}) collective-permute-start(f32[384,128]{1,0:T(8,128)S(1)} %get-tuple-element.46), channel_id=1, source_target_pairs={{0,8},{4,12},{8,0},{12,4},{16,24},{20,28},{24,16},{28,20},{1,9},{5... | collective-permute-start | bytes 589832 | tf_op jit(solution)/shard_map/ppermute | solution.py:64
  11.5 13.9 %collective-permute-start.10 = (f32[384,128]{1,0:T(8,128)S(1)}, f32[384,128]{1,0:T(8,128)S(1)}, u32[]{:S(2)}, u32[]{:S(2)}) collective-permute-start(f32[384,128]{1,0:T(8,128)S(1)} %get-tuple-element.47), channel_id=1, source_target_pairs={{0,16},{4,20},{8,24},{12,28},{16,0},{20,4},{24,8},{28,12},{1,17},{... | collective-permute-start | bytes 589832 | tf_op jit(solution)/shard_map/ppermute | solution.py:64
  16.6 11.6 %collective-permute-start = (f32[256,128]{1,0:T(8,128)S(1)}, f32[256,128]{1,0:T(8,128)S(1)}, u32[]{:S(2)}, u32[]{:S(2)}) collective-permute-start(f32[256,128]{1,0:T(8,128)S(1)} %get-tuple-element.33), channel_id=1, source_target_pairs={{0,24},{4,28},{8,16},{12,20},{16,8},{20,12},{24,0},{28,4},{1,25},{... | collective-permute-start | bytes 393224 | tf_op jit(solution)/shard_map/ppermute | solution.py:64
  20.2 8.8 %collective-permute-start.1 = (f32[256,128]{1,0:T(8,128)S(1)}, f32[256,128]{1,0:T(8,128)S(1)}, u32[]{:S(2)}, u32[]{:S(2)}) collective-permute-start(f32[256,128]{1,0:T(8,128)S(1)} %get-tuple-element.34), channel_id=1, source_target_pairs={{0,8},{4,12},{8,0},{12,4},{16,24},{20,28},{24,16},{28,20},{1,9},{5... | collective-permute-start | bytes 393224 | tf_op jit(solution)/shard_map/ppermute | solution.py:64
  21.9 7.6 %collective-permute-start.2 = (f32[256,128]{1,0:T(8,128)S(1)}, f32[256,128]{1,0:T(8,128)S(1)}, u32[]{:S(2)}, u32[]{:S(2)}) collective-permute-start(f32[256,128]{1,0:T(8,128)S(1)} %get-tuple-element.35), channel_id=1, source_target_pairs={{0,16},{4,20},{8,24},{12,28},{16,0},{20,4},{24,8},{28,12},{1,17},{... | collective-permute-start | bytes 393224 | tf_op jit(solution)/shard_map/ppermute | solution.py:64
  24.5 5.9 %collective-permute-start.7 = (f32[64,896]{1,0:T(8,128)S(1)}, f32[64,896]{1,0:T(8,128)S(1)}, u32[]{:S(2)}, u32[]{:S(2)}) collective-permute-start(f32[64,896]{1,0:T(8,128)S(1)} %get-tuple-element.43.mine_ref), channel_id=1, source_target_pairs={{0,4},{4,0},{8,12},{12,8},{16,20},{20,16},{24,28},{28,24},{1,5},{5... | collective-permute-start | bytes 688136 | tf_op jit(solution)/shard_map/ppermute | solution.py:64
  25.8 4.1 %collective-permute-start.11 = (f32[64,768]{1,0:T(8,128)S(1)}, f32[64,768]{1,0:T(8,128)S(1)}, u32[]{:S(2)}, u32[]{:S(2)}) collective-permute-start(f32[64,768]{1,0:T(8,128)S(1)} %get-tuple-element.48.mine_ref), channel_id=1, source_target_pairs={{0,4},{4,0},{8,12},{12,8},{16,20},{20,16},{24,28},{28,24},{1,5},{5... | collective-permute-start | bytes 589832 | tf_op jit(solution)/shard_map/ppermute | solution.py:64
  29.9 1.4 %collective-permute-start.3 = (f32[64,512]{1,0:T(8,128)S(1)}, f32[64,512]{1,0:T(8,128)S(1)}, u32[]{:S(2)}, u32[]{:S(2)}) collective-permute-start(f32[64,512]{1,0:T(8,128)S(1)} %get-tuple-element.37.mine_ref), channel_id=1, source_target_pairs={{0,4},{4,0},{8,12},{12,8},{16,20},{20,16},{24,28},{28,24},{1,5},{5... | collective-permute-start | bytes 393224 | tf_op jit(solution)/shard_map/ppermute | solution.py:64
  31.6 6.0 %collective-permute-start.14 = (f32[64,256]{1,0:T(8,128)S(1)}, f32[64,256]{1,0:T(8,128)S(1)}, u32[]{:S(2)}, u32[]{:S(2)}) collective-permute-start(f32[64,256]{1,0:T(8,128)S(1)} %shard_map.37), channel_id=1, source_target_pairs={{0,24},{4,28},{8,16},{12,20},{16,8},{20,12},{24,0},{28,4},{1,25},{... | collective-permute-start | bytes 196616 | tf_op jit(solution)/shard_map/ppermute | solution.py:64
  33.6 4.3 %collective-permute-start.13 = (f32[64,256]{1,0:T(8,128)S(1)}, f32[64,256]{1,0:T(8,128)S(1)}, u32[]{:S(2)}, u32[]{:S(2)}) collective-permute-start(f32[64,256]{1,0:T(8,128)S(1)} %shard_map.37), channel_id=1, source_target_pairs={{0,8},{4,12},{8,0},{12,4},{16,24},{20,28},{24,16},{28,20},{1,9},{5... | collective-permute-start | bytes 196616 | tf_op jit(solution)/shard_map/ppermute | solution.py:64
  34.1 4.3 %collective-permute-start.12 = (f32[64,256]{1,0:T(8,128)S(1)}, f32[64,256]{1,0:T(8,128)S(1)}, u32[]{:S(2)}, u32[]{:S(2)}) collective-permute-start(f32[64,256]{1,0:T(8,128)S(1)} %shard_map.37), channel_id=1, source_target_pairs={{0,16},{4,20},{8,24},{12,28},{16,0},{20,4},{24,8},{28,12},{1,17},{... | collective-permute-start | bytes 196616 | tf_op jit(solution)/shard_map/ppermute | solution.py:64
  38.4 6.2 %collective-permute-start.17 = (f32[64,256]{1,0:T(8,128)S(1)}, f32[64,256]{1,0:T(8,128)S(1)}, u32[]{:S(2)}, u32[]{:S(2)}) collective-permute-start(f32[64,256]{1,0:T(8,128)S(1)} %add_add_fusion.1), channel_id=1, source_target_pairs={{0,3},{1,2},{2,1},{3,0},{4,7},{5,6},{6,5},{7,4},{8,11},{9,10},{10,... | collective-permute-start | bytes 196616 | tf_op jit(solution)/shard_map/ppermute | solution.py:64
  42.1 4.5 %collective-permute-start.16 = (f32[64,256]{1,0:T(8,128)S(1)}, f32[64,256]{1,0:T(8,128)S(1)}, u32[]{:S(2)}, u32[]{:S(2)}) collective-permute-start(f32[64,256]{1,0:T(8,128)S(1)} %add_add_fusion.1), channel_id=1, source_target_pairs={{0,1},{1,0},{2,3},{3,2},{4,5},{5,4},{6,7},{7,6},{8,9},{9,8},{10,11... | collective-permute-start | bytes 196616 | tf_op jit(solution)/shard_map/ppermute | solution.py:64
  42.1 5.2 %collective-permute-start.15 = (f32[64,256]{1,0:T(8,128)S(1)}, f32[64,256]{1,0:T(8,128)S(1)}, u32[]{:S(2)}, u32[]{:S(2)}) collective-permute-start(f32[64,256]{1,0:T(8,128)S(1)} %add_add_fusion.1), channel_id=1, source_target_pairs={{0,2},{1,3},{2,0},{3,1},{4,6},{5,7},{6,4},{7,5},{8,10},{9,11},{10,... | collective-permute-start | bytes 196616 | tf_op jit(solution)/shard_map/ppermute | solution.py:64
  47.5 1.3 %collective-permute-start.18 = (f32[64,64]{1,0:T(8,128)S(1)}, f32[64,64]{1,0:T(8,128)S(1)}, u32[]{:S(2)}, u32[]{:S(2)}) collective-permute-start(f32[64,64]{1,0:T(8,128)S(1)} %shard_map.38.mine_ref.after), channel_id=1, source_target_pairs={{0,4},{4,0},{8,12},{12,8},{16,20},{20,16},{24,28},{28,24},{1,5},{5... | collective-permute-start | bytes 49160 | tf_op jit(solution)/shard_map/ppermute | solution.py:64
  48.1 2.1 %collective-permute-start.19 = (f32[64,2176]{1,0:T(8,128)S(1)}, f32[64,2176]{1,0:T(8,128)S(1)}, u32[]{:S(2)}, u32[]{:S(2)}) collective-permute-start(f32[64,2176]{1,0:T(8,128)S(1)} %shard_map.40.mine_ref), channel_id=1, source_target_pairs={{0,4},{4,0},{8,12},{12,8},{16,20},{20,16},{24,28},{28,24},{1,5},{5... | collective-permute-start | bytes 1671176 | tf_op jit(solution)/shard_map/ppermute | solution.py:64
  50.6 5.8 %collective-permute-start.20 = (f32[17,8,128]{2,1,0:T(8,128)S(1)}, f32[17,8,128]{2,1,0:T(8,128)S(1)}, u32[]{:S(2)}, u32[]{:S(2)}) collective-permute-start(f32[17,8,128]{2,1,0:T(8,128)S(1)} %get-tuple-element.53), channel_id=1, source_target_pairs={{0,24},{4,28},{8,16},{12,20},{16,8},{20,12},{24,0},{28,4},{1,25},{... | collective-permute-start | bytes 208904 | tf_op jit(solution)/shard_map/ppermute | solution.py:64
  52.4 4.8 %collective-permute-start.21 = (f32[17,8,128]{2,1,0:T(8,128)S(1)}, f32[17,8,128]{2,1,0:T(8,128)S(1)}, u32[]{:S(2)}, u32[]{:S(2)}) collective-permute-start(f32[17,8,128]{2,1,0:T(8,128)S(1)} %get-tuple-element.54), channel_id=1, source_target_pairs={{0,8},{4,12},{8,0},{12,4},{16,24},{20,28},{24,16},{28,20},{1,9},{5... | collective-permute-start | bytes 208904 | tf_op jit(solution)/shard_map/ppermute | solution.py:64
  53.2 4.3 %collective-permute-start.22 = (f32[17,8,128]{2,1,0:T(8,128)S(1)}, f32[17,8,128]{2,1,0:T(8,128)S(1)}, u32[]{:S(2)}, u32[]{:S(2)}) collective-permute-start(f32[17,8,128]{2,1,0:T(8,128)S(1)} %get-tuple-element.55), channel_id=1, source_target_pairs={{0,16},{4,20},{8,24},{12,28},{16,0},{20,4},{24,8},{28,12},{1,17},{... | collective-permute-start | bytes 208904 | tf_op jit(solution)/shard_map/ppermute | solution.py:64

commit v9 on v8

--- a/solution.py
+++ b/solution.py
@@ -296,11 +296,11 @@
 def core_kernel(chips, me_ref, inverse_ref, mine_ref, other_ref, *outs):
     slabs, each, ny = outs[0].shape
     inverse = reorder(inverse_ref[...], me_ref[0], 2 * chips, 0)
-    inverse = jnp.concatenate([inverse[2 * k * each : (2 * k + 1) * each] for k in range(chips)], axis=0)
+    inverse = stack(jnp.concatenate([inverse[2 * k * each : (2 * k + 1) * each] for k in range(chips)], axis=0))
     for s in range(0, slabs, 2):
         to = min(s + 2, slabs)
         both = mine_ref[:, s * ny : to * ny] + other_ref[:, s * ny : to * ny]
-        value = lax.dot_general(inverse, both, NN, precision=HIGHEST, preferred_element_type=F32)
+        value = dot_split(inverse, halves(both), NN)
         for k in range(chips):
             for slab in range(s, to):
                 lanes = slice((slab - s) * ny, (slab - s + 1) * ny)

time: 58.6 us -> 58.5 us (level)
  no operation moved by 1% of the time
where the time goes in v9:
time: 58.5 us; the launch traced here: 58.3 us
  starting transfers between devices  24.5 us (42%)
  waiting for transfers between devices  23.5 us (40%)
  Pallas kernels  10.1 us (17%)
    ppermute x23, starting transfers between devices, exchange(): return lax.ppermute(value, axis, [(i, i ^ mask) for i in range(size)])  24.5 us
    ppermute x23, waiting for transfers between devices, exchange(): return lax.ppermute(value, axis, [(i, i ^ mask) for i in range(size)])  23.5 us
    pallas_call x4, Pallas kernels, pack(): pl.pallas_call(functools.partial(pack_kernel, ks, chips, first, last, own...  4.59 us
    pallas_call x1, Pallas kernels, factor(): pl.pallas_call(factor_kernel, in_specs=[VMEM] * 2, out_specs=VMEM, out_sh...  1.41 us
  transfers between devices with their start and end apart: 23, of which 19 were waited for; matrix products, arithmetic and copies ran while one was open for 0% of the time, Pallas kernels for 13%

profile of v9, /device:TPU:0, one launch (start us, length us, event | category | flops | bytes accessed | tf_op | source)
XLA Modules:
  0.0 58.3 jit_solution(13568187744040295573)
XLA Ops:
  0.0 1.0 %shard_map.28.after = f32[384,128]{1,0:T(8,128)S(1)} custom-call(s32[1]{0:T(128)} %bitcast.me_ref.after, f32[4224,128]{1,0:T(8,128)} %bitcast.7, s32[1]{0:T(128)} %bitcast.me_ref.after), custom_call_target="tpu_custom_call" | custom-call | tf_op jit(solution)/shard_map/pallas_call | solution.py:97
  1.0 4.0 %collective-permute-start.8 = (f32[384,128]{1,0:T(8,128)S(1)}, f32[384,128]{1,0:T(8,128)S(1)}, u32[]{:S(2)}, u32[]{:S(2)}) collective-permute-start(f32[384,128]{1,0:T(8,128)S(1)} %shard_map.28.after), channel_id=1, source_target_pairs={{0,24},{4,28},{8,16},{12,20},{16,8},{20,12},{24,0},{28,4},{1,25},{... | collective-permute-start | bytes 589832 | tf_op jit(solution)/shard_map/ppermute | solution.py:64
  4.9 1.2 %shard_map.29 = (f32[384,128]{1,0:T(8,128)S(1)}, f32[384,128]{1,0:T(8,128)S(1)}, f32[384,128]{1,0:T(8,128)S(1)}) custom-call(s32[1]{0:T(128)} %bitcast.me_ref.after, f32[4224,128]{1,0:T(8,128)} %bitcast.8, f32[384,128]{1,0:T(8,128)S(1)} %shard_map.28.after), custom_call_target="tpu_custom_call" | custom-call | tf_op jit(solution)/shard_map/pallas_call | solution.py:97
  6.1 1.3 %shard_map.30 = (f32[416,128]{1,0:T(8,128)S(1)}, f32[416,128]{1,0:T(8,128)S(1)}, f32[416,128]{1,0:T(8,128)S(1)}, f32[416,128]{1,0:T(8,128)S(1)}) custom-call(s32[1]{0:T(128)} %bitcast.me_ref.after, f32[4224,128]{1,0:T(8,128)} %bitcast.9, f32[384,128]{1,0:T(8,128)S(1)} %get-tuple-element.31.after.refs_3_), custom_call_target="tpu_custom_call" | custom-call | tf_op jit(solution)/shard_map/pallas_call | solution.py:97
  7.5 1.9 %collective-permute-start.5 = (f32[416,128]{1,0:T(8,128)S(1)}, f32[416,128]{1,0:T(8,128)S(1)}, u32[]{:S(2)}, u32[]{:S(2)}) collective-permute-start(f32[416,128]{1,0:T(8,128)S(1)} %get-tuple-element.41), channel_id=1, source_target_pairs={{0,8},{4,12},{8,0},{12,4},{16,24},{20,28},{24,16},{28,20},{1,9},{5... | collective-permute-start | bytes 638984 | tf_op jit(solution)/shard_map/ppermute | solution.py:64
  9.5 1.5 %collective-permute-start.6 = (f32[416,128]{1,0:T(8,128)S(1)}, f32[416,128]{1,0:T(8,128)S(1)}, u32[]{:S(2)}, u32[]{:S(2)}) collective-permute-start(f32[416,128]{1,0:T(8,128)S(1)} %get-tuple-element.42), channel_id=1, source_target_pairs={{0,16},{4,20},{8,24},{12,28},{16,0},{20,4},{24,8},{28,12},{1,17},{... | collective-permute-start | bytes 638984 | tf_op jit(solution)/shard_map/ppermute | solution.py:64
  11.0 0.5 collective-permute-start.9
  12.0 1.1 %shard_map.31 = (f32[256,128]{1,0:T(8,128)S(1)}, f32[256,128]{1,0:T(8,128)S(1)}, f32[256,128]{1,0:T(8,128)S(1)}, f32[256,128]{1,0:T(8,128)S(1)}) custom-call(s32[1]{0:T(128)} %bitcast.me_ref.after, f32[4224,128]{1,0:T(8,128)} %bitcast.10, f32[416,128]{1,0:T(8,128)S(1)} %get-tuple-element.32.after.refs_3_), custom_call_target="tpu_custom_call" | custom-call | tf_op jit(solution)/shard_map/pallas_call | solution.py:97
  13.1 3.5 %collective-permute-done.4.refs_0_ = f32[416,128]{1,0:T(8,128)S(1)} collective-permute-done((f32[416,128]{1,0:T(8,128)S(1)}, f32[416,128]{1,0:T(8,128)S(1)}, u32[]{:S(2)}, u32[]{:S(2)}) %collective-permute-start.4) | collective-permute-done | bytes 213024 | tf_op jit(solution)/shard_map/ppermute | solution.py:64
  16.6 1.6 %collective-permute-start = (f32[256,128]{1,0:T(8,128)S(1)}, f32[256,128]{1,0:T(8,128)S(1)}, u32[]{:S(2)}, u32[]{:S(2)}) collective-permute-start(f32[256,128]{1,0:T(8,128)S(1)} %get-tuple-element.33), channel_id=1, source_target_pairs={{0,24},{4,28},{8,16},{12,20},{16,8},{20,12},{24,0},{28,4},{1,25},{... | collective-permute-start | bytes 393224 | tf_op jit(solution)/shard_map/ppermute | solution.py:64
  18.2 2.0 %collective-permute-done.5.refs_1_ = f32[416,128]{1,0:T(8,128)S(1)} collective-permute-done((f32[416,128]{1,0:T(8,128)S(1)}, f32[416,128]{1,0:T(8,128)S(1)}, u32[]{:S(2)}, u32[]{:S(2)}) %collective-permute-start.5) | collective-permute-done | bytes 213024 | tf_op jit(solution)/shard_map/ppermute | solution.py:64
  20.2 1.6 %collective-permute-start.1 = (f32[256,128]{1,0:T(8,128)S(1)}, f32[256,128]{1,0:T(8,128)S(1)}, u32[]{:S(2)}, u32[]{:S(2)}) collective-permute-start(f32[256,128]{1,0:T(8,128)S(1)} %get-tuple-element.34), channel_id=1, source_target_pairs={{0,8},{4,12},{8,0},{12,4},{16,24},{20,28},{24,16},{28,20},{1,9},{5... | collective-permute-start | bytes 393224 | tf_op jit(solution)/shard_map/ppermute | solution.py:64
  22.7 1.7 %collective-permute-done.9.refs_1_ = f32[384,128]{1,0:T(8,128)S(1)} collective-permute-done((f32[384,128]{1,0:T(8,128)S(1)}, f32[384,128]{1,0:T(8,128)S(1)}, u32[]{:S(2)}, u32[]{:S(2)}) %collective-permute-start.9) | collective-permute-done | bytes 196640 | tf_op jit(solution)/shard_map/ppermute | solution.py:64
  24.5 0.9 %collective-permute-done.10.refs_2_ = f32[384,128]{1,0:T(8,128)S(1)} collective-permute-done((f32[384,128]{1,0:T(8,128)S(1)}, f32[384,128]{1,0:T(8,128)S(1)}, u32[]{:S(2)}, u32[]{:S(2)}) %collective-permute-start.10) | collective-permute-done | bytes 196640 | tf_op jit(solution)/shard_map/ppermute | solution.py:64
  25.9 2.4 %collective-permute-done.refs_0_ = f32[256,128]{1,0:T(8,128)S(1)} collective-permute-done((f32[256,128]{1,0:T(8,128)S(1)}, f32[256,128]{1,0:T(8,128)S(1)}, u32[]{:S(2)}, u32[]{:S(2)}) %collective-permute-start) | collective-permute-done | bytes 131104 | tf_op jit(solution)/shard_map/ppermute | solution.py:64
  28.3 0.8 %collective-permute-done.1.refs_1_ = f32[256,128]{1,0:T(8,128)S(1)} collective-permute-done((f32[256,128]{1,0:T(8,128)S(1)}, f32[256,128]{1,0:T(8,128)S(1)}, u32[]{:S(2)}, u32[]{:S(2)}) %collective-permute-start.1) | collective-permute-done | bytes 131104 | tf_op jit(solution)/shard_map/ppermute | solution.py:64
  31.6 2.0 %collective-permute-start.14 = (f32[64,256]{1,0:T(8,128)S(1)}, f32[64,256]{1,0:T(8,128)S(1)}, u32[]{:S(2)}, u32[]{:S(2)}) collective-permute-start(f32[64,256]{1,0:T(8,128)S(1)} %shard_map.37), channel_id=1, source_target_pairs={{0,24},{4,28},{8,16},{12,20},{16,8},{20,12},{24,0},{28,4},{1,25},{... | collective-permute-start | bytes 196616 | tf_op jit(solution)/shard_map/ppermute | solution.py:64
  34.1 1.0 %collective-permute-start.12 = (f32[64,256]{1,0:T(8,128)S(1)}, f32[64,256]{1,0:T(8,128)S(1)}, u32[]{:S(2)}, u32[]{:S(2)}) collective-permute-start(f32[64,256]{1,0:T(8,128)S(1)} %shard_map.37), channel_id=1, source_target_pairs={{0,16},{4,20},{8,24},{12,28},{16,0},{20,4},{24,8},{28,12},{1,17},{... | collective-permute-start | bytes 196616 | tf_op jit(solution)/shard_map/ppermute | solution.py:64
  35.2 2.4 %collective-permute-done.14 = f32[64,256]{1,0:T(8,128)S(1)} collective-permute-done((f32[64,256]{1,0:T(8,128)S(1)}, f32[64,256]{1,0:T(8,128)S(1)}, u32[]{:S(2)}, u32[]{:S(2)}) %collective-permute-start.14) | collective-permute-done | bytes 65568 | tf_op jit(solution)/shard_map/ppermute | solution.py:64
  38.4 3.7 %collective-permute-start.17 = (f32[64,256]{1,0:T(8,128)S(1)}, f32[64,256]{1,0:T(8,128)S(1)}, u32[]{:S(2)}, u32[]{:S(2)}) collective-permute-start(f32[64,256]{1,0:T(8,128)S(1)} %add_add_fusion.1), channel_id=1, source_target_pairs={{0,3},{1,2},{2,1},{3,0},{4,7},{5,6},{6,5},{7,4},{8,11},{9,10},{10,... | collective-permute-start | bytes 196616 | tf_op jit(solution)/shard_map/ppermute | solution.py:64
  42.1 0.8 %collective-permute-start.15 = (f32[64,256]{1,0:T(8,128)S(1)}, f32[64,256]{1,0:T(8,128)S(1)}, u32[]{:S(2)}, u32[]{:S(2)}) collective-permute-start(f32[64,256]{1,0:T(8,128)S(1)} %add_add_fusion.1), channel_id=1, source_target_pairs={{0,2},{1,3},{2,0},{3,1},{4,6},{5,7},{6,4},{7,5},{8,10},{9,11},{10,... | collective-permute-start | bytes 196616 | tf_op jit(solution)/shard_map/ppermute | solution.py:64
  42.9 1.8 %collective-permute-done.17 = f32[64,256]{1,0:T(8,128)S(1)} collective-permute-done((f32[64,256]{1,0:T(8,128)S(1)}, f32[64,256]{1,0:T(8,128)S(1)}, u32[]{:S(2)}, u32[]{:S(2)}) %collective-permute-start.17) | collective-permute-done | bytes 65568 | tf_op jit(solution)/shard_map/ppermute | solution.py:64
  44.7 1.9 %collective-permute-done.16 = f32[64,256]{1,0:T(8,128)S(1)} collective-permute-done((f32[64,256]{1,0:T(8,128)S(1)}, f32[64,256]{1,0:T(8,128)S(1)}, u32[]{:S(2)}, u32[]{:S(2)}) %collective-permute-start.16) | collective-permute-done | bytes 65568 | tf_op jit(solution)/shard_map/ppermute | solution.py:64
  46.6 0.7 %collective-permute-done.15 = f32[64,256]{1,0:T(8,128)S(1)} collective-permute-done((f32[64,256]{1,0:T(8,128)S(1)}, f32[64,256]{1,0:T(8,128)S(1)}, u32[]{:S(2)}, u32[]{:S(2)}) %collective-permute-start.15) | collective-permute-done | bytes 65568 | tf_op jit(solution)/shard_map/ppermute | solution.py:64
  48.1 0.6 collective-permute-start.19
  48.8 1.4 %shard_map.39.inverse_ref = f32[64,64]{1,0:T(8,128)S(1)} custom-call(f32[64,64]{1,0:T(8,128)S(1)} %shard_map.38.mine_ref.after, f32[64,64]{1,0:T(8,128)S(1)} %collective-permute-done.18.other_ref), custom_call_target="tpu_custom_call" | custom-call | flops 10000000000 | bytes 1000 | tf_op jit(solution)/shard_map/pallas_call | solution.py:264
  50.5 1.7 %collective-permute-start.20 = (f32[17,8,128]{2,1,0:T(8,128)S(1)}, f32[17,8,128]{2,1,0:T(8,128)S(1)}, u32[]{:S(2)}, u32[]{:S(2)}) collective-permute-start(f32[17,8,128]{2,1,0:T(8,128)S(1)} %get-tuple-element.53), channel_id=1, source_target_pairs={{0,24},{4,28},{8,16},{12,20},{16,8},{20,12},{24,0},{28,4},{1,25},{... | collective-permute-start | bytes 208904 | tf_op jit(solution)/shard_map/ppermute | solution.py:64
  52.2 0.9 %collective-permute-start.21 = (f32[17,8,128]{2,1,0:T(8,128)S(1)}, f32[17,8,128]{2,1,0:T(8,128)S(1)}, u32[]{:S(2)}, u32[]{:S(2)}) collective-permute-start(f32[17,8,128]{2,1,0:T(8,128)S(1)} %get-tuple-element.54), channel_id=1, source_target_pairs={{0,8},{4,12},{8,0},{12,4},{16,24},{20,28},{24,16},{28,20},{1,9},{5... | collective-permute-start | bytes 208904 | tf_op jit(solution)/shard_map/ppermute | solution.py:64
  53.1 1.0 %collective-permute-start.22 = (f32[17,8,128]{2,1,0:T(8,128)S(1)}, f32[17,8,128]{2,1,0:T(8,128)S(1)}, u32[]{:S(2)}, u32[]{:S(2)}) collective-permute-start(f32[17,8,128]{2,1,0:T(8,128)S(1)} %get-tuple-element.55), channel_id=1, source_target_pairs={{0,16},{4,20},{8,24},{12,28},{16,0},{20,4},{24,8},{28,12},{1,17},{... | collective-permute-start | bytes 208904 | tf_op jit(solution)/shard_map/ppermute | solution.py:64
  54.1 2.2 %collective-permute-done.20.refs_0_ = f32[17,8,128]{2,1,0:T(8,128)S(1)} collective-permute-done((f32[17,8,128]{2,1,0:T(8,128)S(1)}, f32[17,8,128]{2,1,0:T(8,128)S(1)}, u32[]{:S(2)}, u32[]{:S(2)}) %collective-permute-start.20) | collective-permute-done | bytes 69664 | tf_op jit(solution)/shard_map/ppermute | solution.py:64
  56.3 0.7 %collective-permute-done.21.refs_1_ = f32[17,8,128]{2,1,0:T(8,128)S(1)} collective-permute-done((f32[17,8,128]{2,1,0:T(8,128)S(1)}, f32[17,8,128]{2,1,0:T(8,128)S(1)}, u32[]{:S(2)}, u32[]{:S(2)}) %collective-permute-start.21) | collective-permute-done | bytes 69664 | tf_op jit(solution)/shard_map/ppermute | solution.py:64
  57.4 0.9 %shard_map.42 = f32[66,8,128]{2,1,0:T(8,128)} custom-call(s32[1]{0:T(128)} %bitcast.me_ref.after, f32[17,8,128]{2,1,0:T(8,128)S(1)} %collective-permute-done.20.refs_0_, f32[17,8,128]{2,1,0:T(8,128)S(1)} %collective-permute-done.21.refs_1_, f32[17,8,128]{2,1,0:T(8,128)S(1)} %collective-permute-done.22.refs_2_, f32[17,8,128]{2,1,0:T(8,128)S(1)} %get-tuple-element.56.refs_3_), custom_call_target="tpu_custom_call" | custom-call | tf_op jit(solution)/shard_map/pallas_call | solution.py:342
  (33 shorter events, 7.3 us)
Async XLA Ops:
  1.0 10.6 %collective-permute-start.8 = (f32[384,128]{1,0:T(8,128)S(1)}, f32[384,128]{1,0:T(8,128)S(1)}, u32[]{:S(2)}, u32[]{:S(2)}) collective-permute-start(f32[384,128]{1,0:T(8,128)S(1)} %shard_map.28.after), channel_id=1, source_target_pairs={{0,24},{4,28},{8,16},{12,20},{16,8},{20,12},{24,0},{28,4},{1,25},{... | collective-permute-start | bytes 589832 | tf_op jit(solution)/shard_map/ppermute | solution.py:64
  6.1 16.2 %copy-start = (f32[512,64]{0,1:T(8,128)S(1)}, f32[512,64]{0,1:T(8,128)}, u32[]{:S(2)}) copy-start(f32[512,64]{0,1:T(8,128)} %param.3) | copy-start | bytes 393220
  7.5 9.2 %collective-permute-start.4 = (f32[416,128]{1,0:T(8,128)S(1)}, f32[416,128]{1,0:T(8,128)S(1)}, u32[]{:S(2)}, u32[]{:S(2)}) collective-permute-start(f32[416,128]{1,0:T(8,128)S(1)} %get-tuple-element.40), channel_id=1, source_target_pairs={{0,24},{4,28},{8,16},{12,20},{16,8},{20,12},{24,0},{28,4},{1,25},{... | collective-permute-start | bytes 638984 | tf_op jit(solution)/shard_map/ppermute | solution.py:64
  7.5 12.7 %collective-permute-start.5 = (f32[416,128]{1,0:T(8,128)S(1)}, f32[416,128]{1,0:T(8,128)S(1)}, u32[]{:S(2)}, u32[]{:S(2)}) collective-permute-start(f32[416,128]{1,0:T(8,128)S(1)} %get-tuple-element.41), channel_id=1, source_target_pairs={{0,8},{4,12},{8,0},{12,4},{16,24},{20,28},{24,16},{28,20},{1,9},{5... | collective-permute-start | bytes 638984 | tf_op jit(solution)/shard_map/ppermute | solution.py:64
  9.5 12.4 %collective-permute-start.6 = (f32[416,128]{1,0:T(8,128)S(1)}, f32[416,128]{1,0:T(8,128)S(1)}, u32[]{:S(2)}, u32[]{:S(2)}) collective-permute-start(f32[416,128]{1,0:T(8,128)S(1)} %get-tuple-element.42), channel_id=1, source_target_pairs={{0,16},{4,20},{8,24},{12,28},{16,0},{20,4},{24,8},{28,12},{1,17},{... | collective-permute-start | bytes 638984 | tf_op jit(solution)/shard_map/ppermute | solution.py:64
  11.0 13.5 %collective-permute-start.9 = (f32[384,128]{1,0:T(8,128)S(1)}, f32[384,128]{1,0:T(8,128)S(1)}, u32[]{:S(2)}, u32[]{:S(2)}) collective-permute-start(f32[384,128]{1,0:T(8,128)S(1)} %get-tuple-element.46), channel_id=1, source_target_pairs={{0,8},{4,12},{8,0},{12,4},{16,24},{20,28},{24,16},{28,20},{1,9},{5... | collective-permute-start | bytes 589832 | tf_op jit(solution)/shard_map/ppermute | solution.py:64
  11.5 13.9 %collective-permute-start.10 = (f32[384,128]{1,0:T(8,128)S(1)}, f32[384,128]{1,0:T(8,128)S(1)}, u32[]{:S(2)}, u32[]{:S(2)}) collective-permute-start(f32[384,128]{1,0:T(8,128)S(1)} %get-tuple-element.47), channel_id=1, source_target_pairs={{0,16},{4,20},{8,24},{12,28},{16,0},{20,4},{24,8},{28,12},{1,17},{... | collective-permute-start | bytes 589832 | tf_op jit(solution)/shard_map/ppermute | solution.py:64
  16.6 11.6 %collective-permute-start = (f32[256,128]{1,0:T(8,128)S(1)}, f32[256,128]{1,0:T(8,128)S(1)}, u32[]{:S(2)}, u32[]{:S(2)}) collective-permute-start(f32[256,128]{1,0:T(8,128)S(1)} %get-tuple-element.33), channel_id=1, source_target_pairs={{0,24},{4,28},{8,16},{12,20},{16,8},{20,12},{24,0},{28,4},{1,25},{... | collective-permute-start | bytes 393224 | tf_op jit(solution)/shard_map/ppermute | solution.py:64
  20.2 8.8 %collective-permute-start.1 = (f32[256,128]{1,0:T(8,128)S(1)}, f32[256,128]{1,0:T(8,128)S(1)}, u32[]{:S(2)}, u32[]{:S(2)}) collective-permute-start(f32[256,128]{1,0:T(8,128)S(1)} %get-tuple-element.34), channel_id=1, source_target_pairs={{0,8},{4,12},{8,0},{12,4},{16,24},{20,28},{24,16},{28,20},{1,9},{5... | collective-permute-start | bytes 393224 | tf_op jit(solution)/shard_map/ppermute | solution.py:64
  21.9 7.6 %collective-permute-start.2 = (f32[256,128]{1,0:T(8,128)S(1)}, f32[256,128]{1,0:T(8,128)S(1)}, u32[]{:S(2)}, u32[]{:S(2)}) collective-permute-start(f32[256,128]{1,0:T(8,128)S(1)} %get-tuple-element.35), channel_id=1, source_target_pairs={{0,16},{4,20},{8,24},{12,28},{16,0},{20,4},{24,8},{28,12},{1,17},{... | collective-permute-start | bytes 393224 | tf_op jit(solution)/shard_map/ppermute | solution.py:64
  24.5 5.9 %collective-permute-start.7 = (f32[64,896]{1,0:T(8,128)S(1)}, f32[64,896]{1,0:T(8,128)S(1)}, u32[]{:S(2)}, u32[]{:S(2)}) collective-permute-start(f32[64,896]{1,0:T(8,128)S(1)} %get-tuple-element.43.mine_ref), channel_id=1, source_target_pairs={{0,4},{4,0},{8,12},{12,8},{16,20},{20,16},{24,28},{28,24},{1,5},{5... | collective-permute-start | bytes 688136 | tf_op jit(solution)/shard_map/ppermute | solution.py:64
  25.8 4.1 %collective-permute-start.11 = (f32[64,768]{1,0:T(8,128)S(1)}, f32[64,768]{1,0:T(8,128)S(1)}, u32[]{:S(2)}, u32[]{:S(2)}) collective-permute-start(f32[64,768]{1,0:T(8,128)S(1)} %get-tuple-element.48.mine_ref), channel_id=1, source_target_pairs={{0,4},{4,0},{8,12},{12,8},{16,20},{20,16},{24,28},{28,24},{1,5},{5... | collective-permute-start | bytes 589832 | tf_op jit(solution)/shard_map/ppermute | solution.py:64
  29.9 1.4 %collective-permute-start.3 = (f32[64,512]{1,0:T(8,128)S(1)}, f32[64,512]{1,0:T(8,128)S(1)}, u32[]{:S(2)}, u32[]{:S(2)}) collective-permute-start(f32[64,512]{1,0:T(8,128)S(1)} %get-tuple-element.37.mine_ref), channel_id=1, source_target_pairs={{0,4},{4,0},{8,12},{12,8},{16,20},{20,16},{24,28},{28,24},{1,5},{5... | collective-permute-start | bytes 393224 | tf_op jit(solution)/shard_map/ppermute | solution.py:64
  31.6 6.0 %collective-permute-start.14 = (f32[64,256]{1,0:T(8,128)S(1)}, f32[64,256]{1,0:T(8,128)S(1)}, u32[]{:S(2)}, u32[]{:S(2)}) collective-permute-start(f32[64,256]{1,0:T(8,128)S(1)} %shard_map.37), channel_id=1, source_target_pairs={{0,24},{4,28},{8,16},{12,20},{16,8},{20,12},{24,0},{28,4},{1,25},{... | collective-permute-start | bytes 196616 | tf_op jit(solution)/shard_map/ppermute | solution.py:64
  33.6 4.3 %collective-permute-start.13 = (f32[64,256]{1,0:T(8,128)S(1)}, f32[64,256]{1,0:T(8,128)S(1)}, u32[]{:S(2)}, u32[]{:S(2)}) collective-permute-start(f32[64,256]{1,0:T(8,128)S(1)} %shard_map.37), channel_id=1, source_target_pairs={{0,8},{4,12},{8,0},{12,4},{16,24},{20,28},{24,16},{28,20},{1,9},{5... | collective-permute-start | bytes 196616 | tf_op jit(solution)/shard_map/ppermute | solution.py:64
  34.1 4.3 %collective-permute-start.12 = (f32[64,256]{1,0:T(8,128)S(1)}, f32[64,256]{1,0:T(8,128)S(1)}, u32[]{:S(2)}, u32[]{:S(2)}) collective-permute-start(f32[64,256]{1,0:T(8,128)S(1)} %shard_map.37), channel_id=1, source_target_pairs={{0,16},{4,20},{8,24},{12,28},{16,0},{20,4},{24,8},{28,12},{1,17},{... | collective-permute-start | bytes 196616 | tf_op jit(solution)/shard_map/ppermute | solution.py:64
  38.4 6.2 %collective-permute-start.17 = (f32[64,256]{1,0:T(8,128)S(1)}, f32[64,256]{1,0:T(8,128)S(1)}, u32[]{:S(2)}, u32[]{:S(2)}) collective-permute-start(f32[64,256]{1,0:T(8,128)S(1)} %add_add_fusion.1), channel_id=1, source_target_pairs={{0,3},{1,2},{2,1},{3,0},{4,7},{5,6},{6,5},{7,4},{8,11},{9,10},{10,... | collective-permute-start | bytes 196616 | tf_op jit(solution)/shard_map/ppermute | solution.py:64
  42.1 4.5 %collective-permute-start.16 = (f32[64,256]{1,0:T(8,128)S(1)}, f32[64,256]{1,0:T(8,128)S(1)}, u32[]{:S(2)}, u32[]{:S(2)}) collective-permute-start(f32[64,256]{1,0:T(8,128)S(1)} %add_add_fusion.1), channel_id=1, source_target_pairs={{0,1},{1,0},{2,3},{3,2},{4,5},{5,4},{6,7},{7,6},{8,9},{9,8},{10,11... | collective-permute-start | bytes 196616 | tf_op jit(solution)/shard_map/ppermute | solution.py:64
  42.1 5.2 %collective-permute-start.15 = (f32[64,256]{1,0:T(8,128)S(1)}, f32[64,256]{1,0:T(8,128)S(1)}, u32[]{:S(2)}, u32[]{:S(2)}) collective-permute-start(f32[64,256]{1,0:T(8,128)S(1)} %add_add_fusion.1), channel_id=1, source_target_pairs={{0,2},{1,3},{2,0},{3,1},{4,6},{5,7},{6,4},{7,5},{8,10},{9,11},{10,... | collective-permute-start | bytes 196616 | tf_op jit(solution)/shard_map/ppermute | solution.py:64
  47.5 1.3 %collective-permute-start.18 = (f32[64,64]{1,0:T(8,128)S(1)}, f32[64,64]{1,0:T(8,128)S(1)}, u32[]{:S(2)}, u32[]{:S(2)}) collective-permute-start(f32[64,64]{1,0:T(8,128)S(1)} %shard_map.38.mine_ref.after), channel_id=1, source_target_pairs={{0,4},{4,0},{8,12},{12,8},{16,20},{20,16},{24,28},{28,24},{1,5},{5... | collective-permute-start | bytes 49160 | tf_op jit(solution)/shard_map/ppermute | solution.py:64
  48.1 2.1 %collective-permute-start.19 = (f32[64,2176]{1,0:T(8,128)S(1)}, f32[64,2176]{1,0:T(8,128)S(1)}, u32[]{:S(2)}, u32[]{:S(2)}) collective-permute-start(f32[64,2176]{1,0:T(8,128)S(1)} %shard_map.40.mine_ref), channel_id=1, source_target_pairs={{0,4},{4,0},{8,12},{12,8},{16,20},{20,16},{24,28},{28,24},{1,5},{5... | collective-permute-start | bytes 1671176 | tf_op jit(solution)/shard_map/ppermute | solution.py:64
  50.5 5.8 %collective-permute-start.20 = (f32[17,8,128]{2,1,0:T(8,128)S(1)}, f32[17,8,128]{2,1,0:T(8,128)S(1)}, u32[]{:S(2)}, u32[]{:S(2)}) collective-permute-start(f32[17,8,128]{2,1,0:T(8,128)S(1)} %get-tuple-element.53), channel_id=1, source_target_pairs={{0,24},{4,28},{8,16},{12,20},{16,8},{20,12},{24,0},{28,4},{1,25},{... | collective-permute-start | bytes 208904 | tf_op jit(solution)/shard_map/ppermute | solution.py:64
  52.2 4.8 %collective-permute-start.21 = (f32[17,8,128]{2,1,0:T(8,128)S(1)}, f32[17,8,128]{2,1,0:T(8,128)S(1)}, u32[]{:S(2)}, u32[]{:S(2)}) collective-permute-start(f32[17,8,128]{2,1,0:T(8,128)S(1)} %get-tuple-element.54), channel_id=1, source_target_pairs={{0,8},{4,12},{8,0},{12,4},{16,24},{20,28},{24,16},{28,20},{1,9},{5... | collective-permute-start | bytes 208904 | tf_op jit(solution)/shard_map/ppermute | solution.py:64
  53.1 4.3 %collective-permute-start.22 = (f32[17,8,128]{2,1,0:T(8,128)S(1)}, f32[17,8,128]{2,1,0:T(8,128)S(1)}, u32[]{:S(2)}, u32[]{:S(2)}) collective-permute-start(f32[17,8,128]{2,1,0:T(8,128)S(1)} %get-tuple-element.55), channel_id=1, source_target_pairs={{0,16},{4,20},{8,24},{12,28},{16,0},{20,4},{24,8},{28,12},{1,17},{... | collective-permute-start | bytes 208904 | tf_op jit(solution)/shard_map/ppermute | solution.py:64

commit v10 on v9

--- a/solution.py
+++ b/solution.py
@@ -124,7 +124,7 @@
 
 def project_kernel(count, left, width, me_ref, start_ref, *refs):
     chips, me = (start_ref.shape[1] // width) // 2, me_ref[0]
-    refs, (out_ref, high_ref, low_ref, *rest_refs) = in_order(refs[:chips]), refs[chips:]
+    refs, (out_ref, high_ref, low_ref, *rest_refs) = refs[:chips][::-1], refs[chips:]
     ny = refs[0].shape[1]
     parts = [start_ref[:, i * width : (i + 1) * width] for i in range(2 * chips)]
     odd = (me & 1) != 0
@@ -150,7 +150,7 @@
         out_specs=[VMEM] * (3 + len(rest)),
         out_shape=[columns, pairs, pairs] + rest,
         compiler_params=PARAMS,
-    )(me, start_t, *for_order(blocks))
+    )(me, start_t, *reversed(blocks))
 
 
 def split_slabs(high_ref, low_ref, count, ny):
@@ -194,6 +194,23 @@
         for term in reversed(got):
             value = value + term
         low *= len(masks) + 1
+    return value
+
+
+def sum_round(value, axis, size):
+    ring, low = [0, 1, 3, 2], 1
+    while low < size:
+        if 2 * low == size:
+            return value + exchange(value, axis, low, size)
+        got = []
+        for step in range(1, 4):
+            digits = [(i // low) % 4 for i in range(size)]
+            to = [ring[(ring.index(digit) + step) % 4] for digit in digits]
+            pairs = [(i, i + (to[i] - digits[i]) * low) for i in range(size)]
+            got.append(lax.ppermute(value, axis, pairs))
+        for term in reversed(got):
+            value = value + term
+        low *= 4
     return value
 
 
@@ -377,7 +394,7 @@
         raw = raw_part(mine, other, split, raw, me, last - first, ny, chips, last == own)
         pairs += split[:2]
         rests += split[2:]
-    raw = sum_over(sum_over(raw, "fib", 2, n), "blk", 1, layers)
+    raw = sum_round(sum_over(raw, "fib", 2, n), "blk", layers)
     gram = gram_part(raw)
     sums = mixed(raw, pairs + rests, me, gram, counts, chips, ny)
     inverse = factor(gram, exchange(gram, "fib", 1, n))

time: 58.5 us -> 58.1 us (level)
  waiting for transfers between devices: 23.5 us -> 21.1 us
  starting transfers between devices: 24.5 us -> 26.6 us
    ppermute x0 -> x3, starting transfers between devices: none -> 5.68 us  [sum_round(): got.append(lax.ppermute(value, axis, pairs))]
    ppermute x23 -> x20, waiting for transfers between devices: 23.5 us -> 18.3 us  [exchange(): return lax.ppermute(value, axis, [(i, i ^ mask) for i in range(size)])]
    ppermute x23 -> x20, starting transfers between devices: 24.5 us -> 20.9 us  [exchange(): return lax.ppermute(value, axis, [(i, i ^ mask) for i in range(size)])]
    ppermute x0 -> x3, waiting for transfers between devices: none -> 2.82 us  [sum_round(): got.append(lax.ppermute(value, axis, pairs))]
  transfers between devices with their start and end apart: 23 -> 23, of which waited for: 19 -> 18; matrix products, arithmetic and copies ran while one was open for 0% -> 0% of each run, Pallas kernels for 13% -> 13%
where the time goes in v10:
time: 58.1 us; the launch traced here: 57.9 us
  starting transfers between devices  26.6 us (46%)
  waiting for transfers between devices  21.1 us (36%)
  Pallas kernels  10.1 us (17%)
    ppermute x20, starting transfers between devices, exchange(): return lax.ppermute(value, axis, [(i, i ^ mask) for i in range(size)])  20.9 us
    ppermute x20, waiting for transfers between devices, exchange(): return lax.ppermute(value, axis, [(i, i ^ mask) for i in range(size)])  18.3 us
    ppermute x3, starting transfers between devices, sum_round(): got.append(lax.ppermute(value, axis, pairs))  5.68 us
    pallas_call x4, Pallas kernels, pack(): pl.pallas_call(functools.partial(pack_kernel, ks, chips, first, last, own...  4.59 us
    ppermute x3, waiting for transfers between devices, sum_round(): got.append(lax.ppermute(value, axis, pairs))  2.82 us
    pallas_call x1, Pallas kernels, factor(): pl.pallas_call(factor_kernel, in_specs=[VMEM] * 2, out_specs=VMEM, out_sh...  1.41 us
  transfers between devices with their start and end apart: 23, of which 18 were waited for; matrix products, arithmetic and copies ran while one was open for 0% of the time, Pallas kernels for 13%

profile of v10, /device:TPU:0, one launch (start us, length us, event | category | flops | bytes accessed | tf_op | source)
XLA Modules:
  0.0 57.9 jit_solution(7418150517289202458)
XLA Ops:
  0.0 1.0 %shard_map.28.after = f32[384,128]{1,0:T(8,128)S(1)} custom-call(s32[1]{0:T(128)} %bitcast.me_ref.after, f32[4224,128]{1,0:T(8,128)} %bitcast.7, s32[1]{0:T(128)} %bitcast.me_ref.after), custom_call_target="tpu_custom_call" | custom-call | tf_op jit(solution)/shard_map/pallas_call | solution.py:97
  1.0 4.0 %collective-permute-start.8 = (f32[384,128]{1,0:T(8,128)S(1)}, f32[384,128]{1,0:T(8,128)S(1)}, u32[]{:S(2)}, u32[]{:S(2)}) collective-permute-start(f32[384,128]{1,0:T(8,128)S(1)} %shard_map.28.after), channel_id=1, source_target_pairs={{0,24},{4,28},{8,16},{12,20},{16,8},{20,12},{24,0},{28,4},{1,25},{... | collective-permute-start | bytes 589832 | tf_op jit(solution)/shard_map/ppermute | solution.py:64
  4.9 1.2 %shard_map.29 = (f32[384,128]{1,0:T(8,128)S(1)}, f32[384,128]{1,0:T(8,128)S(1)}, f32[384,128]{1,0:T(8,128)S(1)}) custom-call(s32[1]{0:T(128)} %bitcast.me_ref.after, f32[4224,128]{1,0:T(8,128)} %bitcast.8, f32[384,128]{1,0:T(8,128)S(1)} %shard_map.28.after), custom_call_target="tpu_custom_call" | custom-call | tf_op jit(solution)/shard_map/pallas_call | solution.py:97
  6.1 1.3 %shard_map.30 = (f32[416,128]{1,0:T(8,128)S(1)}, f32[416,128]{1,0:T(8,128)S(1)}, f32[416,128]{1,0:T(8,128)S(1)}, f32[416,128]{1,0:T(8,128)S(1)}) custom-call(s32[1]{0:T(128)} %bitcast.me_ref.after, f32[4224,128]{1,0:T(8,128)} %bitcast.9, f32[384,128]{1,0:T(8,128)S(1)} %get-tuple-element.31.after.refs_3_), custom_call_target="tpu_custom_call" | custom-call | tf_op jit(solution)/shard_map/pallas_call | solution.py:97
  7.5 2.0 %collective-permute-start.5 = (f32[416,128]{1,0:T(8,128)S(1)}, f32[416,128]{1,0:T(8,128)S(1)}, u32[]{:S(2)}, u32[]{:S(2)}) collective-permute-start(f32[416,128]{1,0:T(8,128)S(1)} %get-tuple-element.41), channel_id=1, source_target_pairs={{0,16},{4,20},{8,24},{12,28},{16,0},{20,4},{24,8},{28,12},{1,17},{... | collective-permute-start | bytes 638984 | tf_op jit(solution)/shard_map/ppermute | solution.py:64
  9.5 1.5 %collective-permute-start.6 = (f32[416,128]{1,0:T(8,128)S(1)}, f32[416,128]{1,0:T(8,128)S(1)}, u32[]{:S(2)}, u32[]{:S(2)}) collective-permute-start(f32[416,128]{1,0:T(8,128)S(1)} %get-tuple-element.42), channel_id=1, source_target_pairs={{0,8},{4,12},{8,0},{12,4},{16,24},{20,28},{24,16},{28,20},{1,9},{5... | collective-permute-start | bytes 638984 | tf_op jit(solution)/shard_map/ppermute | solution.py:64
  11.9 1.1 %shard_map.31 = (f32[256,128]{1,0:T(8,128)S(1)}, f32[256,128]{1,0:T(8,128)S(1)}, f32[256,128]{1,0:T(8,128)S(1)}, f32[256,128]{1,0:T(8,128)S(1)}) custom-call(s32[1]{0:T(128)} %bitcast.me_ref.after, f32[4224,128]{1,0:T(8,128)} %bitcast.10, f32[416,128]{1,0:T(8,128)S(1)} %get-tuple-element.32.after.refs_3_), custom_call_target="tpu_custom_call" | custom-call | tf_op jit(solution)/shard_map/pallas_call | solution.py:97
  13.1 3.5 %collective-permute-done.4.refs_0_ = f32[416,128]{1,0:T(8,128)S(1)} collective-permute-done((f32[416,128]{1,0:T(8,128)S(1)}, f32[416,128]{1,0:T(8,128)S(1)}, u32[]{:S(2)}, u32[]{:S(2)}) %collective-permute-start.4) | collective-permute-done | bytes 213024 | tf_op jit(solution)/shard_map/ppermute | solution.py:64
  16.6 1.6 %collective-permute-start = (f32[256,128]{1,0:T(8,128)S(1)}, f32[256,128]{1,0:T(8,128)S(1)}, u32[]{:S(2)}, u32[]{:S(2)}) collective-permute-start(f32[256,128]{1,0:T(8,128)S(1)} %get-tuple-element.33), channel_id=1, source_target_pairs={{0,24},{4,28},{8,16},{12,20},{16,8},{20,12},{24,0},{28,4},{1,25},{... | collective-permute-start | bytes 393224 | tf_op jit(solution)/shard_map/ppermute | solution.py:64
  18.2 1.6 %collective-permute-done.5.refs_1_ = f32[416,128]{1,0:T(8,128)S(1)} collective-permute-done((f32[416,128]{1,0:T(8,128)S(1)}, f32[416,128]{1,0:T(8,128)S(1)}, u32[]{:S(2)}, u32[]{:S(2)}) %collective-permute-start.5) | collective-permute-done | bytes 213024 | tf_op jit(solution)/shard_map/ppermute | solution.py:64
  19.8 0.9 %collective-permute-start.1 = (f32[256,128]{1,0:T(8,128)S(1)}, f32[256,128]{1,0:T(8,128)S(1)}, u32[]{:S(2)}, u32[]{:S(2)}) collective-permute-start(f32[256,128]{1,0:T(8,128)S(1)} %get-tuple-element.34), channel_id=1, source_target_pairs={{0,16},{4,20},{8,24},{12,28},{16,0},{20,4},{24,8},{28,12},{1,17},{... | collective-permute-start | bytes 393224 | tf_op jit(solution)/shard_map/ppermute | solution.py:64
  20.8 1.5 %collective-permute-start.2 = (f32[256,128]{1,0:T(8,128)S(1)}, f32[256,128]{1,0:T(8,128)S(1)}, u32[]{:S(2)}, u32[]{:S(2)}) collective-permute-start(f32[256,128]{1,0:T(8,128)S(1)} %get-tuple-element.35), channel_id=1, source_target_pairs={{0,8},{4,12},{8,0},{12,4},{16,24},{20,28},{24,16},{28,20},{1,9},{5... | collective-permute-start | bytes 393224 | tf_op jit(solution)/shard_map/ppermute | solution.py:64
  22.7 2.8 %collective-permute-done.9.refs_1_ = f32[384,128]{1,0:T(8,128)S(1)} collective-permute-done((f32[384,128]{1,0:T(8,128)S(1)}, f32[384,128]{1,0:T(8,128)S(1)}, u32[]{:S(2)}, u32[]{:S(2)}) %collective-permute-start.9) | collective-permute-done | bytes 196640 | tf_op jit(solution)/shard_map/ppermute | solution.py:64
  25.9 0.6 collective-permute-start.11
  26.5 1.8 %collective-permute-done.refs_0_ = f32[256,128]{1,0:T(8,128)S(1)} collective-permute-done((f32[256,128]{1,0:T(8,128)S(1)}, f32[256,128]{1,0:T(8,128)S(1)}, u32[]{:S(2)}, u32[]{:S(2)}) %collective-permute-start) | collective-permute-done | bytes 131104 | tf_op jit(solution)/shard_map/ppermute | solution.py:64
  31.2 2.4 %collective-permute-start.14 = (f32[64,256]{1,0:T(8,128)S(1)}, f32[64,256]{1,0:T(8,128)S(1)}, u32[]{:S(2)}, u32[]{:S(2)}) collective-permute-start(f32[64,256]{1,0:T(8,128)S(1)} %shard_map.37), channel_id=1, source_target_pairs={{0,24},{4,28},{8,16},{12,20},{16,8},{20,12},{24,0},{28,4},{1,25},{... | collective-permute-start | bytes 196616 | tf_op jit(solution)/shard_map/ppermute | solution.py:64
  34.1 0.6 %collective-permute-start.12 = (f32[64,256]{1,0:T(8,128)S(1)}, f32[64,256]{1,0:T(8,128)S(1)}, u32[]{:S(2)}, u32[]{:S(2)}) collective-permute-start(f32[64,256]{1,0:T(8,128)S(1)} %shard_map.37), channel_id=1, source_target_pairs={{0,16},{4,20},{8,24},{12,28},{16,0},{20,4},{24,8},{28,12},{1,17},{... | collective-permute-start | bytes 196616 | tf_op jit(solution)/shard_map/ppermute | solution.py:64
  34.8 2.1 %collective-permute-done.14 = f32[64,256]{1,0:T(8,128)S(1)} collective-permute-done((f32[64,256]{1,0:T(8,128)S(1)}, f32[64,256]{1,0:T(8,128)S(1)}, u32[]{:S(2)}, u32[]{:S(2)}) %collective-permute-start.14) | collective-permute-done | bytes 65568 | tf_op jit(solution)/shard_map/ppermute | solution.py:64
  36.8 1.1 %collective-permute-done.13 = f32[64,256]{1,0:T(8,128)S(1)} collective-permute-done((f32[64,256]{1,0:T(8,128)S(1)}, f32[64,256]{1,0:T(8,128)S(1)}, u32[]{:S(2)}, u32[]{:S(2)}) %collective-permute-start.13) | collective-permute-done | bytes 65568 | tf_op jit(solution)/shard_map/ppermute | solution.py:64
  38.4 1.6 %collective-permute-start.17 = (f32[64,256]{1,0:T(8,128)S(1)}, f32[64,256]{1,0:T(8,128)S(1)}, u32[]{:S(2)}, u32[]{:S(2)}) collective-permute-start(f32[64,256]{1,0:T(8,128)S(1)} %add_add_fusion.1), channel_id=1, source_target_pairs={{0,1},{1,3},{2,0},{3,2},{4,5},{5,7},{6,4},{7,6},{8,9},{9,11},{10,8... | collective-permute-start | bytes 196616 | tf_op jit(solution)/shard_map/ppermute | solution.py:210
  40.1 2.5 %collective-permute-start.16 = (f32[64,256]{1,0:T(8,128)S(1)}, f32[64,256]{1,0:T(8,128)S(1)}, u32[]{:S(2)}, u32[]{:S(2)}) collective-permute-start(f32[64,256]{1,0:T(8,128)S(1)} %add_add_fusion.1), channel_id=1, source_target_pairs={{0,3},{1,2},{2,1},{3,0},{4,7},{5,6},{6,5},{7,4},{8,11},{9,10},{10,... | collective-permute-start | bytes 196616 | tf_op jit(solution)/shard_map/ppermute | solution.py:210
  42.5 1.6 %collective-permute-start.15 = (f32[64,256]{1,0:T(8,128)S(1)}, f32[64,256]{1,0:T(8,128)S(1)}, u32[]{:S(2)}, u32[]{:S(2)}) collective-permute-start(f32[64,256]{1,0:T(8,128)S(1)} %add_add_fusion.1), channel_id=1, source_target_pairs={{0,2},{1,0},{2,3},{3,1},{4,6},{5,4},{6,7},{7,5},{8,10},{9,8},{10,1... | collective-permute-start | bytes 196616 | tf_op jit(solution)/shard_map/ppermute | solution.py:210
  44.1 1.1 %collective-permute-done.17 = f32[64,256]{1,0:T(8,128)S(1)} collective-permute-done((f32[64,256]{1,0:T(8,128)S(1)}, f32[64,256]{1,0:T(8,128)S(1)}, u32[]{:S(2)}, u32[]{:S(2)}) %collective-permute-start.17) | collective-permute-done | bytes 65568 | tf_op jit(solution)/shard_map/ppermute | solution.py:210
  45.2 1.1 %collective-permute-done.16 = f32[64,256]{1,0:T(8,128)S(1)} collective-permute-done((f32[64,256]{1,0:T(8,128)S(1)}, f32[64,256]{1,0:T(8,128)S(1)}, u32[]{:S(2)}, u32[]{:S(2)}) %collective-permute-start.16) | collective-permute-done | bytes 65568 | tf_op jit(solution)/shard_map/ppermute | solution.py:210
  46.2 0.7 %collective-permute-done.15 = f32[64,256]{1,0:T(8,128)S(1)} collective-permute-done((f32[64,256]{1,0:T(8,128)S(1)}, f32[64,256]{1,0:T(8,128)S(1)}, u32[]{:S(2)}, u32[]{:S(2)}) %collective-permute-start.15) | collective-permute-done | bytes 65568 | tf_op jit(solution)/shard_map/ppermute | solution.py:210
  48.4 1.4 %shard_map.39.inverse_ref = f32[64,64]{1,0:T(8,128)S(1)} custom-call(f32[64,64]{1,0:T(8,128)S(1)} %shard_map.38.mine_ref.after, f32[64,64]{1,0:T(8,128)S(1)} %collective-permute-done.18.other_ref), custom_call_target="tpu_custom_call" | custom-call | flops 10000000000 | bytes 1000 | tf_op jit(solution)/shard_map/pallas_call | solution.py:281
  50.2 1.8 %collective-permute-start.20 = (f32[17,8,128]{2,1,0:T(8,128)S(1)}, f32[17,8,128]{2,1,0:T(8,128)S(1)}, u32[]{:S(2)}, u32[]{:S(2)}) collective-permute-start(f32[17,8,128]{2,1,0:T(8,128)S(1)} %get-tuple-element.53), channel_id=1, source_target_pairs={{0,24},{4,28},{8,16},{12,20},{16,8},{20,12},{24,0},{28,4},{1,25},{... | collective-permute-start | bytes 208904 | tf_op jit(solution)/shard_map/ppermute | solution.py:64
  52.0 0.6 %collective-permute-start.21 = (f32[17,8,128]{2,1,0:T(8,128)S(1)}, f32[17,8,128]{2,1,0:T(8,128)S(1)}, u32[]{:S(2)}, u32[]{:S(2)}) collective-permute-start(f32[17,8,128]{2,1,0:T(8,128)S(1)} %get-tuple-element.54), channel_id=1, source_target_pairs={{0,8},{4,12},{8,0},{12,4},{16,24},{20,28},{24,16},{28,20},{1,9},{5... | collective-permute-start | bytes 208904 | tf_op jit(solution)/shard_map/ppermute | solution.py:64
  52.6 1.1 %collective-permute-start.22 = (f32[17,8,128]{2,1,0:T(8,128)S(1)}, f32[17,8,128]{2,1,0:T(8,128)S(1)}, u32[]{:S(2)}, u32[]{:S(2)}) collective-permute-start(f32[17,8,128]{2,1,0:T(8,128)S(1)} %get-tuple-element.55), channel_id=1, source_target_pairs={{0,16},{4,20},{8,24},{12,28},{16,0},{20,4},{24,8},{28,12},{1,17},{... | collective-permute-start | bytes 208904 | tf_op jit(solution)/shard_map/ppermute | solution.py:64
  53.7 2.2 %collective-permute-done.20.refs_0_ = f32[17,8,128]{2,1,0:T(8,128)S(1)} collective-permute-done((f32[17,8,128]{2,1,0:T(8,128)S(1)}, f32[17,8,128]{2,1,0:T(8,128)S(1)}, u32[]{:S(2)}, u32[]{:S(2)}) %collective-permute-start.20) | collective-permute-done | bytes 69664 | tf_op jit(solution)/shard_map/ppermute | solution.py:64
  55.9 0.6 %collective-permute-done.21.refs_1_ = f32[17,8,128]{2,1,0:T(8,128)S(1)} collective-permute-done((f32[17,8,128]{2,1,0:T(8,128)S(1)}, f32[17,8,128]{2,1,0:T(8,128)S(1)}, u32[]{:S(2)}, u32[]{:S(2)}) %collective-permute-start.21) | collective-permute-done | bytes 69664 | tf_op jit(solution)/shard_map/ppermute | solution.py:64
  57.1 0.9 %shard_map.42 = f32[66,8,128]{2,1,0:T(8,128)} custom-call(s32[1]{0:T(128)} %bitcast.me_ref.after, f32[17,8,128]{2,1,0:T(8,128)S(1)} %collective-permute-done.20.refs_0_, f32[17,8,128]{2,1,0:T(8,128)S(1)} %collective-permute-done.21.refs_1_, f32[17,8,128]{2,1,0:T(8,128)S(1)} %collective-permute-done.22.refs_2_, f32[17,8,128]{2,1,0:T(8,128)S(1)} %get-tuple-element.56.refs_3_), custom_call_target="tpu_custom_call" | custom-call | tf_op jit(solution)/shard_map/pallas_call | solution.py:359
  (33 shorter events, 8.1 us)
Async XLA Ops:
  1.0 10.5 %collective-permute-start.8 = (f32[384,128]{1,0:T(8,128)S(1)}, f32[384,128]{1,0:T(8,128)S(1)}, u32[]{:S(2)}, u32[]{:S(2)}) collective-permute-start(f32[384,128]{1,0:T(8,128)S(1)} %shard_map.28.after), channel_id=1, source_target_pairs={{0,24},{4,28},{8,16},{12,20},{16,8},{20,12},{24,0},{28,4},{1,25},{... | collective-permute-start | bytes 589832 | tf_op jit(solution)/shard_map/ppermute | solution.py:64
  6.1 16.2 %copy-start = (f32[512,64]{0,1:T(8,128)S(1)}, f32[512,64]{0,1:T(8,128)}, u32[]{:S(2)}) copy-start(f32[512,64]{0,1:T(8,128)} %param.3) | copy-start | bytes 393220
  7.5 9.1 %collective-permute-start.4 = (f32[416,128]{1,0:T(8,128)S(1)}, f32[416,128]{1,0:T(8,128)S(1)}, u32[]{:S(2)}, u32[]{:S(2)}) collective-permute-start(f32[416,128]{1,0:T(8,128)S(1)} %get-tuple-element.40), channel_id=1, source_target_pairs={{0,24},{4,28},{8,16},{12,20},{16,8},{20,12},{24,0},{28,4},{1,25},{... | collective-permute-start | bytes 638984 | tf_op jit(solution)/shard_map/ppermute | solution.py:64
  7.5 12.3 %collective-permute-start.5 = (f32[416,128]{1,0:T(8,128)S(1)}, f32[416,128]{1,0:T(8,128)S(1)}, u32[]{:S(2)}, u32[]{:S(2)}) collective-permute-start(f32[416,128]{1,0:T(8,128)S(1)} %get-tuple-element.41), channel_id=1, source_target_pairs={{0,16},{4,20},{8,24},{12,28},{16,0},{20,4},{24,8},{28,12},{1,17},{... | collective-permute-start | bytes 638984 | tf_op jit(solution)/shard_map/ppermute | solution.py:64
  9.5 11.3 %collective-permute-start.6 = (f32[416,128]{1,0:T(8,128)S(1)}, f32[416,128]{1,0:T(8,128)S(1)}, u32[]{:S(2)}, u32[]{:S(2)}) collective-permute-start(f32[416,128]{1,0:T(8,128)S(1)} %get-tuple-element.42), channel_id=1, source_target_pairs={{0,8},{4,12},{8,0},{12,4},{16,24},{20,28},{24,16},{28,20},{1,9},{5... | collective-permute-start | bytes 638984 | tf_op jit(solution)/shard_map/ppermute | solution.py:64
  11.0 14.5 %collective-permute-start.9 = (f32[384,128]{1,0:T(8,128)S(1)}, f32[384,128]{1,0:T(8,128)S(1)}, u32[]{:S(2)}, u32[]{:S(2)}) collective-permute-start(f32[384,128]{1,0:T(8,128)S(1)} %get-tuple-element.46), channel_id=1, source_target_pairs={{0,16},{4,20},{8,24},{12,28},{16,0},{20,4},{24,8},{28,12},{1,17},{... | collective-permute-start | bytes 589832 | tf_op jit(solution)/shard_map/ppermute | solution.py:64
  11.5 14.0 %collective-permute-start.10 = (f32[384,128]{1,0:T(8,128)S(1)}, f32[384,128]{1,0:T(8,128)S(1)}, u32[]{:S(2)}, u32[]{:S(2)}) collective-permute-start(f32[384,128]{1,0:T(8,128)S(1)} %get-tuple-element.47), channel_id=1, source_target_pairs={{0,8},{4,12},{8,0},{12,4},{16,24},{20,28},{24,16},{28,20},{1,9},{5... | collective-permute-start | bytes 589832 | tf_op jit(solution)/shard_map/ppermute | solution.py:64
  16.6 11.7 %collective-permute-start = (f32[256,128]{1,0:T(8,128)S(1)}, f32[256,128]{1,0:T(8,128)S(1)}, u32[]{:S(2)}, u32[]{:S(2)}) collective-permute-start(f32[256,128]{1,0:T(8,128)S(1)} %get-tuple-element.33), channel_id=1, source_target_pairs={{0,24},{4,28},{8,16},{12,20},{16,8},{20,12},{24,0},{28,4},{1,25},{... | collective-permute-start | bytes 393224 | tf_op jit(solution)/shard_map/ppermute | solution.py:64
  19.8 9.0 %collective-permute-start.1 = (f32[256,128]{1,0:T(8,128)S(1)}, f32[256,128]{1,0:T(8,128)S(1)}, u32[]{:S(2)}, u32[]{:S(2)}) collective-permute-start(f32[256,128]{1,0:T(8,128)S(1)} %get-tuple-element.34), channel_id=1, source_target_pairs={{0,16},{4,20},{8,24},{12,28},{16,0},{20,4},{24,8},{28,12},{1,17},{... | collective-permute-start | bytes 393224 | tf_op jit(solution)/shard_map/ppermute | solution.py:64
  20.8 8.3 %collective-permute-start.2 = (f32[256,128]{1,0:T(8,128)S(1)}, f32[256,128]{1,0:T(8,128)S(1)}, u32[]{:S(2)}, u32[]{:S(2)}) collective-permute-start(f32[256,128]{1,0:T(8,128)S(1)} %get-tuple-element.35), channel_id=1, source_target_pairs={{0,8},{4,12},{8,0},{12,4},{16,24},{20,28},{24,16},{28,20},{1,9},{5... | collective-permute-start | bytes 393224 | tf_op jit(solution)/shard_map/ppermute | solution.py:64
  25.5 4.3 %collective-permute-start.7 = (f32[64,896]{1,0:T(8,128)S(1)}, f32[64,896]{1,0:T(8,128)S(1)}, u32[]{:S(2)}, u32[]{:S(2)}) collective-permute-start(f32[64,896]{1,0:T(8,128)S(1)} %get-tuple-element.43.mine_ref), channel_id=1, source_target_pairs={{0,4},{4,0},{8,12},{12,8},{16,20},{20,16},{24,28},{28,24},{1,5},{5... | collective-permute-start | bytes 688136 | tf_op jit(solution)/shard_map/ppermute | solution.py:64
  25.9 3.6 %collective-permute-start.11 = (f32[64,768]{1,0:T(8,128)S(1)}, f32[64,768]{1,0:T(8,128)S(1)}, u32[]{:S(2)}, u32[]{:S(2)}) collective-permute-start(f32[64,768]{1,0:T(8,128)S(1)} %get-tuple-element.48.mine_ref), channel_id=1, source_target_pairs={{0,4},{4,0},{8,12},{12,8},{16,20},{20,16},{24,28},{28,24},{1,5},{5... | collective-permute-start | bytes 589832 | tf_op jit(solution)/shard_map/ppermute | solution.py:64
  29.4 1.4 %collective-permute-start.3 = (f32[64,512]{1,0:T(8,128)S(1)}, f32[64,512]{1,0:T(8,128)S(1)}, u32[]{:S(2)}, u32[]{:S(2)}) collective-permute-start(f32[64,512]{1,0:T(8,128)S(1)} %get-tuple-element.37.mine_ref), channel_id=1, source_target_pairs={{0,4},{4,0},{8,12},{12,8},{16,20},{20,16},{24,28},{28,24},{1,5},{5... | collective-permute-start | bytes 393224 | tf_op jit(solution)/shard_map/ppermute | solution.py:64
  31.2 5.6 %collective-permute-start.14 = (f32[64,256]{1,0:T(8,128)S(1)}, f32[64,256]{1,0:T(8,128)S(1)}, u32[]{:S(2)}, u32[]{:S(2)}) collective-permute-start(f32[64,256]{1,0:T(8,128)S(1)} %shard_map.37), channel_id=1, source_target_pairs={{0,24},{4,28},{8,16},{12,20},{16,8},{20,12},{24,0},{28,4},{1,25},{... | collective-permute-start | bytes 196616 | tf_op jit(solution)/shard_map/ppermute | solution.py:64
  33.6 4.3 %collective-permute-start.13 = (f32[64,256]{1,0:T(8,128)S(1)}, f32[64,256]{1,0:T(8,128)S(1)}, u32[]{:S(2)}, u32[]{:S(2)}) collective-permute-start(f32[64,256]{1,0:T(8,128)S(1)} %shard_map.37), channel_id=1, source_target_pairs={{0,8},{4,12},{8,0},{12,4},{16,24},{20,28},{24,16},{28,20},{1,9},{5... | collective-permute-start | bytes 196616 | tf_op jit(solution)/shard_map/ppermute | solution.py:64
  34.1 4.3 %collective-permute-start.12 = (f32[64,256]{1,0:T(8,128)S(1)}, f32[64,256]{1,0:T(8,128)S(1)}, u32[]{:S(2)}, u32[]{:S(2)}) collective-permute-start(f32[64,256]{1,0:T(8,128)S(1)} %shard_map.37), channel_id=1, source_target_pairs={{0,16},{4,20},{8,24},{12,28},{16,0},{20,4},{24,8},{28,12},{1,17},{... | collective-permute-start | bytes 196616 | tf_op jit(solution)/shard_map/ppermute | solution.py:64
  38.4 6.8 %collective-permute-start.17 = (f32[64,256]{1,0:T(8,128)S(1)}, f32[64,256]{1,0:T(8,128)S(1)}, u32[]{:S(2)}, u32[]{:S(2)}) collective-permute-start(f32[64,256]{1,0:T(8,128)S(1)} %add_add_fusion.1), channel_id=1, source_target_pairs={{0,1},{1,3},{2,0},{3,2},{4,5},{5,7},{6,4},{7,6},{8,9},{9,11},{10,8... | collective-permute-start | bytes 196616 | tf_op jit(solution)/shard_map/ppermute | solution.py:210
  40.1 6.2 %collective-permute-start.16 = (f32[64,256]{1,0:T(8,128)S(1)}, f32[64,256]{1,0:T(8,128)S(1)}, u32[]{:S(2)}, u32[]{:S(2)}) collective-permute-start(f32[64,256]{1,0:T(8,128)S(1)} %add_add_fusion.1), channel_id=1, source_target_pairs={{0,3},{1,2},{2,1},{3,0},{4,7},{5,6},{6,5},{7,4},{8,11},{9,10},{10,... | collective-permute-start | bytes 196616 | tf_op jit(solution)/shard_map/ppermute | solution.py:210
  42.5 4.4 %collective-permute-start.15 = (f32[64,256]{1,0:T(8,128)S(1)}, f32[64,256]{1,0:T(8,128)S(1)}, u32[]{:S(2)}, u32[]{:S(2)}) collective-permute-start(f32[64,256]{1,0:T(8,128)S(1)} %add_add_fusion.1), channel_id=1, source_target_pairs={{0,2},{1,0},{2,3},{3,1},{4,6},{5,4},{6,7},{7,5},{8,10},{9,8},{10,1... | collective-permute-start | bytes 196616 | tf_op jit(solution)/shard_map/ppermute | solution.py:210
  47.2 1.3 %collective-permute-start.18 = (f32[64,64]{1,0:T(8,128)S(1)}, f32[64,64]{1,0:T(8,128)S(1)}, u32[]{:S(2)}, u32[]{:S(2)}) collective-permute-start(f32[64,64]{1,0:T(8,128)S(1)} %shard_map.38.mine_ref.after), channel_id=1, source_target_pairs={{0,4},{4,0},{8,12},{12,8},{16,20},{20,16},{24,28},{28,24},{1,5},{5... | collective-permute-start | bytes 49160 | tf_op jit(solution)/shard_map/ppermute | solution.py:64
  47.8 2.1 %collective-permute-start.19 = (f32[64,2176]{1,0:T(8,128)S(1)}, f32[64,2176]{1,0:T(8,128)S(1)}, u32[]{:S(2)}, u32[]{:S(2)}) collective-permute-start(f32[64,2176]{1,0:T(8,128)S(1)} %shard_map.40.mine_ref), channel_id=1, source_target_pairs={{0,4},{4,0},{8,12},{12,8},{16,20},{20,16},{24,28},{28,24},{1,5},{5... | collective-permute-start | bytes 1671176 | tf_op jit(solution)/shard_map/ppermute | solution.py:64
  50.2 5.8 %collective-permute-start.20 = (f32[17,8,128]{2,1,0:T(8,128)S(1)}, f32[17,8,128]{2,1,0:T(8,128)S(1)}, u32[]{:S(2)}, u32[]{:S(2)}) collective-permute-start(f32[17,8,128]{2,1,0:T(8,128)S(1)} %get-tuple-element.53), channel_id=1, source_target_pairs={{0,24},{4,28},{8,16},{12,20},{16,8},{20,12},{24,0},{28,4},{1,25},{... | collective-permute-start | bytes 208904 | tf_op jit(solution)/shard_map/ppermute | solution.py:64
  52.0 4.5 %collective-permute-start.21 = (f32[17,8,128]{2,1,0:T(8,128)S(1)}, f32[17,8,128]{2,1,0:T(8,128)S(1)}, u32[]{:S(2)}, u32[]{:S(2)}) collective-permute-start(f32[17,8,128]{2,1,0:T(8,128)S(1)} %get-tuple-element.54), channel_id=1, source_target_pairs={{0,8},{4,12},{8,0},{12,4},{16,24},{20,28},{24,16},{28,20},{1,9},{5... | collective-permute-start | bytes 208904 | tf_op jit(solution)/shard_map/ppermute | solution.py:64
  52.6 4.4 %collective-permute-start.22 = (f32[17,8,128]{2,1,0:T(8,128)S(1)}, f32[17,8,128]{2,1,0:T(8,128)S(1)}, u32[]{:S(2)}, u32[]{:S(2)}) collective-permute-start(f32[17,8,128]{2,1,0:T(8,128)S(1)} %get-tuple-element.55), channel_id=1, source_target_pairs={{0,16},{4,20},{8,24},{12,28},{16,0},{20,4},{24,8},{28,12},{1,17},{... | collective-permute-start | bytes 208904 | tf_op jit(solution)/shard_map/ppermute | solution.py:64

commit v11 on v10

--- a/solution.py
+++ b/solution.py
@@ -339,14 +339,14 @@
     chips = len(refs)
     refs = in_order(refs)
     chip = lax.div(me_ref[0], 2)
+    for k in range(left):
+        parts = [ref[own][:, k * cells : (k + 1) * cells] for ref in refs]
+        rest[k] = reorder(jnp.concatenate(parts, axis=1), chip, chips, 1)
     copies = []
     for k, ref in enumerate(refs):
         to = out_ref.at[pl.ds((chip ^ k) * own, own)]
         copies.append(pltpu.make_async_copy(ref.at[pl.ds(0, own)], to, sems.at[k]))
         copies[-1].start()
-    for k in range(left):
-        parts = [ref[own][:, k * cells : (k + 1) * cells] for ref in refs]
-        rest[k] = reorder(jnp.concatenate(parts, axis=1), chip, chips, 1)
     copies.append(pltpu.make_async_copy(rest, out_ref.at[pl.ds(chips * own, left)], sems.at[chips]))
     copies[-1].start()
     for copy in copies:

time: 58.1 us -> 58.1 us (level)
  no operation moved by 1% of the time
where the time goes in v11:
time: 58.1 us; the launch traced here: 57.9 us
  starting transfers between devices  26.6 us (46%)
  waiting for transfers between devices  21.1 us (36%)
  Pallas kernels  10.1 us (17%)
    ppermute x20, starting transfers between devices, exchange(): return lax.ppermute(value, axis, [(i, i ^ mask) for i in range(size)])  20.9 us
    ppermute x20, waiting for transfers between devices, exchange(): return lax.ppermute(value, axis, [(i, i ^ mask) for i in range(size)])  18.3 us
    ppermute x3, starting transfers between devices, sum_round(): got.append(lax.ppermute(value, axis, pairs))  5.68 us
    pallas_call x4, Pallas kernels, pack(): pl.pallas_call(functools.partial(pack_kernel, ks, chips, first, last, own...  4.59 us
    ppermute x3, waiting for transfers between devices, sum_round(): got.append(lax.ppermute(value, axis, pairs))  2.82 us
    pallas_call x1, Pallas kernels, factor(): pl.pallas_call(factor_kernel, in_specs=[VMEM] * 2, out_specs=VMEM, out_sh...  1.41 us
  transfers between devices with their start and end apart: 23, of which 18 were waited for; matrix products, arithmetic and copies ran while one was open for 0% of the time, Pallas kernels for 13%

profile of v11, /device:TPU:0, one launch (start us, length us, event | category | flops | bytes accessed | tf_op | source)
XLA Modules:
  0.0 57.9 jit_solution(7418150517289202458)
XLA Ops:
  0.0 1.0 %shard_map.28.after = f32[384,128]{1,0:T(8,128)S(1)} custom-call(s32[1]{0:T(128)} %bitcast.me_ref.after, f32[4224,128]{1,0:T(8,128)} %bitcast.7, s32[1]{0:T(128)} %bitcast.me_ref.after), custom_call_target="tpu_custom_call" | custom-call | tf_op jit(solution)/shard_map/pallas_call | solution.py:97
  1.0 4.0 %collective-permute-start.8 = (f32[384,128]{1,0:T(8,128)S(1)}, f32[384,128]{1,0:T(8,128)S(1)}, u32[]{:S(2)}, u32[]{:S(2)}) collective-permute-start(f32[384,128]{1,0:T(8,128)S(1)} %shard_map.28.after), channel_id=1, source_target_pairs={{0,24},{4,28},{8,16},{12,20},{16,8},{20,12},{24,0},{28,4},{1,25},{... | collective-permute-start | bytes 589832 | tf_op jit(solution)/shard_map/ppermute | solution.py:64
  4.9 1.2 %shard_map.29 = (f32[384,128]{1,0:T(8,128)S(1)}, f32[384,128]{1,0:T(8,128)S(1)}, f32[384,128]{1,0:T(8,128)S(1)}) custom-call(s32[1]{0:T(128)} %bitcast.me_ref.after, f32[4224,128]{1,0:T(8,128)} %bitcast.8, f32[384,128]{1,0:T(8,128)S(1)} %shard_map.28.after), custom_call_target="tpu_custom_call" | custom-call | tf_op jit(solution)/shard_map/pallas_call | solution.py:97
  6.1 1.3 %shard_map.30 = (f32[416,128]{1,0:T(8,128)S(1)}, f32[416,128]{1,0:T(8,128)S(1)}, f32[416,128]{1,0:T(8,128)S(1)}, f32[416,128]{1,0:T(8,128)S(1)}) custom-call(s32[1]{0:T(128)} %bitcast.me_ref.after, f32[4224,128]{1,0:T(8,128)} %bitcast.9, f32[384,128]{1,0:T(8,128)S(1)} %get-tuple-element.31.after.refs_3_), custom_call_target="tpu_custom_call" | custom-call | tf_op jit(solution)/shard_map/pallas_call | solution.py:97
  7.5 2.0 %collective-permute-start.5 = (f32[416,128]{1,0:T(8,128)S(1)}, f32[416,128]{1,0:T(8,128)S(1)}, u32[]{:S(2)}, u32[]{:S(2)}) collective-permute-start(f32[416,128]{1,0:T(8,128)S(1)} %get-tuple-element.41), channel_id=1, source_target_pairs={{0,16},{4,20},{8,24},{12,28},{16,0},{20,4},{24,8},{28,12},{1,17},{... | collective-permute-start | bytes 638984 | tf_op jit(solution)/shard_map/ppermute | solution.py:64
  9.5 1.5 %collective-permute-start.6 = (f32[416,128]{1,0:T(8,128)S(1)}, f32[416,128]{1,0:T(8,128)S(1)}, u32[]{:S(2)}, u32[]{:S(2)}) collective-permute-start(f32[416,128]{1,0:T(8,128)S(1)} %get-tuple-element.42), channel_id=1, source_target_pairs={{0,8},{4,12},{8,0},{12,4},{16,24},{20,28},{24,16},{28,20},{1,9},{5... | collective-permute-start | bytes 638984 | tf_op jit(solution)/shard_map/ppermute | solution.py:64
  11.9 1.1 %shard_map.31 = (f32[256,128]{1,0:T(8,128)S(1)}, f32[256,128]{1,0:T(8,128)S(1)}, f32[256,128]{1,0:T(8,128)S(1)}, f32[256,128]{1,0:T(8,128)S(1)}) custom-call(s32[1]{0:T(128)} %bitcast.me_ref.after, f32[4224,128]{1,0:T(8,128)} %bitcast.10, f32[416,128]{1,0:T(8,128)S(1)} %get-tuple-element.32.after.refs_3_), custom_call_target="tpu_custom_call" | custom-call | tf_op jit(solution)/shard_map/pallas_call | solution.py:97
  13.1 3.5 %collective-permute-done.4.refs_0_ = f32[416,128]{1,0:T(8,128)S(1)} collective-permute-done((f32[416,128]{1,0:T(8,128)S(1)}, f32[416,128]{1,0:T(8,128)S(1)}, u32[]{:S(2)}, u32[]{:S(2)}) %collective-permute-start.4) | collective-permute-done | bytes 213024 | tf_op jit(solution)/shard_map/ppermute | solution.py:64
  16.6 1.6 %collective-permute-start = (f32[256,128]{1,0:T(8,128)S(1)}, f32[256,128]{1,0:T(8,128)S(1)}, u32[]{:S(2)}, u32[]{:S(2)}) collective-permute-start(f32[256,128]{1,0:T(8,128)S(1)} %get-tuple-element.33), channel_id=1, source_target_pairs={{0,24},{4,28},{8,16},{12,20},{16,8},{20,12},{24,0},{28,4},{1,25},{... | collective-permute-start | bytes 393224 | tf_op jit(solution)/shard_map/ppermute | solution.py:64
  18.2 1.6 %collective-permute-done.5.refs_1_ = f32[416,128]{1,0:T(8,128)S(1)} collective-permute-done((f32[416,128]{1,0:T(8,128)S(1)}, f32[416,128]{1,0:T(8,128)S(1)}, u32[]{:S(2)}, u32[]{:S(2)}) %collective-permute-start.5) | collective-permute-done | bytes 213024 | tf_op jit(solution)/shard_map/ppermute | solution.py:64
  19.8 0.9 %collective-permute-start.1 = (f32[256,128]{1,0:T(8,128)S(1)}, f32[256,128]{1,0:T(8,128)S(1)}, u32[]{:S(2)}, u32[]{:S(2)}) collective-permute-start(f32[256,128]{1,0:T(8,128)S(1)} %get-tuple-element.34), channel_id=1, source_target_pairs={{0,16},{4,20},{8,24},{12,28},{16,0},{20,4},{24,8},{28,12},{1,17},{... | collective-permute-start | bytes 393224 | tf_op jit(solution)/shard_map/ppermute | solution.py:64
  20.8 1.5 %collective-permute-start.2 = (f32[256,128]{1,0:T(8,128)S(1)}, f32[256,128]{1,0:T(8,128)S(1)}, u32[]{:S(2)}, u32[]{:S(2)}) collective-permute-start(f32[256,128]{1,0:T(8,128)S(1)} %get-tuple-element.35), channel_id=1, source_target_pairs={{0,8},{4,12},{8,0},{12,4},{16,24},{20,28},{24,16},{28,20},{1,9},{5... | collective-permute-start | bytes 393224 | tf_op jit(solution)/shard_map/ppermute | solution.py:64
  22.7 2.8 %collective-permute-done.9.refs_1_ = f32[384,128]{1,0:T(8,128)S(1)} collective-permute-done((f32[384,128]{1,0:T(8,128)S(1)}, f32[384,128]{1,0:T(8,128)S(1)}, u32[]{:S(2)}, u32[]{:S(2)}) %collective-permute-start.9) | collective-permute-done | bytes 196640 | tf_op jit(solution)/shard_map/ppermute | solution.py:64
  25.9 0.6 collective-permute-start.11
  26.5 1.8 %collective-permute-done.refs_0_ = f32[256,128]{1,0:T(8,128)S(1)} collective-permute-done((f32[256,128]{1,0:T(8,128)S(1)}, f32[256,128]{1,0:T(8,128)S(1)}, u32[]{:S(2)}, u32[]{:S(2)}) %collective-permute-start) | collective-permute-done | bytes 131104 | tf_op jit(solution)/shard_map/ppermute | solution.py:64
  31.2 2.4 %collective-permute-start.14 = (f32[64,256]{1,0:T(8,128)S(1)}, f32[64,256]{1,0:T(8,128)S(1)}, u32[]{:S(2)}, u32[]{:S(2)}) collective-permute-start(f32[64,256]{1,0:T(8,128)S(1)} %shard_map.37), channel_id=1, source_target_pairs={{0,24},{4,28},{8,16},{12,20},{16,8},{20,12},{24,0},{28,4},{1,25},{... | collective-permute-start | bytes 196616 | tf_op jit(solution)/shard_map/ppermute | solution.py:64
  34.1 0.6 %collective-permute-start.12 = (f32[64,256]{1,0:T(8,128)S(1)}, f32[64,256]{1,0:T(8,128)S(1)}, u32[]{:S(2)}, u32[]{:S(2)}) collective-permute-start(f32[64,256]{1,0:T(8,128)S(1)} %shard_map.37), channel_id=1, source_target_pairs={{0,16},{4,20},{8,24},{12,28},{16,0},{20,4},{24,8},{28,12},{1,17},{... | collective-permute-start | bytes 196616 | tf_op jit(solution)/shard_map/ppermute | solution.py:64
  34.8 2.1 %collective-permute-done.14 = f32[64,256]{1,0:T(8,128)S(1)} collective-permute-done((f32[64,256]{1,0:T(8,128)S(1)}, f32[64,256]{1,0:T(8,128)S(1)}, u32[]{:S(2)}, u32[]{:S(2)}) %collective-permute-start.14) | collective-permute-done | bytes 65568 | tf_op jit(solution)/shard_map/ppermute | solution.py:64
  36.8 1.1 %collective-permute-done.13 = f32[64,256]{1,0:T(8,128)S(1)} collective-permute-done((f32[64,256]{1,0:T(8,128)S(1)}, f32[64,256]{1,0:T(8,128)S(1)}, u32[]{:S(2)}, u32[]{:S(2)}) %collective-permute-start.13) | collective-permute-done | bytes 65568 | tf_op jit(solution)/shard_map/ppermute | solution.py:64
  38.4 1.6 %collective-permute-start.17 = (f32[64,256]{1,0:T(8,128)S(1)}, f32[64,256]{1,0:T(8,128)S(1)}, u32[]{:S(2)}, u32[]{:S(2)}) collective-permute-start(f32[64,256]{1,0:T(8,128)S(1)} %add_add_fusion.1), channel_id=1, source_target_pairs={{0,1},{1,3},{2,0},{3,2},{4,5},{5,7},{6,4},{7,6},{8,9},{9,11},{10,8... | collective-permute-start | bytes 196616 | tf_op jit(solution)/shard_map/ppermute | solution.py:210
  40.1 2.5 %collective-permute-start.16 = (f32[64,256]{1,0:T(8,128)S(1)}, f32[64,256]{1,0:T(8,128)S(1)}, u32[]{:S(2)}, u32[]{:S(2)}) collective-permute-start(f32[64,256]{1,0:T(8,128)S(1)} %add_add_fusion.1), channel_id=1, source_target_pairs={{0,3},{1,2},{2,1},{3,0},{4,7},{5,6},{6,5},{7,4},{8,11},{9,10},{10,... | collective-permute-start | bytes 196616 | tf_op jit(solution)/shard_map/ppermute | solution.py:210
  42.5 1.6 %collective-permute-start.15 = (f32[64,256]{1,0:T(8,128)S(1)}, f32[64,256]{1,0:T(8,128)S(1)}, u32[]{:S(2)}, u32[]{:S(2)}) collective-permute-start(f32[64,256]{1,0:T(8,128)S(1)} %add_add_fusion.1), channel_id=1, source_target_pairs={{0,2},{1,0},{2,3},{3,1},{4,6},{5,4},{6,7},{7,5},{8,10},{9,8},{10,1... | collective-permute-start | bytes 196616 | tf_op jit(solution)/shard_map/ppermute | solution.py:210
  44.1 1.1 %collective-permute-done.17 = f32[64,256]{1,0:T(8,128)S(1)} collective-permute-done((f32[64,256]{1,0:T(8,128)S(1)}, f32[64,256]{1,0:T(8,128)S(1)}, u32[]{:S(2)}, u32[]{:S(2)}) %collective-permute-start.17) | collective-permute-done | bytes 65568 | tf_op jit(solution)/shard_map/ppermute | solution.py:210
  45.2 1.1 %collective-permute-done.16 = f32[64,256]{1,0:T(8,128)S(1)} collective-permute-done((f32[64,256]{1,0:T(8,128)S(1)}, f32[64,256]{1,0:T(8,128)S(1)}, u32[]{:S(2)}, u32[]{:S(2)}) %collective-permute-start.16) | collective-permute-done | bytes 65568 | tf_op jit(solution)/shard_map/ppermute | solution.py:210
  46.2 0.7 %collective-permute-done.15 = f32[64,256]{1,0:T(8,128)S(1)} collective-permute-done((f32[64,256]{1,0:T(8,128)S(1)}, f32[64,256]{1,0:T(8,128)S(1)}, u32[]{:S(2)}, u32[]{:S(2)}) %collective-permute-start.15) | collective-permute-done | bytes 65568 | tf_op jit(solution)/shard_map/ppermute | solution.py:210
  48.4 1.4 %shard_map.39.inverse_ref = f32[64,64]{1,0:T(8,128)S(1)} custom-call(f32[64,64]{1,0:T(8,128)S(1)} %shard_map.38.mine_ref.after, f32[64,64]{1,0:T(8,128)S(1)} %collective-permute-done.18.other_ref), custom_call_target="tpu_custom_call" | custom-call | flops 10000000000 | bytes 1000 | tf_op jit(solution)/shard_map/pallas_call | solution.py:281
  50.2 1.8 %collective-permute-start.20 = (f32[17,8,128]{2,1,0:T(8,128)S(1)}, f32[17,8,128]{2,1,0:T(8,128)S(1)}, u32[]{:S(2)}, u32[]{:S(2)}) collective-permute-start(f32[17,8,128]{2,1,0:T(8,128)S(1)} %get-tuple-element.53), channel_id=1, source_target_pairs={{0,24},{4,28},{8,16},{12,20},{16,8},{20,12},{24,0},{28,4},{1,25},{... | collective-permute-start | bytes 208904 | tf_op jit(solution)/shard_map/ppermute | solution.py:64
  52.0 0.6 %collective-permute-start.21 = (f32[17,8,128]{2,1,0:T(8,128)S(1)}, f32[17,8,128]{2,1,0:T(8,128)S(1)}, u32[]{:S(2)}, u32[]{:S(2)}) collective-permute-start(f32[17,8,128]{2,1,0:T(8,128)S(1)} %get-tuple-element.54), channel_id=1, source_target_pairs={{0,8},{4,12},{8,0},{12,4},{16,24},{20,28},{24,16},{28,20},{1,9},{5... | collective-permute-start | bytes 208904 | tf_op jit(solution)/shard_map/ppermute | solution.py:64
  52.6 1.1 %collective-permute-start.22 = (f32[17,8,128]{2,1,0:T(8,128)S(1)}, f32[17,8,128]{2,1,0:T(8,128)S(1)}, u32[]{:S(2)}, u32[]{:S(2)}) collective-permute-start(f32[17,8,128]{2,1,0:T(8,128)S(1)} %get-tuple-element.55), channel_id=1, source_target_pairs={{0,16},{4,20},{8,24},{12,28},{16,0},{20,4},{24,8},{28,12},{1,17},{... | collective-permute-start | bytes 208904 | tf_op jit(solution)/shard_map/ppermute | solution.py:64
  53.7 2.2 %collective-permute-done.20.refs_0_ = f32[17,8,128]{2,1,0:T(8,128)S(1)} collective-permute-done((f32[17,8,128]{2,1,0:T(8,128)S(1)}, f32[17,8,128]{2,1,0:T(8,128)S(1)}, u32[]{:S(2)}, u32[]{:S(2)}) %collective-permute-start.20) | collective-permute-done | bytes 69664 | tf_op jit(solution)/shard_map/ppermute | solution.py:64
  55.9 0.6 %collective-permute-done.21.refs_1_ = f32[17,8,128]{2,1,0:T(8,128)S(1)} collective-permute-done((f32[17,8,128]{2,1,0:T(8,128)S(1)}, f32[17,8,128]{2,1,0:T(8,128)S(1)}, u32[]{:S(2)}, u32[]{:S(2)}) %collective-permute-start.21) | collective-permute-done | bytes 69664 | tf_op jit(solution)/shard_map/ppermute | solution.py:64
  57.1 0.9 %shard_map.42 = f32[66,8,128]{2,1,0:T(8,128)} custom-call(s32[1]{0:T(128)} %bitcast.me_ref.after, f32[17,8,128]{2,1,0:T(8,128)S(1)} %collective-permute-done.20.refs_0_, f32[17,8,128]{2,1,0:T(8,128)S(1)} %collective-permute-done.21.refs_1_, f32[17,8,128]{2,1,0:T(8,128)S(1)} %collective-permute-done.22.refs_2_, f32[17,8,128]{2,1,0:T(8,128)S(1)} %get-tuple-element.56.refs_3_), custom_call_target="tpu_custom_call" | custom-call | tf_op jit(solution)/shard_map/pallas_call | solution.py:359
  (33 shorter events, 8.1 us)
Async XLA Ops:
  1.0 10.5 %collective-permute-start.8 = (f32[384,128]{1,0:T(8,128)S(1)}, f32[384,128]{1,0:T(8,128)S(1)}, u32[]{:S(2)}, u32[]{:S(2)}) collective-permute-start(f32[384,128]{1,0:T(8,128)S(1)} %shard_map.28.after), channel_id=1, source_target_pairs={{0,24},{4,28},{8,16},{12,20},{16,8},{20,12},{24,0},{28,4},{1,25},{... | collective-permute-start | bytes 589832 | tf_op jit(solution)/shard_map/ppermute | solution.py:64
  6.1 16.2 %copy-start = (f32[512,64]{0,1:T(8,128)S(1)}, f32[512,64]{0,1:T(8,128)}, u32[]{:S(2)}) copy-start(f32[512,64]{0,1:T(8,128)} %param.3) | copy-start | bytes 393220
  7.5 9.1 %collective-permute-start.4 = (f32[416,128]{1,0:T(8,128)S(1)}, f32[416,128]{1,0:T(8,128)S(1)}, u32[]{:S(2)}, u32[]{:S(2)}) collective-permute-start(f32[416,128]{1,0:T(8,128)S(1)} %get-tuple-element.40), channel_id=1, source_target_pairs={{0,24},{4,28},{8,16},{12,20},{16,8},{20,12},{24,0},{28,4},{1,25},{... | collective-permute-start | bytes 638984 | tf_op jit(solution)/shard_map/ppermute | solution.py:64
  7.5 12.3 %collective-permute-start.5 = (f32[416,128]{1,0:T(8,128)S(1)}, f32[416,128]{1,0:T(8,128)S(1)}, u32[]{:S(2)}, u32[]{:S(2)}) collective-permute-start(f32[416,128]{1,0:T(8,128)S(1)} %get-tuple-element.41), channel_id=1, source_target_pairs={{0,16},{4,20},{8,24},{12,28},{16,0},{20,4},{24,8},{28,12},{1,17},{... | collective-permute-start | bytes 638984 | tf_op jit(solution)/shard_map/ppermute | solution.py:64
  9.5 11.3 %collective-permute-start.6 = (f32[416,128]{1,0:T(8,128)S(1)}, f32[416,128]{1,0:T(8,128)S(1)}, u32[]{:S(2)}, u32[]{:S(2)}) collective-permute-start(f32[416,128]{1,0:T(8,128)S(1)} %get-tuple-element.42), channel_id=1, source_target_pairs={{0,8},{4,12},{8,0},{12,4},{16,24},{20,28},{24,16},{28,20},{1,9},{5... | collective-permute-start | bytes 638984 | tf_op jit(solution)/shard_map/ppermute | solution.py:64
  11.0 14.5 %collective-permute-start.9 = (f32[384,128]{1,0:T(8,128)S(1)}, f32[384,128]{1,0:T(8,128)S(1)}, u32[]{:S(2)}, u32[]{:S(2)}) collective-permute-start(f32[384,128]{1,0:T(8,128)S(1)} %get-tuple-element.46), channel_id=1, source_target_pairs={{0,16},{4,20},{8,24},{12,28},{16,0},{20,4},{24,8},{28,12},{1,17},{... | collective-permute-start | bytes 589832 | tf_op jit(solution)/shard_map/ppermute | solution.py:64
  11.5 14.0 %collective-permute-start.10 = (f32[384,128]{1,0:T(8,128)S(1)}, f32[384,128]{1,0:T(8,128)S(1)}, u32[]{:S(2)}, u32[]{:S(2)}) collective-permute-start(f32[384,128]{1,0:T(8,128)S(1)} %get-tuple-element.47), channel_id=1, source_target_pairs={{0,8},{4,12},{8,0},{12,4},{16,24},{20,28},{24,16},{28,20},{1,9},{5... | collective-permute-start | bytes 589832 | tf_op jit(solution)/shard_map/ppermute | solution.py:64
  16.6 11.7 %collective-permute-start = (f32[256,128]{1,0:T(8,128)S(1)}, f32[256,128]{1,0:T(8,128)S(1)}, u32[]{:S(2)}, u32[]{:S(2)}) collective-permute-start(f32[256,128]{1,0:T(8,128)S(1)} %get-tuple-element.33), channel_id=1, source_target_pairs={{0,24},{4,28},{8,16},{12,20},{16,8},{20,12},{24,0},{28,4},{1,25},{... | collective-permute-start | bytes 393224 | tf_op jit(solution)/shard_map/ppermute | solution.py:64
  19.8 9.0 %collective-permute-start.1 = (f32[256,128]{1,0:T(8,128)S(1)}, f32[256,128]{1,0:T(8,128)S(1)}, u32[]{:S(2)}, u32[]{:S(2)}) collective-permute-start(f32[256,128]{1,0:T(8,128)S(1)} %get-tuple-element.34), channel_id=1, source_target_pairs={{0,16},{4,20},{8,24},{12,28},{16,0},{20,4},{24,8},{28,12},{1,17},{... | collective-permute-start | bytes 393224 | tf_op jit(solution)/shard_map/ppermute | solution.py:64
  20.8 8.3 %collective-permute-start.2 = (f32[256,128]{1,0:T(8,128)S(1)}, f32[256,128]{1,0:T(8,128)S(1)}, u32[]{:S(2)}, u32[]{:S(2)}) collective-permute-start(f32[256,128]{1,0:T(8,128)S(1)} %get-tuple-element.35), channel_id=1, source_target_pairs={{0,8},{4,12},{8,0},{12,4},{16,24},{20,28},{24,16},{28,20},{1,9},{5... | collective-permute-start | bytes 393224 | tf_op jit(solution)/shard_map/ppermute | solution.py:64
  25.5 4.3 %collective-permute-start.7 = (f32[64,896]{1,0:T(8,128)S(1)}, f32[64,896]{1,0:T(8,128)S(1)}, u32[]{:S(2)}, u32[]{:S(2)}) collective-permute-start(f32[64,896]{1,0:T(8,128)S(1)} %get-tuple-element.43.mine_ref), channel_id=1, source_target_pairs={{0,4},{4,0},{8,12},{12,8},{16,20},{20,16},{24,28},{28,24},{1,5},{5... | collective-permute-start | bytes 688136 | tf_op jit(solution)/shard_map/ppermute | solution.py:64
  25.9 3.6 %collective-permute-start.11 = (f32[64,768]{1,0:T(8,128)S(1)}, f32[64,768]{1,0:T(8,128)S(1)}, u32[]{:S(2)}, u32[]{:S(2)}) collective-permute-start(f32[64,768]{1,0:T(8,128)S(1)} %get-tuple-element.48.mine_ref), channel_id=1, source_target_pairs={{0,4},{4,0},{8,12},{12,8},{16,20},{20,16},{24,28},{28,24},{1,5},{5... | collective-permute-start | bytes 589832 | tf_op jit(solution)/shard_map/ppermute | solution.py:64
  29.4 1.4 %collective-permute-start.3 = (f32[64,512]{1,0:T(8,128)S(1)}, f32[64,512]{1,0:T(8,128)S(1)}, u32[]{:S(2)}, u32[]{:S(2)}) collective-permute-start(f32[64,512]{1,0:T(8,128)S(1)} %get-tuple-element.37.mine_ref), channel_id=1, source_target_pairs={{0,4},{4,0},{8,12},{12,8},{16,20},{20,16},{24,28},{28,24},{1,5},{5... | collective-permute-start | bytes 393224 | tf_op jit(solution)/shard_map/ppermute | solution.py:64
  31.2 5.6 %collective-permute-start.14 = (f32[64,256]{1,0:T(8,128)S(1)}, f32[64,256]{1,0:T(8,128)S(1)}, u32[]{:S(2)}, u32[]{:S(2)}) collective-permute-start(f32[64,256]{1,0:T(8,128)S(1)} %shard_map.37), channel_id=1, source_target_pairs={{0,24},{4,28},{8,16},{12,20},{16,8},{20,12},{24,0},{28,4},{1,25},{... | collective-permute-start | bytes 196616 | tf_op jit(solution)/shard_map/ppermute | solution.py:64
  33.6 4.3 %collective-permute-start.13 = (f32[64,256]{1,0:T(8,128)S(1)}, f32[64,256]{1,0:T(8,128)S(1)}, u32[]{:S(2)}, u32[]{:S(2)}) collective-permute-start(f32[64,256]{1,0:T(8,128)S(1)} %shard_map.37), channel_id=1, source_target_pairs={{0,8},{4,12},{8,0},{12,4},{16,24},{20,28},{24,16},{28,20},{1,9},{5... | collective-permute-start | bytes 196616 | tf_op jit(solution)/shard_map/ppermute | solution.py:64
  34.1 4.3 %collective-permute-start.12 = (f32[64,256]{1,0:T(8,128)S(1)}, f32[64,256]{1,0:T(8,128)S(1)}, u32[]{:S(2)}, u32[]{:S(2)}) collective-permute-start(f32[64,256]{1,0:T(8,128)S(1)} %shard_map.37), channel_id=1, source_target_pairs={{0,16},{4,20},{8,24},{12,28},{16,0},{20,4},{24,8},{28,12},{1,17},{... | collective-permute-start | bytes 196616 | tf_op jit(solution)/shard_map/ppermute | solution.py:64
  38.4 6.8 %collective-permute-start.17 = (f32[64,256]{1,0:T(8,128)S(1)}, f32[64,256]{1,0:T(8,128)S(1)}, u32[]{:S(2)}, u32[]{:S(2)}) collective-permute-start(f32[64,256]{1,0:T(8,128)S(1)} %add_add_fusion.1), channel_id=1, source_target_pairs={{0,1},{1,3},{2,0},{3,2},{4,5},{5,7},{6,4},{7,6},{8,9},{9,11},{10,8... | collective-permute-start | bytes 196616 | tf_op jit(solution)/shard_map/ppermute | solution.py:210
  40.1 6.2 %collective-permute-start.16 = (f32[64,256]{1,0:T(8,128)S(1)}, f32[64,256]{1,0:T(8,128)S(1)}, u32[]{:S(2)}, u32[]{:S(2)}) collective-permute-start(f32[64,256]{1,0:T(8,128)S(1)} %add_add_fusion.1), channel_id=1, source_target_pairs={{0,3},{1,2},{2,1},{3,0},{4,7},{5,6},{6,5},{7,4},{8,11},{9,10},{10,... | collective-permute-start | bytes 196616 | tf_op jit(solution)/shard_map/ppermute | solution.py:210
  42.5 4.4 %collective-permute-start.15 = (f32[64,256]{1,0:T(8,128)S(1)}, f32[64,256]{1,0:T(8,128)S(1)}, u32[]{:S(2)}, u32[]{:S(2)}) collective-permute-start(f32[64,256]{1,0:T(8,128)S(1)} %add_add_fusion.1), channel_id=1, source_target_pairs={{0,2},{1,0},{2,3},{3,1},{4,6},{5,4},{6,7},{7,5},{8,10},{9,8},{10,1... | collective-permute-start | bytes 196616 | tf_op jit(solution)/shard_map/ppermute | solution.py:210
  47.2 1.3 %collective-permute-start.18 = (f32[64,64]{1,0:T(8,128)S(1)}, f32[64,64]{1,0:T(8,128)S(1)}, u32[]{:S(2)}, u32[]{:S(2)}) collective-permute-start(f32[64,64]{1,0:T(8,128)S(1)} %shard_map.38.mine_ref.after), channel_id=1, source_target_pairs={{0,4},{4,0},{8,12},{12,8},{16,20},{20,16},{24,28},{28,24},{1,5},{5... | collective-permute-start | bytes 49160 | tf_op jit(solution)/shard_map/ppermute | solution.py:64
  47.8 2.1 %collective-permute-start.19 = (f32[64,2176]{1,0:T(8,128)S(1)}, f32[64,2176]{1,0:T(8,128)S(1)}, u32[]{:S(2)}, u32[]{:S(2)}) collective-permute-start(f32[64,2176]{1,0:T(8,128)S(1)} %shard_map.40.mine_ref), channel_id=1, source_target_pairs={{0,4},{4,0},{8,12},{12,8},{16,20},{20,16},{24,28},{28,24},{1,5},{5... | collective-permute-start | bytes 1671176 | tf_op jit(solution)/shard_map/ppermute | solution.py:64
  50.2 5.8 %collective-permute-start.20 = (f32[17,8,128]{2,1,0:T(8,128)S(1)}, f32[17,8,128]{2,1,0:T(8,128)S(1)}, u32[]{:S(2)}, u32[]{:S(2)}) collective-permute-start(f32[17,8,128]{2,1,0:T(8,128)S(1)} %get-tuple-element.53), channel_id=1, source_target_pairs={{0,24},{4,28},{8,16},{12,20},{16,8},{20,12},{24,0},{28,4},{1,25},{... | collective-permute-start | bytes 208904 | tf_op jit(solution)/shard_map/ppermute | solution.py:64
  52.0 4.5 %collective-permute-start.21 = (f32[17,8,128]{2,1,0:T(8,128)S(1)}, f32[17,8,128]{2,1,0:T(8,128)S(1)}, u32[]{:S(2)}, u32[]{:S(2)}) collective-permute-start(f32[17,8,128]{2,1,0:T(8,128)S(1)} %get-tuple-element.54), channel_id=1, source_target_pairs={{0,8},{4,12},{8,0},{12,4},{16,24},{20,28},{24,16},{28,20},{1,9},{5... | collective-permute-start | bytes 208904 | tf_op jit(solution)/shard_map/ppermute | solution.py:64
  52.6 4.4 %collective-permute-start.22 = (f32[17,8,128]{2,1,0:T(8,128)S(1)}, f32[17,8,128]{2,1,0:T(8,128)S(1)}, u32[]{:S(2)}, u32[]{:S(2)}) collective-permute-start(f32[17,8,128]{2,1,0:T(8,128)S(1)} %get-tuple-element.55), channel_id=1, source_target_pairs={{0,16},{4,20},{8,24},{12,28},{16,0},{20,4},{24,8},{28,12},{1,17},{... | collective-permute-start | bytes 208904 | tf_op jit(solution)/shard_map/ppermute | solution.py:64
